TPU v7x, 32 devices: a whole 2x2x4 slice. The times are simulated.
32 devices in a mesh: pack: 8 (over z, x), seq: 4 (over y, core).
Axes of the slice: x: 2, y: 2, z: 4, core: 2. Of those that a mesh axis runs over, the one named last changes fastest.
Arguments:
- tokens: bfloat16 [16, 2304, 1152], P('pack', 'seq'), may hold values from -6 to 6
- condition: bfloat16 [16, 2304, 1152], P('pack', 'seq'), may hold values from -6 to 6
- image_ids: int32 [16, 2304], P('pack', 'seq'), may hold values from 0 to 8, as said below
- ada_weight: bfloat16 [1152, 6912], P('pack', 'seq'), may hold values from -0.1875 to 0.1875
- attn_weight: bfloat16 [1152, 3456], P('pack', 'seq'), may hold values from -0.1875 to 0.1875
- out_weight: bfloat16 [1152, 1152], P('pack', 'seq'), may hold values from -0.75 to 0.75
- up_weight: bfloat16 [1152, 4608], P('pack', 'seq'), may hold values from -0.1875 to 0.1875
- down_weight: bfloat16 [4608, 1152], P('pack', 'seq'), may hold values from -0.09375 to 0.09375
- biases: bfloat16 [16128], P(('pack', 'seq')), may hold values from -1.5 to 1.5
- cotangent: bfloat16 [16, 2304, 1152], P('pack', 'seq'), may hold values from -6 to 6
Outputs:
- block_out: bfloat16 [16, 2304, 1152], P('pack', 'seq')
- tokens_grad: float32 [16, 2304, 1152], P('pack', 'seq')
- condition_grad: float32 [16, 2304, 1152], P('pack', 'seq')
- ada_grad: float32 [1152, 6912], P('pack', 'seq')
- attn_grad: float32 [1152, 3456], P('pack', 'seq')
- out_grad: float32 [1152, 1152], P('pack', 'seq')
- up_grad: float32 [1152, 4608], P('pack', 'seq')
- down_grad: float32 [4608, 1152], P('pack', 'seq')
- bias_grad: float32 [16128], P(('pack', 'seq'))
Inputs may be any that keep to these rules, and one draw needn't show every extreme that they name: `image_ids`: in each row the image numbers start at 0, never fall and rise by at most one from a position to the next; in each aligned block of 2 rows one row holds a single image and the other holds 9 images.
All inputs are finite; a program needn't handle non-finite values.
Results may differ from a plain program's by a relative error of at most 0.014.
The roundings to bfloat16 on the way count: a program that leaves them out, or rounds other values in their place, can miss the bound.
Values may be sent and summed in bfloat16 or wider, within the bound.
No kernel may reach another device: no remote copies, remote signals or barrier semaphores. Data moves between devices by JAX's collectives and lax.ppermute only.
A program may use at most 576 MiB of HBM per device.

v0:
```python
from functools import partial

import jax
import jax.numpy as jnp
from jax import lax
from jax.sharding import PartitionSpec as P

D = 1152
HEADS = 16
HD = 72
FF = 4608
HG = 4


EPS = 1e-06


def modulate(values, shift_by, scale_by):
    center = values - jnp.mean(values, axis=-1, keepdims=True)
    spread = jnp.mean(center * center, axis=-1, keepdims=True)
    return center * lax.rsqrt(spread + EPS) * (1.0 + scale_by) + shift_by


def project(inputs, weight, offset):
    return jnp.einsum("rqd,dc->rqc", inputs, weight, preferred_element_type=jnp.float32) + offset


def back_project(gradient, weight):
    return jnp.einsum("rqc,dc->rqd", gradient, weight, preferred_element_type=jnp.float32)


def weight_grad(inputs, gradient):
    return jnp.einsum("rqd,rqc->dc", inputs, gradient, preferred_element_type=jnp.float32)


def token_sum(gradient):
    return jnp.sum(gradient.astype(jnp.float32), axis=(0, 1))


def heads_first(values):
    return values.reshape(values.shape[0], values.shape[1], HEADS // HG, HG, HD).transpose(
        2, 0, 1, 3, 4
    )


def heads_back(values):
    return values.transpose(1, 2, 0, 3, 4).reshape(values.shape[1], values.shape[2], D)


def masked_scores(query_part, key_part, same_image):
    scores = jnp.einsum(
        "rqhe,rkhe->rhqk", query_part, key_part, preferred_element_type=jnp.float32
    ) * HD ** (-0.5)
    return jnp.where(same_image[:, None], scores, -1e30)


def attend_forward(queries, key_rows, value_rows, same_image):

    def per_group(pieces):
        query_part, key_part, value_part = pieces
        scores = masked_scores(query_part, key_part, same_image)
        highest = jnp.max(scores, axis=-1, keepdims=True)
        numerators = jnp.exp(scores - highest)
        row_total = jnp.sum(numerators, axis=-1, keepdims=True)
        chances = (numerators / row_total).astype(jnp.bfloat16)
        mixture = jnp.einsum(
            "rhqk,rkhe->rqhe", chances, value_part, preferred_element_type=jnp.float32
        )
        return (mixture, highest + jnp.log(row_total))

    mixture, logsum = lax.map(
        per_group, (heads_first(queries), heads_first(key_rows), heads_first(value_rows))
    )
    return (heads_back(mixture), logsum)


def attend_backward(grad_out, queries, key_rows, value_rows, logsum, same_image):
    inv_root = HD ** (-0.5)

    def per_group(pieces):
        query_part, key_part, value_part, grad_part, logsum_part = pieces
        chances = jnp.exp(masked_scores(query_part, key_part, same_image) - logsum_part)
        value_grad = jnp.einsum(
            "rhqk,rqhe->rkhe",
            chances.astype(jnp.bfloat16),
            grad_part,
            preferred_element_type=jnp.float32,
        )
        chance_grad = jnp.einsum(
            "rqhe,rkhe->rhqk", grad_part, value_part, preferred_element_type=jnp.float32
        )
        score_grad = (
            chances * (chance_grad - jnp.sum(chances * chance_grad, axis=-1, keepdims=True))
        ).astype(jnp.bfloat16)
        query_grad = (
            jnp.einsum("rhqk,rkhe->rqhe", score_grad, key_part, preferred_element_type=jnp.float32)
            * inv_root
        )
        key_grad = (
            jnp.einsum(
                "rhqk,rqhe->rkhe", score_grad, query_part, preferred_element_type=jnp.float32
            )
            * inv_root
        )
        return (query_grad, key_grad, value_grad)

    results = lax.map(
        per_group,
        (
            heads_first(queries),
            heads_first(key_rows),
            heads_first(value_rows),
            heads_first(grad_out),
            logsum,
        ),
    )
    return (heads_back(results[0]), heads_back(results[1]), heads_back(results[2]))


def collect(ada_weight, attn_weight, out_weight, up_weight, down_weight, biases):
    ada_cols, attn_cols, out_cols, up_cols, down_cols, bias_cols = (
        lax.all_gather(ada_weight, "seq", axis=1, tiled=True),
        lax.all_gather(attn_weight, "seq", axis=1, tiled=True),
        lax.all_gather(out_weight, "seq", axis=1, tiled=True),
        lax.all_gather(up_weight, "seq", axis=1, tiled=True),
        lax.all_gather(down_weight, "seq", axis=1, tiled=True),
        lax.all_gather(biases[None], "seq", axis=1, tiled=True),
    )
    gathered = (
        lax.all_gather(ada_cols, "pack", axis=0, tiled=True),
        lax.all_gather(attn_cols, "pack", axis=0, tiled=True),
        lax.all_gather(out_cols, "pack", axis=0, tiled=True),
        lax.all_gather(up_cols, "pack", axis=0, tiled=True),
        lax.all_gather(down_cols, "pack", axis=0, tiled=True),
        lax.all_gather(bias_cols, "pack", axis=0, tiled=True),
    )
    return tuple(gathered[:5]) + (gathered[5].reshape(-1),)


def reduce_grads(ada_whole, attn_whole, out_whole, up_whole, down_whole, bias_whole):
    pack_count = lax.axis_size("pack")
    bias_rows = bias_whole.reshape(pack_count, -1)
    partial_sums = (
        lax.psum_scatter(ada_whole, "pack", scatter_dimension=0, tiled=True),
        lax.psum_scatter(attn_whole, "pack", scatter_dimension=0, tiled=True),
        lax.psum_scatter(out_whole, "pack", scatter_dimension=0, tiled=True),
        lax.psum_scatter(up_whole, "pack", scatter_dimension=0, tiled=True),
        lax.psum_scatter(down_whole, "pack", scatter_dimension=0, tiled=True),
        lax.psum_scatter(bias_rows, "pack", scatter_dimension=0, tiled=True),
    )
    owner_sums = (
        lax.psum_scatter(partial_sums[0], "seq", scatter_dimension=1, tiled=True),
        lax.psum_scatter(partial_sums[1], "seq", scatter_dimension=1, tiled=True),
        lax.psum_scatter(partial_sums[2], "seq", scatter_dimension=1, tiled=True),
        lax.psum_scatter(partial_sums[3], "seq", scatter_dimension=1, tiled=True),
        lax.psum_scatter(partial_sums[4], "seq", scatter_dimension=1, tiled=True),
        lax.psum_scatter(partial_sums[5], "seq", scatter_dimension=1, tiled=True),
    )
    return tuple(owner_sums[:5]) + (owner_sums[5].reshape(-1),)


def per_device(
    tokens,
    condition,
    image_ids,
    ada_weight,
    attn_weight,
    out_weight,
    up_weight,
    down_weight,
    biases,
    cotangent,
):
    ada_mat, attn_mat, out_mat, up_mat, down_mat, offsets = collect(
        ada_weight, attn_weight, out_weight, up_weight, down_weight, biases
    )
    ada_offset = offsets[: 6 * D]
    query_offset = offsets[6 * D : 7 * D]
    value_offset = offsets[7 * D : 8 * D]
    out_offset = offsets[8 * D : 9 * D]
    up_offset = offsets[9 * D : 9 * D + FF]
    down_offset = offsets[9 * D + FF :]
    tokens_wide = tokens.astype(jnp.float32)
    silu_value, silu_pull = jax.vjp(jax.nn.silu, condition.astype(jnp.float32))
    cond_act = silu_value.astype(jnp.bfloat16)
    modulation = project(cond_act, ada_mat, ada_offset)
    shift_mix, scale_mix, gate_mix, shift_feed, scale_feed, gate_feed = jnp.split(
        modulation, 6, axis=-1
    )
    attn_norm, attn_pull = jax.vjp(modulate, tokens_wide, shift_mix, scale_mix)
    attn_input = attn_norm.astype(jnp.bfloat16)
    qkv_offset = jnp.concatenate([query_offset, jnp.zeros_like(query_offset), value_offset])
    projected = project(attn_input, attn_mat, qkv_offset).astype(jnp.bfloat16)
    queries = projected[..., :D]
    key_local = projected[..., D : 2 * D]
    value_local = projected[..., 2 * D :]
    key_rows, value_rows, key_images = (
        lax.all_gather(key_local, "seq", axis=1, tiled=True),
        lax.all_gather(value_local, "seq", axis=1, tiled=True),
        lax.all_gather(image_ids, "seq", axis=1, tiled=True),
    )
    same_image = image_ids[:, :, None] == key_images[:, None, :]
    mixture, logsum = attend_forward(queries, key_rows, value_rows, same_image)
    attn_out = mixture.astype(jnp.bfloat16)
    branch_mix = project(attn_out, out_mat, out_offset)
    middle = tokens_wide + gate_mix * branch_mix
    feed_norm, feed_pull = jax.vjp(modulate, middle, shift_feed, scale_feed)
    feed_input = feed_norm.astype(jnp.bfloat16)
    hidden = project(feed_input, up_mat, up_offset)
    active, gelu_pull = jax.vjp(partial(jax.nn.gelu, approximate=True), hidden)
    active_low = active.astype(jnp.bfloat16)
    branch_feed = project(active_low, down_mat, down_offset)
    block_out = (middle + gate_feed * branch_feed).astype(jnp.bfloat16)
    upstream = cotangent.astype(jnp.float32)
    gate_feed_grad = upstream * branch_feed
    feed_out_grad = (upstream * gate_feed).astype(jnp.bfloat16)
    down_whole = weight_grad(active_low, feed_out_grad)
    (hidden_grad,) = gelu_pull(back_project(feed_out_grad, down_mat))
    hidden_low = hidden_grad.astype(jnp.bfloat16)
    up_whole = weight_grad(feed_input, hidden_low)
    middle_part, shift_feed_grad, scale_feed_grad = feed_pull(back_project(hidden_low, up_mat))
    middle_grad = upstream + middle_part
    gate_mix_grad = middle_grad * branch_mix
    mix_out_grad = (middle_grad * gate_mix).astype(jnp.bfloat16)
    out_whole = weight_grad(attn_out, mix_out_grad)
    attn_out_grad = back_project(mix_out_grad, out_mat).astype(jnp.bfloat16)
    query_grad, key_grad_rows, value_grad_rows = attend_backward(
        attn_out_grad, queries, key_rows, value_rows, logsum, same_image
    )
    key_grad, value_grad = (
        lax.psum_scatter(key_grad_rows, "seq", scatter_dimension=1, tiled=True),
        lax.psum_scatter(value_grad_rows, "seq", scatter_dimension=1, tiled=True),
    )
    projected_grad = jnp.concatenate([query_grad, key_grad, value_grad], axis=-1).astype(
        jnp.bfloat16
    )
    attn_whole = weight_grad(attn_input, projected_grad)
    token_part, shift_mix_grad, scale_mix_grad = attn_pull(back_project(projected_grad, attn_mat))
    tokens_grad = middle_grad + token_part
    modulation_grad = jnp.concatenate(
        [
            shift_mix_grad,
            scale_mix_grad,
            gate_mix_grad,
            shift_feed_grad,
            scale_feed_grad,
            gate_feed_grad,
        ],
        axis=-1,
    ).astype(jnp.bfloat16)
    ada_whole = weight_grad(cond_act, modulation_grad)
    (condition_grad,) = silu_pull(back_project(modulation_grad, ada_mat))
    projected_sum = token_sum(projected_grad)
    bias_whole = jnp.concatenate(
        [
            token_sum(modulation_grad),
            projected_sum[:D],
            projected_sum[2 * D :],
            token_sum(mix_out_grad),
            token_sum(hidden_low),
            token_sum(feed_out_grad),
        ]
    )
    ada_grad, attn_grad, out_grad, up_grad, down_grad, bias_grad = reduce_grads(
        ada_whole, attn_whole, out_whole, up_whole, down_whole, bias_whole
    )
    return (
        block_out,
        tokens_grad,
        condition_grad,
        ada_grad,
        attn_grad,
        out_grad,
        up_grad,
        down_grad,
        bias_grad,
    )


def solution(mesh):
    in_specs = (
        P("pack", "seq", None),
        P("pack", "seq", None),
        P("pack", "seq"),
        P("pack", "seq"),
        P("pack", "seq"),
        P("pack", "seq"),
        P("pack", "seq"),
        P("pack", "seq"),
        P(("pack", "seq")),
        P("pack", "seq", None),
    )
    out_specs = (
        P("pack", "seq", None),
        P("pack", "seq", None),
        P("pack", "seq", None),
        P("pack", "seq"),
        P("pack", "seq"),
        P("pack", "seq"),
        P("pack", "seq"),
        P("pack", "seq"),
        P(("pack", "seq")),
    )
    return jax.shard_map(
        per_device, mesh=mesh, in_specs=in_specs, out_specs=out_specs, check_vma=False
    )
```

profile of v0, /device:TPU:1, one launch (start us, length us, event | category | flops | bytes accessed | tf_op | source)
XLA Modules:
  0.0 3708.0 jit_solution(5934266305148818333)
XLA Ops:
  8.0 26.5 all-gather.35.cloned.1.call-done
  63.8 31.5 all-reduce.1
  97.9 159.2 %all-gather.17.cloned.1.call-done = bf16[1152,6912]{1,0:T(8,128)(2,1)} async-done(((bf16[144,6912]{1,0:T(8,128)(2,1)}), bf16[1152,6912]{1,0:T(8,128)(2,1)}) %all-gather.17.cloned.1.call-update) | async-done | bytes 15925264 | tf_op jit(solution)/shard_map/all_gather | solution.py:130
  257.1 30.5 convolution_add_fusion
  293.6 84.1 %all-gather.19.cloned.1.call-done = bf16[1152,3456]{1,0:T(8,128)(2,1)} async-done(((bf16[144,3456]{1,0:T(8,128)(2,1)}), bf16[1152,3456]{1,0:T(8,128)(2,1)}) %all-gather.19.cloned.1.call-update) | async-done | bytes 7962640 | tf_op jit(solution)/shard_map/all_gather | solution.py:131
  425.4 64.5 %all-gather.23.cloned.1.call-done = bf16[2,2304,1152]{2,1,0:T(8,128)(2,1)} async-done(((bf16[2,576,1152]{2,1,0:T(8,128)(2,1)}), bf16[2,2304,1152]{2,1,0:T(8,128)(2,1)}) %all-gather.23.cloned.1.call-update) | async-done | bytes 10616848 | tf_op jit(solution)/shard_map/all_gather | solution.py:198
  515.4 47.7 %all-gather.21.cloned.1.call-done = bf16[2,2304,1152]{2,1,0:T(8,128)(2,1)} async-done(((bf16[2,576,1152]{2,1,0:T(8,128)(2,1)}), bf16[2,2304,1152]{2,1,0:T(8,128)(2,1)}) %all-gather.21.cloned.1.call-update) | async-done | bytes 10616848 | tf_op jit(solution)/shard_map/all_gather | solution.py:199
  589.8 260.6 %while.28 = (s32[]{:T(128)}, bf16[4,2,576,4,72]{2,4,3,1,0:T(8,128)(2,1)}, f32[4,2,4,576,1]{3,2,1,4,0:T(4,128)}, bf16[4,2,2304,4,72]{2,4,3,1,0:T(8,128)(2,1)}, bf...) while((s32[]{:T(128)}, ...), condition=%wide.region_5.6_spmd.clone, body=%wide.region_2.5_spmd.clone.sunk | while | flops 3187699200 | bytes 166951568 | solution.py:71
  591.8 20.3 fusion.141
  612.1 20.8 fusion.142
  633.0 20.7 bitcast_dynamic-update-slice_fusion.10
  676.9 20.9 fusion.142
  697.8 20.8 bitcast_dynamic-update-slice_fusion.10
  741.8 20.6 fusion.142
  762.4 20.7 bitcast_dynamic-update-slice_fusion.10
  806.5 20.3 fusion.142
  826.8 21.9 bitcast_dynamic-update-slice_fusion.10
  878.4 20.2 fusion.65
  898.6 27.4 all-gather.33.cloned.1.call-done
  926.0 34.3 convert_reduce_fusion.1
  960.3 23.9 multiply_reduce_fusion.1
  984.3 30.1 fusion.107
  1030.8 523.1 %while.29 = (s32[]{:T(128)}, bf16[4,2,576,4,72]{2,4,3,1,0:T(8,128)(2,1)}, f32[4,2,2304,4,72]{2,4,3,0,1:T(8,128)}, f32[4,2,2304,4,72]{2,4,3,0,1:T(8,128)}, bf16[4...) while((s32[]{:T(128)}, ...), condition=%wide.region_12.13_spmd.clone, body=%wide.region_10.12_spmd.clone.sunk | while | flops 7743979008 | bytes 368170688 | solution.py:107
  1051.4 31.6 multiply_reduce_fusion.4
  1083.0 34.1 multiply_convert_fusion.9
  1182.1 31.6 multiply_reduce_fusion.4
  1213.7 34.1 multiply_convert_fusion.9
  1312.8 31.6 multiply_reduce_fusion.4
  1344.5 34.1 multiply_convert_fusion.9
  1443.5 31.6 multiply_reduce_fusion.4
  1475.1 34.1 multiply_convert_fusion.9
  1553.9 22.3 copy.105
  1576.3 23.9 copy.103
  1617.5 112.3 %reduce-scatter.24.cloned.1.call-done = f32[2,576,1152]{2,1,0:T(8,128)} async-done(((f32[2,2304,1152]{2,1,0:T(8,128)}), f32[2,576,1152]{2,1,0:T(8,128)}) %reduce-scatter.24.cloned.1.call-update) | async-done | bytes 5308432 | tf_op jit(solution)/shard_map/reduce_scatter | solution.py:232
  1734.1 153.2 %reduce-scatter.22.cloned.1.call-done = f32[2,576,1152]{2,1,0:T(8,128)} async-done(((f32[2,2304,1152]{2,1,0:T(8,128)}), f32[2,576,1152]{2,1,0:T(8,128)}) %reduce-scatter.22.cloned.1.call-update) | async-done | bytes 5308432 | tf_op jit(solution)/shard_map/reduce_scatter | solution.py:231
  1952.7 28.6 convolution_bitcast_fusion
  1982.0 25.2 convolution_bitcast_fusion.2
  2009.9 20.3 convolution_bitcast_fusion.1
  2030.3 238.1 %reduce-scatter.28.cloned.1.call-done = f32[144,3456]{1,0:T(8,128)} async-done(((f32[1152,3456]{1,0:T(8,128)}), f32[144,3456]{1,0:T(8,128)}) %reduce-scatter.28.cloned.1.call-update) | async-done | bytes 1990672 | tf_op jit(solution)/shard_map/reduce_scatter | solution.py:145
  2272.0 512.2 %reduce-scatter.26.cloned.1.call-done = f32[144,6912]{1,0:T(8,128)} async-done(((f32[1152,6912]{1,0:T(8,128)}), f32[144,6912]{1,0:T(8,128)}) %reduce-scatter.26.cloned.1.call-update) | async-done | bytes 3981328 | tf_op jit(solution)/shard_map/reduce_scatter | solution.py:144
  2790.6 344.2 %reduce-scatter.36.cloned.1.call-done = f32[576,1152]{1,0:T(8,128)} async-done(((f32[4608,1152]{1,0:T(8,128)}), f32[576,1152]{1,0:T(8,128)}) %reduce-scatter.36.cloned.1.call-update) | async-done | bytes 2654224 | tf_op jit(solution)/shard_map/reduce_scatter | solution.py:148
  3139.3 23.4 reduce-scatter.42.cloned.1.call-done
  3187.9 326.3 %reduce-scatter.32.cloned.1.call-done = f32[144,4608]{1,0:T(8,128)} async-done(((f32[1152,4608]{1,0:T(8,128)}), f32[144,4608]{1,0:T(8,128)}) %reduce-scatter.32.cloned.1.call-update) | async-done | bytes 2654224 | tf_op jit(solution)/shard_map/reduce_scatter | solution.py:147
  3514.4 28.6 all-reduce.2
  3557.2 29.5 fusion.86
  3588.9 33.9 reduce-scatter.38.cloned.1.call-done
  3625.7 36.9 reduce-scatter.44.cloned.1.call-done
  3662.7 38.2 %reduce-scatter.34.cloned.1.call-done = f32[144,1152]{1,0:T(8,128)} async-done(((f32[144,4608]{1,0:T(8,128)}), f32[144,1152]{1,0:T(8,128)}) %reduce-scatter.34.cloned.1.call-update) | async-done | bytes 663568 | tf_op jit(solution)/shard_map/reduce_scatter | solution.py:155
  (330 shorter events, 662.4 us)
Async XLA Ops:
  7.2 27.3 all-gather.35.cloned.1.call-start
  7.2 32.8 copy-start.28
  7.9 249.2 %all-gather.17.cloned.1.call-start = ((), (), s32[]{:S(2)}) async-start(), calls=%async_computation.12 | async-start | bytes 17915904 | tf_op jit(solution)/shard_map/all_gather | solution.py:130
  39.9 15.8 copy-start.51
  39.9 15.8 copy-start.52
  39.9 17.1 copy-start.53
  39.9 56.0 %copy-start = (bf16[2,576,1152]{2,1,0:T(8,128)(2,1)S(1)}, bf16[2,576,1152]{2,1,0:T(8,128)(2,1)}, u32[]{:S(2)}) copy-start(bf16[2,576,1152]{2,1,0:T(8,128)(2,1)} %param.14) | copy-start | bytes 7962628
  40.0 337.7 %all-gather.19.cloned.1.call-start = ((), (), s32[]{:S(2)}) async-start(), calls=%async_computation.13 | async-start | bytes 8957952 | tf_op jit(solution)/shard_map/all_gather | solution.py:131
  54.5 350.6 %all-gather.27.cloned.1.call-start = ((), (), s32[]{:S(2)}) async-start(), calls=%async_computation.17 | async-start | bytes 1658880 | tf_op jit(solution)/shard_map/all_gather | solution.py:125
  55.1 362.0 %all-gather.31.cloned.1.call-start = ((), (), s32[]{:S(2)}) async-start(), calls=%async_computation.19 | async-start | bytes 1843200 | tf_op jit(solution)/shard_map/all_gather | solution.py:126
  55.6 434.3 %all-gather.23.cloned.1.call-start = ((), (), s32[]{:S(2)}) async-start(), calls=%async_computation.15 | async-start | bytes 13271040 | tf_op jit(solution)/shard_map/all_gather | solution.py:198
  96.4 191.2 %copy-start.29 = (f32[2,576]{1,0:T(2,128)}, f32[2,576]{1,0:T(2,128)S(1)}, u32[]{:S(2)}) copy-start(f32[2,576]{1,0:T(2,128)S(1)} %broadcast_multiply_fusion.1) | copy-start | bytes 13828
  97.8 189.8 %copy-start.31 = (f32[2,576]{1,0:T(2,128)}, f32[2,576]{1,0:T(2,128)S(1)}, u32[]{:S(2)}) copy-start(f32[2,576]{1,0:T(2,128)S(1)} %fusion.102) | copy-start | bytes 13828
  395.3 167.7 %all-gather.21.cloned.1.call-start = ((), (), s32[]{:S(2)}) async-start(), calls=%async_computation.14 | async-start | bytes 13271040 | tf_op jit(solution)/shard_map/all_gather | solution.py:199
  396.1 458.3 %all-gather.25.cloned.1.call-start = ((), (), s32[]{:S(2)}) async-start(), calls=%async_computation.16 | async-start | bytes 2985984 | tf_op jit(solution)/shard_map/all_gather | solution.py:132
  405.0 473.3 %all-gather.29.cloned.1.call-start = ((), (), s32[]{:S(2)}) async-start(), calls=%async_computation.18 | async-start | bytes 11943936 | tf_op jit(solution)/shard_map/all_gather | solution.py:133
  405.8 520.2 %all-gather.33.cloned.1.call-start = ((), (), s32[]{:S(2)}) async-start(), calls=%async_computation.20 | async-start | bytes 11943936 | tf_op jit(solution)/shard_map/all_gather | solution.py:134
  419.7 1310.1 %reduce-scatter.24.cloned.1.call-start = ((), (), s32[]{:S(2)}) async-start(), calls=%async_computation.22 | async-start | bytes 26542080 | tf_op jit(solution)/shard_map/reduce_scatter | solution.py:232
  612.1 20.8 copy-start.13
  676.9 20.9 copy-start.13
  741.8 20.6 copy-start.13
  806.5 20.3 copy-start.13
  850.5 15.3 copy-start.24
  865.8 118.4 %copy-start.34 = (f32[2,576]{1,0:T(2,128)}, f32[2,576]{1,0:T(2,128)S(1)}, u32[]{:S(2)}) copy-start(f32[2,576]{1,0:T(2,128)S(1)} %broadcast_multiply_fusion) | copy-start | bytes 13828
  869.5 114.8 %copy-start.38 = (f32[2,576]{1,0:T(2,128)}, f32[2,576]{1,0:T(2,128)S(1)}, u32[]{:S(2)}) copy-start(f32[2,576]{1,0:T(2,128)S(1)} %fusion.103) | copy-start | bytes 13828
  878.3 20.2 copy-start.23
  878.3 47.6 %copy-start.49 = (f32[4608]{0:T(1024)S(1)}, f32[4608]{0:T(1024)}, u32[]{:S(2)}) copy-start(f32[4608]{0:T(1024)} %slice_convert_fusion.1) | copy-start | bytes 55300
  960.3 24.0 copy-start.42
  984.3 30.1 copy-start.5
  1117.1 18.0 copy-start.10
  1247.8 18.1 copy-start.10
  1277.5 14.9 copy-start.11
  1378.6 18.0 copy-start.10
  1509.2 17.9 copy-start.10
  1576.2 311.0 %reduce-scatter.22.cloned.1.call-start = ((), (), s32[]{:S(2)}) async-start(), calls=%async_computation.21 | async-start | bytes 26542080 | tf_op jit(solution)/shard_map/reduce_scatter | solution.py:231
  1600.2 407.1 %reduce-scatter.30.cloned.1.call-start = ((), (), s32[]{:S(2)}) async-start(), calls=%async_computation.25 | async-start | bytes 5971968 | tf_op jit(solution)/shard_map/reduce_scatter | solution.py:146
  1610.3 658.1 %reduce-scatter.28.cloned.1.call-start = ((), (), s32[]{:S(2)}) async-start(), calls=%async_computation.24 | async-start | bytes 17915904 | tf_op jit(solution)/shard_map/reduce_scatter | solution.py:145
  1617.5 272.7 %copy-start.15 = (bf16[2,576,1152]{2,1,0:T(8,128)(2,1)}, bf16[2,576,1152]{2,1,0:T(8,128)(2,1)S(1)}, u32[]{:S(2)}) copy-start(bf16[2,576,1152]{2,1,0:T(8,128)(2,1)S(1)} %copy.106) | copy-start | bytes 7962628
  1908.1 876.1 %reduce-scatter.26.cloned.1.call-start = ((), (), s32[]{:S(2)}) async-start(), calls=%async_computation.23 | async-start | bytes 35831808 | tf_op jit(solution)/shard_map/reduce_scatter | solution.py:144
  1981.3 1153.5 %reduce-scatter.36.cloned.1.call-start = ((), (), s32[]{:S(2)}) async-start(), calls=%async_computation.28 | async-start | bytes 23887872 | tf_op jit(solution)/shard_map/reduce_scatter | solution.py:148
  2007.3 1155.4 %reduce-scatter.42.cloned.1.call-start = ((), (), s32[]{:S(2)}) async-start(), calls=%async_computation.32 | async-start | bytes 1474560
  2009.9 1504.3 %reduce-scatter.32.cloned.1.call-start = ((), (), s32[]{:S(2)}) async-start(), calls=%async_computation.26 | async-start | bytes 23887872 | tf_op jit(solution)/shard_map/reduce_scatter | solution.py:147
  2030.2 1556.5 %reduce-scatter.40.cloned.1.call-start = ((), (), s32[]{:S(2)}) async-start(), calls=%async_computation.31 | async-start | bytes 4423680
  2272.0 1350.8 %reduce-scatter.38.cloned.1.call-start = ((), (), s32[]{:S(2)}) async-start(), calls=%async_computation.30 | async-start | bytes 8847360
  2790.6 872.1 %reduce-scatter.44.cloned.1.call-start = ((), (), s32[]{:S(2)}) async-start(), calls=%async_computation.33 | async-start | bytes 3686400
  3138.6 562.3 %reduce-scatter.34.cloned.1.call-start = ((), (), s32[]{:S(2)}) async-start(), calls=%async_computation.27 | async-start | bytes 3317760 | tf_op jit(solution)/shard_map/reduce_scatter | solution.py:155
  3181.9 332.3 %copy-start.48 = (f32[4608]{0:T(1024)S(1)}, f32[4608]{0:T(1024)}, u32[]{:S(2)}) copy-start(f32[4608]{0:T(1024)} %get-tuple-element.314) | copy-start | bytes 55300
  3181.9 332.4 %copy-start.47 = (f32[1152]{0:T(1024)S(1)}, f32[1152]{0:T(1024)}, u32[]{:S(2)}) copy-start(f32[1152]{0:T(1024)} %get-tuple-element.283) | copy-start | bytes 13828
  (50 other events, 265.0 us)
Sparse Core Ops, SparseCore 0:
  9.6 24.8 all-gather.34
  40.1 216.9 all-gather.16
  259.8 117.7 all-gather.18
  379.1 17.2 all-gather.26
  397.8 19.2 all-gather.30
  419.0 70.8 all-gather.22
  492.1 70.9 all-gather.20
  565.8 53.3 all-gather.24
  621.4 151.8 all-gather.28
  775.3 150.6 all-gather.32
  1576.3 153.3 reduce-scatter.23
  1732.4 154.7 reduce-scatter.21
  1890.8 104.0 reduce-scatter.29
  1999.1 269.1 reduce-scatter.27
  2272.6 511.5 reduce-scatter.25
  2788.4 346.3 reduce-scatter.35
  3137.8 24.8 reduce-scatter.41
  3166.9 347.2 reduce-scatter.31
  3516.8 39.5 reduce-scatter.39
  3558.9 63.8 reduce-scatter.37
  3625.9 36.6 reduce-scatter.43
  3666.0 34.8 reduce-scatter.33
where the time goes:
time: 3720 us; the launch traced here: 3710 us
  waiting for transfers between devices  2240 us (60%)
  matrix products  857 us (23%)
  other arithmetic  311 us (8%)
  local copies, waits for them, and re-layouts  182 us (5%)
  blocking collectives  102 us (3%)
    reduce_scatter x1, waiting for transfers between devices, reduce_grads(): lax.psum_scatter(ada_whole, 'pack', scatter_dimension=0, tiled=True)  512 us
    reduce_scatter x1, waiting for transfers between devices, reduce_grads(): lax.psum_scatter(down_whole, 'pack', scatter_dimension=0, tiled=True)  344 us
    reduce_scatter x1, waiting for transfers between devices, reduce_grads(): lax.psum_scatter(up_whole, 'pack', scatter_dimension=0, tiled=True)  326 us
    reduce_scatter x1, waiting for transfers between devices, reduce_grads(): lax.psum_scatter(attn_whole, 'pack', scatter_dimension=0, tiled=True)  238 us
    dot_general x8, matrix products, masked_scores(): jnp.einsum('rqhe,rkhe->rhqk', query_part, key_part, preferred_element_typ...  207 us
    all_gather x1, waiting for transfers between devices, collect(): lax.all_gather(ada_cols, 'pack', axis=0, tiled=True)  159 us
    reduce_scatter x1, waiting for transfers between devices, per_device(): lax.psum_scatter(key_grad_rows, 'seq', scatter_dimension=1, tiled=True)  153 us
    convert_element_type x4, other arithmetic, per_group(): score_grad = (chances * (chance_grad - jnp.sum(chances * chance_grad, axi...  136 us
  transfers between devices with their start and end apart: 22, of which 17 were waited for; matrix products, arithmetic and copies ran while one was open for 18% of the time, Pallas kernels for 0%

commit v1 on v0

v1 whole, which is shorter than its diff:
```python
import functools
import math
from functools import partial

import jax
import jax.numpy as jnp
from jax import lax
from jax.experimental import pallas as pl
from jax.experimental.pallas import tpu as pltpu
from jax.sharding import PartitionSpec as P

D = 1152
HEADS = 16
HD = 72
FF = 4608
EPS = 1e-06
F32 = jnp.float32
BF = jnp.bfloat16
ROOT = HD ** (-0.5)
C2 = ROOT * math.log2(math.e)
BIG = 1e30
IMAGES = 9
NN = (((1,), (0,)), ((), ()))
NT = (((1,), (1,)), ((), ()))
TN = (((0,), (0,)), ((), ()))


def dot(a, b, dims=NN):
    return lax.dot_general(a, b, dims, preferred_element_type=F32)


def lanes(n, w):
    return lax.broadcasted_iota(jnp.int32, (n, w), 1)


def pick(width, out_width, offset, copies):
    r = lax.broadcasted_iota(jnp.int32, (width, out_width), 0) - offset
    c = lax.broadcasted_iota(jnp.int32, (width, out_width), 1)
    hit = (r == c) & (c < HD)
    if copies == 2:
        hit = hit | ((r == c - HD) & (c >= HD) & (c < 2 * HD))
    return jnp.where(hit, 1.0, 0.0).astype(BF)


def split3(v):
    a = v.astype(BF).astype(F32)
    r = v - a
    b = r.astype(BF).astype(F32)
    return a, b, r - b


def aug_query(q_block, h, ids, extra=None):
    n, w = q_block.shape
    q = dot(q_block, pick(w, 256, h * HD, 2)) * C2
    lane = lanes(n, 256)
    hi = q.astype(BF).astype(F32)
    out = jnp.where(lane < HD, hi, q - hi)
    out = jnp.where(lane == 2 * HD + ids, BIG, out)
    if extra is not None:
        for t, part in enumerate(split3(extra)):
            out = jnp.where(lane == 2 * HD + IMAGES + t, part, out)
    return out.astype(BF)


def aug_key(k_block, h, ids):
    n, w = k_block.shape
    k = dot(k_block, pick(w, 256, h * HD, 2))
    lane = lanes(n, 256)
    tag = (lane >= 2 * HD) & (lane < 2 * HD + IMAGES) & (lane != 2 * HD + ids)
    out = jnp.where(tag, -1.0, k)
    out = jnp.where((lane >= 2 * HD + IMAGES) & (lane < 2 * HD + IMAGES + 3), 1.0, out)
    return out.astype(BF)


def aug_value(v_block, h, ones):
    n, w = v_block.shape
    v = dot(v_block, pick(w, 128, h * HD, 1))
    lane = lanes(n, 128)
    return jnp.where((lane >= HD) & (lane < HD + ones), 1.0, v).astype(BF)


def forward_kernel(
    hpd, tq, tk, lo_ref, hi_ref, qkv_q, qkv_ref, ids_q, ids_ref, o_ref, lse_ref,
    kaug, vaug, s_scr, qa_scr, best_scr, acc_scr,
):
    r = pl.program_id(0)
    i = pl.program_id(1)
    w = hpd * HD
    length = qkv_ref.shape[1]

    @pl.when(i == 0)
    def _():
        def build(j, _):
            rows = pl.ds(pl.multiple_of(j * tk, tk), tk)
            ids = ids_ref[0, rows, :]
            kb = qkv_ref[0, rows, w : 2 * w]
            vb = qkv_ref[0, rows, 2 * w : 3 * w]
            for h in range(hpd):
                kaug[h, rows, :] = aug_key(kb, h, ids)
                vaug[h, rows, :] = aug_value(vb, h, 1)
            return 0

        lax.fori_loop(0, length // tk, build, 0)

    lo = lo_ref[r, i]
    hi = hi_ref[r, i]
    qb = qkv_q[0, :, 0:w]
    ids = ids_q[0]
    lane = lanes(tq, 128)
    for h in range(hpd):
        qa_scr[h] = aug_query(qb, h, ids)
    best_scr[...] = jnp.full((hpd, tq, 128), -3e38, F32)
    acc_scr[...] = jnp.zeros((hpd, tq, 128), F32)

    def first(j, _):
        rows = pl.ds(pl.multiple_of(j * tk, tk), tk)
        for h in range(hpd):
            s = dot(qa_scr[h], kaug[h, rows, :], NT)
            s_scr[h, :, rows] = s
            best = s[:, 0:128]
            for t in range(1, tk // 128):
                best = jnp.maximum(best, s[:, t * 128 : (t + 1) * 128])
            best_scr[h] = jnp.maximum(best_scr[h], best)
        return 0

    lax.fori_loop(lo, hi, first, 0)
    for h in range(hpd):
        best_scr[h] = jnp.broadcast_to(jnp.max(best_scr[h], axis=1, keepdims=True), (tq, 128))

    def second(j, _):
        rows = pl.ds(pl.multiple_of(j * tk, tk), tk)
        for h in range(hpd):
            top = best_scr[h]
            s = s_scr[h, :, rows]
            p = jnp.concatenate(
                [
                    jnp.exp2(s[:, t * 128 : (t + 1) * 128] - top).astype(BF)
                    for t in range(tk // 128)
                ],
                axis=1,
            )
            acc_scr[h] += dot(p, vaug[h, rows, :])
        return 0

    lax.fori_loop(lo, hi, second, 0)
    out = jnp.zeros((tq, w), F32)
    lse_all = jnp.zeros((tq, 128), F32)
    for h in range(hpd):
        acc = acc_scr[h]
        total = acc[:, HD : HD + 1]
        o = (acc / total).astype(BF)
        o = jnp.where(lane < HD, o, 0).astype(BF)
        out = out + dot(o, pick(w, 128, h * HD, 1), NT)
        lse_all = jnp.where(lane == h, best_scr[h] + jnp.log2(total), lse_all)
    o_ref[0] = out.astype(BF)
    lse_ref[0] = lse_all


def attend_forward(qkv, ids, hpd, tq, tk):
    rows, length, _ = qkv.shape
    w = hpd * HD
    lo, hi = block_ranges(ids, tq, tk)
    column = ids[..., None]
    return pl.pallas_call(
        partial(forward_kernel, hpd, tq, tk),
        grid_spec=pltpu.PrefetchScalarGridSpec(
            num_scalar_prefetch=2,
            grid=(rows, length // tq),
            in_specs=[
                pl.BlockSpec((1, tq, 3 * w), lambda r, i, *_: (r, i, 0)),
                pl.BlockSpec((1, length, 3 * w), lambda r, i, *_: (r, 0, 0)),
                pl.BlockSpec((1, tq, 1), lambda r, i, *_: (r, i, 0)),
                pl.BlockSpec((1, length, 1), lambda r, i, *_: (r, 0, 0)),
            ],
            out_specs=[
                pl.BlockSpec((1, tq, w), lambda r, i, *_: (r, i, 0)),
                pl.BlockSpec((1, tq, 128), lambda r, i, *_: (r, i, 0)),
            ],
            scratch_shapes=[
                pltpu.VMEM((hpd, length, 256), BF),
                pltpu.VMEM((hpd, length, 128), BF),
                pltpu.VMEM((hpd, tq, length), F32),
                pltpu.VMEM((hpd, tq, 256), BF),
                pltpu.VMEM((hpd, tq, 128), F32),
                pltpu.VMEM((hpd, tq, 128), F32),
            ],
        ),
        out_shape=[
            jax.ShapeDtypeStruct((rows, length, w), BF),
            jax.ShapeDtypeStruct((rows, length, 128), F32),
        ],
        compiler_params=pltpu.CompilerParams(vmem_limit_bytes=58 << 20),
        cost_estimate=pl.CostEstimate(
            flops=12 * length * length * rows * w,
            bytes_accessed=8 * rows * length * w,
            transcendentals=rows * length * length * hpd,
        ),
        name="attend_forward",
    )(lo, hi, qkv, qkv, column, column)


def backward_kernel(
    hpd, tq, tk, lo_ref, hi_ref, qkv_ref, g_ref, o_ref, lse_ref, ids_ref, dp_ref,
    qaug, qraw, gaug, dq, kaug, vaug, dka, dva,
):
    r = pl.program_id(0)
    w = hpd * HD
    length = qkv_ref.shape[1]
    step = 256

    def build(i, _):
        rows = pl.ds(pl.multiple_of(i * step, step), step)
        ids = ids_ref[0, rows, :]
        lane = lanes(step, 128)
        qb = qkv_ref[0, rows, 0:w]
        kb = qkv_ref[0, rows, w : 2 * w]
        vb = qkv_ref[0, rows, 2 * w : 3 * w]
        for h in range(hpd):
            lse = lse_ref[0, rows, h : h + 1]
            qaug[h, rows, :] = aug_query(qb, h, ids, -lse)
            e = pick(w, 128, h * HD, 1)
            qraw[h, rows, :] = dot(qb, e).astype(BF)
            g = dot(g_ref[0, rows, :], e)
            o = dot(o_ref[0, rows, :], e)
            delta = jnp.sum(g * o, axis=1, keepdims=True)
            for t, part in enumerate(split3(-delta)):
                g = jnp.where(lane == HD + t, part, g)
            gaug[h, rows, :] = g.astype(BF)
            kaug[h, rows, :] = aug_key(kb, h, ids)
            vaug[h, rows, :] = aug_value(vb, h, 3)
            dq[h, rows, :] = jnp.zeros((step, 128), F32)
        return 0

    lax.fori_loop(0, length // step, build, 0)

    def put(values, n):
        lane = lanes(n, 128)
        full = None
        for h in range(hpd):
            part = dot(
                jnp.where(lane < HD, values[h], 0).astype(BF), pick(w, 128, h * HD, 1), NT
            )
            full = part if full is None else full + part
        return full.astype(BF)

    def per_key(j, _):
        krows = pl.ds(pl.multiple_of(j * tk, tk), tk)
        dka[...] = jnp.zeros((hpd, tk, 128), F32)
        dva[...] = jnp.zeros((hpd, tk, 128), F32)

        def per_query(i, _):
            rows = pl.ds(pl.multiple_of(i * tq, tq), tq)
            for h in range(hpd):
                ka = kaug[h, krows, :]
                va = vaug[h, krows, :]
                ga = gaug[h, rows, :]
                p = jnp.exp2(dot(ka, qaug[h, rows, :], NT))
                dp = dot(va, ga, NT)
                dva[h] += dot(p.astype(BF), ga)
                ds = (p * dp).astype(BF)
                dka[h] += dot(ds, qraw[h, rows, :])
                dq[h, rows, :] += dot(ds, ka[:, :128], TN)
            return 0

        lax.fori_loop(lo_ref[r, j], hi_ref[r, j], per_query, 0)
        dp_ref[0, krows, w : 2 * w] = put([dka[h] * ROOT for h in range(hpd)], tk)
        dp_ref[0, krows, 2 * w : 3 * w] = put([dva[h] for h in range(hpd)], tk)
        return 0

    lax.fori_loop(0, length // tk, per_key, 0)

    def finish(i, _):
        rows = pl.ds(pl.multiple_of(i * step, step), step)
        dp_ref[0, rows, 0:w] = put([dq[h, rows, :] * ROOT for h in range(hpd)], step)
        return 0

    lax.fori_loop(0, length // step, finish, 0)


def attend_backward(qkv, g, o, lse, ids, hpd, tq, tk):
    rows, length, _ = qkv.shape
    w = hpd * HD
    lo, hi = block_ranges(ids, tk, tq)

    def spec(n):
        return pl.BlockSpec((1, length, n), lambda r, *_: (r, 0, 0))

    return pl.pallas_call(
        partial(backward_kernel, hpd, tq, tk),
        grid_spec=pltpu.PrefetchScalarGridSpec(
            num_scalar_prefetch=2,
            grid=(rows,),
            in_specs=[spec(3 * w), spec(w), spec(w), spec(128), spec(1)],
            out_specs=spec(3 * w),
            scratch_shapes=[
                pltpu.VMEM((hpd, length, 256), BF),
                pltpu.VMEM((hpd, length, 128), BF),
                pltpu.VMEM((hpd, length, 128), BF),
                pltpu.VMEM((hpd, length, 128), F32),
                pltpu.VMEM((hpd, length, 256), BF),
                pltpu.VMEM((hpd, length, 128), BF),
                pltpu.VMEM((hpd, tk, 128), F32),
                pltpu.VMEM((hpd, tk, 128), F32),
            ],
        ),
        out_shape=jax.ShapeDtypeStruct((rows, length, 3 * w), BF),
        compiler_params=pltpu.CompilerParams(vmem_limit_bytes=58 << 20),
        cost_estimate=pl.CostEstimate(
            flops=30 * length * length * rows * w,
            bytes_accessed=18 * rows * length * w,
            transcendentals=rows * length * length * hpd,
        ),
        name="attend_backward",
    )(lo, hi, qkv, g, o, lse, ids[..., None])


def block_ranges(ids, mine, theirs):
    rows, length = ids.shape
    own = ids.reshape(rows, length // mine, mine)
    far = ids.reshape(rows, length // theirs, theirs)
    before = far[:, None, :, -1] < own[:, :, None, 0]
    reached = far[:, None, :, 0] <= own[:, :, None, -1]
    return (
        jnp.sum(before.astype(jnp.int32), axis=-1),
        jnp.sum(reached.astype(jnp.int32), axis=-1),
    )


def params(mib=58):
    return pltpu.CompilerParams(vmem_limit_bytes=mib << 20)


def cost(units, count, moved):
    return pl.CostEstimate(
        flops=int(2 * units * count * D * D), bytes_accessed=int(moved), transcendentals=0
    )


def once(shape, index):
    return pl.BlockSpec(shape, index, pipeline_mode=pl.Buffered(1))


def row_tile(count):
    return 288 if count % 288 == 0 else count


def norm_of(values):
    center = values - jnp.mean(values, axis=-1, keepdims=True)
    spread = jnp.mean(center * center, axis=-1, keepdims=True)
    inverse = lax.rsqrt(spread + EPS)
    return center * inverse, inverse


def norm_back(gradient, n, inverse):
    return (
        gradient
        - jnp.mean(gradient, axis=-1, keepdims=True)
        - n * jnp.mean(gradient * n, axis=-1, keepdims=True)
    ) * inverse


def mix_input_kernel(cond_ref, x_ref, ada_ref, bias_ref, act_ref, input_ref, scale_ref):
    cond = cond_ref[...].astype(F32)
    act = (cond / (1.0 + jnp.exp(-cond))).astype(BF)
    act_ref[...] = act
    parts = [dot(act, ada_ref[i]) for i in range(4)]
    shift = jnp.concatenate(parts[:2], axis=1) + bias_ref[0]
    scale = jnp.concatenate(parts[2:], axis=1) + bias_ref[1]
    normed, _ = norm_of(x_ref[...].astype(F32))
    scale_ref[...] = scale.astype(BF)
    input_ref[...] = (normed * (1.0 + scale) + shift).astype(BF)


def mix_input(cond, x, ada, bias):
    count = cond.shape[0]
    tm = row_tile(count)
    rows = pl.BlockSpec((tm, D), lambda i: (i, 0))
    return pl.pallas_call(
        mix_input_kernel,
        grid=(count // tm,),
        in_specs=[rows, rows, once((4, D, D // 2), lambda i: (0, 0, 0)),
                  once((2, 1, D), lambda i: (0, 0, 0))],
        out_specs=[rows, rows, rows],
        out_shape=[jax.ShapeDtypeStruct((count, D), BF)] * 3,
        compiler_params=params(),
        cost_estimate=cost(2, count, 10 * count * D + 4 * D * D),
        name="mix_input",
    )(cond, x, ada, bias)


def before_feed_kernel(
    act_ref, attn_ref, x_ref, cot_ref, ada_ref, out_ref, ada_bias, out_bias,
    gates_ref, mix_ref, middle_ref, input_ref, grad_ref,
):
    act = act_ref[...]
    gate_mix = dot(act, ada_ref[0]) + ada_bias[0]
    gates_ref[0] = gate_mix.astype(BF)
    branch_mix = dot(attn_ref[...], out_ref[...]) + out_bias[...]
    mix_ref[...] = branch_mix.astype(BF)
    middle = x_ref[...].astype(F32) + gate_mix * branch_mix
    middle_ref[...] = middle
    normed, _ = norm_of(middle)
    scale_feed = dot(act, ada_ref[2]) + ada_bias[2]
    gates_ref[1] = scale_feed.astype(BF)
    shift_feed = dot(act, ada_ref[1]) + ada_bias[1]
    input_ref[...] = (normed * (1.0 + scale_feed) + shift_feed).astype(BF)
    gate_feed = dot(act, ada_ref[3]) + ada_bias[3]
    gates_ref[2] = gate_feed.astype(BF)
    grad_ref[...] = (cot_ref[...].astype(F32) * gate_feed).astype(BF)


def before_feed(act, attn_out, x, cot, ada, out_mat, ada_bias, out_bias):
    count = act.shape[0]
    tm = row_tile(count)
    rows = pl.BlockSpec((tm, D), lambda i: (i, 0))
    return pl.pallas_call(
        before_feed_kernel,
        grid=(count // tm,),
        in_specs=[rows, rows, rows, rows, once((4, D, D), lambda i: (0, 0, 0)),
                  once((D, D), lambda i: (0, 0)), once((4, 1, D), lambda i: (0, 0, 0)),
                  once((1, D), lambda i: (0, 0))],
        out_specs=[pl.BlockSpec((3, tm, D), lambda i: (0, i, 0)), rows, rows, rows, rows],
        out_shape=[
            jax.ShapeDtypeStruct((3, count, D), BF),
            jax.ShapeDtypeStruct((count, D), BF),
            jax.ShapeDtypeStruct((count, D), F32),
            jax.ShapeDtypeStruct((count, D), BF),
            jax.ShapeDtypeStruct((count, D), BF),
        ],
        compiler_params=params(),
        cost_estimate=cost(5, count, 24 * count * D + 10 * D * D),
        name="before_feed",
    )(act, attn_out, x, cot, ada, out_mat, ada_bias, out_bias)


GELU_A = math.sqrt(2.0 / math.pi)
GELU_B = 0.044715


def feed_kernel(
    tm, input_ref, grad_ref, up_ref, down_ref, bias_ref,
    branch_out, shift_out, up_grad_ref, down_grad_ref, bias_grad_ref,
    branch, shift, active, hidden_grad, sem,
):
    t = pl.program_id(0)
    count = input_ref.shape[0]

    @pl.when(t == 0)
    def _():
        branch[...] = jnp.zeros_like(branch)
        shift[...] = jnp.zeros_like(shift)

    total = jnp.zeros((1, active.shape[1]), F32)
    for m in range(count // tm):
        rows = slice(m * tm, (m + 1) * tm)
        h = dot(input_ref[rows, :], up_ref[0]) + bias_ref[0]
        square = h * h
        th = jnp.tanh(GELU_A * h * (1.0 + GELU_B * square))
        half = 0.5 * (1.0 + th)
        act = (h * half).astype(BF)
        slope = half + (0.5 * GELU_A) * h * (1.0 - th * th) * (1.0 + 3.0 * GELU_B * square)
        active[rows, :] = act
        hidden = dot(grad_ref[rows, :], down_ref[0], NT) * slope
        low = hidden.astype(BF)
        hidden_grad[rows, :] = low
        total = total + jnp.sum(low.astype(F32), axis=0, keepdims=True)
        branch[rows, :] += dot(act, down_ref[0])
        shift[rows, :] += dot(low, up_ref[0], NT)
    bias_grad_ref[0] = total
    down_grad_ref[0] = dot(active[...], grad_ref[...], TN).astype(BF)
    up_grad_ref[0] = dot(input_ref[...], hidden_grad[...], TN).astype(BF)

    @pl.when(t == pl.num_programs(0) - 1)
    def _():
        first = pltpu.make_async_copy(branch, branch_out, sem.at[0])
        second = pltpu.make_async_copy(shift, shift_out, sem.at[1])
        first.start()
        second.start()
        first.wait()
        second.wait()


def feed(feed_input, feed_grad, ups, downs, up_bias):
    count = feed_input.shape[0]
    seqs, _, nf = ups.shape
    tm = 384 if count % 384 == 0 else count
    whole = once((count, D), lambda t: (0, 0))
    place = lambda t: (t, 0, 0)
    return pl.pallas_call(
        partial(feed_kernel, tm),
        grid_spec=pltpu.PrefetchScalarGridSpec(
            num_scalar_prefetch=0,
            grid=(seqs,),
            in_specs=[whole, whole, pl.BlockSpec((1, D, nf), place), pl.BlockSpec((1, nf, D), place),
                      pl.BlockSpec((1, 1, nf), place)],
            out_specs=[
                pl.BlockSpec(memory_space=pl.ANY),
                pl.BlockSpec(memory_space=pl.ANY),
                pl.BlockSpec((1, D, nf), place),
                pl.BlockSpec((1, nf, D), place),
                pl.BlockSpec((1, 1, nf), place),
            ],
            scratch_shapes=[
                pltpu.VMEM((count, D), F32),
                pltpu.VMEM((count, D), F32),
                pltpu.VMEM((count, nf), BF),
                pltpu.VMEM((count, nf), BF),
                pltpu.SemaphoreType.DMA((2,)),
            ],
        ),
        out_shape=[
            jax.ShapeDtypeStruct((count, D), F32),
            jax.ShapeDtypeStruct((count, D), F32),
            jax.ShapeDtypeStruct((seqs, D, nf), BF),
            jax.ShapeDtypeStruct((seqs, nf, D), BF),
            jax.ShapeDtypeStruct((seqs, 1, nf), F32),
        ],
        compiler_params=params(62),
        cost_estimate=cost(24 * FF // (4 * D), count, 16 * count * D + 8 * FF * D),
        name="feed",
    )(feed_input, feed_grad, ups, downs, up_bias)


def after_feed_kernel(
    branch_ref, shift_ref, middle_ref, gates_ref, mix_ref, cot_ref, out_ref, bias_ref,
    block_ref, late_ref, mix_grad_ref, attn_grad_ref, middle_grad_ref,
):
    cot = cot_ref[...].astype(F32)
    middle = middle_ref[...]
    branch = branch_ref[...] + bias_ref[...]
    block_ref[...] = (middle + gates_ref[2].astype(F32) * branch).astype(BF)
    late_ref[3] = (cot * branch).astype(BF)
    shift = shift_ref[...]
    late_ref[1] = shift.astype(BF)
    normed, inverse = norm_of(middle)
    late_ref[2] = (shift * normed).astype(BF)
    middle_grad = cot + norm_back(shift * (1.0 + gates_ref[1].astype(F32)), normed, inverse)
    middle_grad_ref[...] = middle_grad
    late_ref[0] = (middle_grad * mix_ref[...].astype(F32)).astype(BF)
    mix_grad = (middle_grad * gates_ref[0].astype(F32)).astype(BF)
    mix_grad_ref[...] = mix_grad
    attn_grad_ref[...] = dot(mix_grad, out_ref[...], NT).astype(BF)


def after_feed(branch, shift, middle, gates, mix, cot, out_mat, down_bias):
    count = branch.shape[0]
    tm = row_tile(count)
    rows = pl.BlockSpec((tm, D), lambda i: (i, 0))
    return pl.pallas_call(
        after_feed_kernel,
        grid=(count // tm,),
        in_specs=[rows, rows, rows, pl.BlockSpec((3, tm, D), lambda i: (0, i, 0)), rows, rows,
                  once((D, D), lambda i: (0, 0)), once((1, D), lambda i: (0, 0))],
        out_specs=[rows, pl.BlockSpec((4, tm, D), lambda i: (0, i, 0)), rows, rows, rows],
        out_shape=[
            jax.ShapeDtypeStruct((count, D), BF),
            jax.ShapeDtypeStruct((4, count, D), BF),
            jax.ShapeDtypeStruct((count, D), BF),
            jax.ShapeDtypeStruct((count, D), BF),
            jax.ShapeDtypeStruct((count, D), F32),
        ],
        compiler_params=params(),
        cost_estimate=cost(1, count, 44 * count * D),
        name="after_feed",
    )(branch, shift, middle, gates, mix, cot, out_mat, down_bias)


def token_products_kernel(order, act_ref, grad_ref, out_ref, sum_ref):
    grad = grad_ref[0]
    out_ref[0] = dot(act_ref[...], grad, TN).astype(BF)
    sum_ref[0] = jnp.sum(grad.astype(F32), axis=0, keepdims=True)


def token_products(order, act, grads):
    parts, count, _ = grads.shape
    return pl.pallas_call(
        token_products_kernel,
        grid_spec=pltpu.PrefetchScalarGridSpec(
            num_scalar_prefetch=1,
            grid=(parts,),
            in_specs=[once((count, D), lambda t, o: (0, 0)),
                      pl.BlockSpec((1, count, D), lambda t, o: (o[t], 0, 0))],
            out_specs=[pl.BlockSpec((1, D, D), lambda t, o: (t, 0, 0)),
                       pl.BlockSpec((1, 1, D), lambda t, o: (o[t], 0, 0))],
        ),
        out_shape=[
            jax.ShapeDtypeStruct((parts, D, D), BF),
            jax.ShapeDtypeStruct((parts, 1, D), F32),
        ],
        compiler_params=params(),
        cost_estimate=cost(parts, count, 2 * (parts + 1) * count * D + 2 * parts * D * D),
        name="token_products",
    )(order, act, grads)


def to_condition_kernel(parts, last, grads_ref, ada_ref, *refs):
    out_ref, total = refs[-2:]
    t = pl.program_id(1)
    part = dot(grads_ref[0], ada_ref[0], NT)

    @pl.when(t == 0)
    def _():
        total[...] = part + refs[0][...] if last else part

    @pl.when(t > 0)
    def _():
        total[...] += part

    @pl.when(t == parts - 1)
    def _():
        if last:
            cond = refs[1][...].astype(F32)
            gate = 1.0 / (1.0 + jnp.exp(-cond))
            out_ref[...] = total[...] * (gate * (1.0 + cond * (1.0 - gate)))
        else:
            out_ref[...] = total[...]


def to_condition(grads, ada, *rest):
    parts, count, _ = grads.shape
    tm = count // 2 if count % 32 == 0 else count
    rows = pl.BlockSpec((tm, D), lambda m, t: (m, 0))
    return pl.pallas_call(
        partial(to_condition_kernel, parts, len(rest) > 0),
        grid=(count // tm, parts),
        in_specs=[pl.BlockSpec((1, tm, D), lambda m, t: (t, m, 0)),
                  pl.BlockSpec((1, D, D), lambda m, t: (t, 0, 0))] + [rows] * len(rest),
        out_specs=rows,
        scratch_shapes=[pltpu.VMEM((tm, D), F32)],
        out_shape=jax.ShapeDtypeStruct((count, D), F32),
        compiler_params=params(),
        cost_estimate=cost(parts, count, 2 * parts * count * D + 12 * count * D),
        name="to_condition",
    )(grads, ada, *rest)


class Places:
    def __init__(self, packs, seqs):
        self.packs, self.seqs = packs, seqs
        self.rings, self.sides = packs // 2, seqs // 2
        self.pack = lax.axis_index("pack")
        self.seq = lax.axis_index("seq")
        self.a, self.b = self.pack // 2, self.pack % 2
        self.y, self.c = self.seq // 2, self.seq % 2

    def ring(self, value, k):
        n = self.rings
        pairs = [(a * 2 + b, ((a + k) % n) * 2 + b) for a in range(n) for b in range(2)]
        return lax.ppermute(value, "pack", pairs)

    def cross(self, value):
        return lax.ppermute(value, "pack", [(p, p ^ 1) for p in range(self.packs)])

    def side(self, value, k):
        n = self.sides
        pairs = [(y * 2 + c, ((y + k) % n) * 2 + c) for y in range(n) for c in range(2)]
        return lax.ppermute(value, "seq", pairs)

    def core(self, value):
        return lax.ppermute(value, "seq", [(s, s ^ 1) for s in range(self.seqs)])

    def gather_by(self, shard, members):
        groups = [[p * self.seqs + s for s in group for p in range(self.packs)] for group in members]
        out = lax.all_gather(
            shard, ("pack", "seq"), axis=0, tiled=True, axis_index_groups=groups
        )
        return out.reshape((len(members[0]), self.packs) + shard.shape)

    def gather_seq(self, value):
        whole = jnp.zeros((self.seqs,) + value.shape, value.dtype)
        rest = (0,) * value.ndim
        for k in range(self.sides):
            block = value if k == 0 else self.side(value, k)
            side = (self.y - k + self.sides) % self.sides
            whole = lax.dynamic_update_slice(whole, block[None], (side * 2 + self.c,) + rest)
            whole = lax.dynamic_update_slice(
                whole, self.core(block)[None], (side * 2 + 1 - self.c,) + rest
            )
        return whole

    def two(self, own, other):
        return jnp.where(self.c == 0, own, other), jnp.where(self.c == 0, other, own)

    def ring_blocks(self, value):
        return [value if k == 0 else self.ring(value, k) for k in range(self.rings)]

    def ring_join(self, blocks):
        rest = (0,) * blocks[0].ndim
        part = jnp.zeros((self.rings,) + blocks[0].shape, blocks[0].dtype)
        for k, block in enumerate(blocks):
            place = (self.a - k + self.rings) % self.rings
            part = lax.dynamic_update_slice(part, block[None], (place,) + rest)
        return part

    def cross_join(self, part, other):
        rest = (0,) * (part.ndim - 1)
        whole = jnp.zeros((self.rings, 2) + part.shape[1:], part.dtype)
        whole = lax.dynamic_update_slice(whole, part[:, None], (0, self.b) + rest)
        whole = lax.dynamic_update_slice(whole, other[:, None], (0, 1 - self.b) + rest)
        return whole.reshape((self.packs,) + part.shape[1:])

    def gather_pack(self, value):
        part = self.ring_join(self.ring_blocks(value))
        return self.cross_join(part, self.cross(part))

    def scatter_all(self, whole):
        r, n = whole.shape[2:]
        order = [[p * self.seqs + s for s in range(self.seqs) for p in range(self.packs)]]
        return lax.psum_scatter(
            whole.reshape(-1, n), ("pack", "seq"), scatter_dimension=0, tiled=True,
            axis_index_groups=order,
        )

    def reduce_core(self, pieces):
        give = lax.dynamic_index_in_dim(pieces, 1 - self.c, 1, False)
        keep = lax.dynamic_index_in_dim(pieces, self.c, 1, False)
        return add(keep, self.core(give), kind=pieces.dtype)

    def reduce_cross(self, whole):
        split = whole.reshape((whole.shape[0], self.rings, 2) + whole.shape[2:])
        give = lax.dynamic_index_in_dim(split, 1 - self.b, 2, False)
        keep = lax.dynamic_index_in_dim(split, self.b, 2, False)
        return add(keep, self.cross(give), kind=whole.dtype)

    def reduce_ring(self, part):
        groups = [[a * 2 + b for a in range(self.rings)] for b in range(2)]
        parts = lax.all_to_all(part, "pack", 1, 1, axis_index_groups=groups, tiled=True)
        return jnp.sum(parts.astype(F32), axis=1)

    def reduce_pack(self, whole):
        return self.reduce_ring(self.reduce_cross(whole[None]))[0]

    def reduce_side(self, pieces):
        terms = [lax.dynamic_index_in_dim(pieces, self.y, 0, False)]
        for k in range(1, self.sides):
            block = lax.dynamic_index_in_dim(pieces, (self.y + k) % self.sides, 0, False)
            terms.append(self.side(block, k))
        return add(*terms, kind=pieces.dtype)

def after(value, first):
    return lax.optimization_barrier((value, first))


def add(*terms, kind=BF):
    total = terms[0].astype(F32)
    for term in terms[1:]:
        total = total + term.astype(F32)
    return total.astype(kind)


def token_sum(gradient):
    return jnp.sum(gradient.astype(F32), axis=0)


def per_device(packs, seqs, tokens, condition, image_ids, ada_weight, attn_weight, out_weight,
               up_weight, down_weight, biases, cotangent):
    at = Places(packs, seqs)
    rows, own = image_ids.shape
    length = own * seqs
    count = rows * own
    hpd = HEADS // seqs
    w = hpd * HD
    r = D // packs
    rf = FF // packs
    n2 = 4 * D // seqs
    nf = FF // seqs

    bias_len = biases.shape[0]
    padded = -(-bias_len // 512) * 512
    half = D // 2
    ids = at.gather_seq(image_ids).transpose(1, 0, 2).reshape(rows, length)
    first = jnp.where(ids[0, length - 1] == 0, 0, 1)
    row_order = [first, 1 - first]

    def in_order(values):
        return jnp.where(
            first == 0, jnp.concatenate(values, axis=0), jnp.concatenate(values[::-1], axis=0)
        )

    if seqs == 4:
        left, right = ada_weight[:, :D], ada_weight[:, D:]
        head, tail = ada_weight[:, :half], ada_weight[:, half:]
        side_got = lax.ppermute(jnp.where(at.seq == 0, right, head), "seq", [(0, 2), (1, 3)])
        core_got = lax.ppermute(
            jnp.where(at.seq == 0, jnp.roll(left, half, axis=1), jnp.where(at.seq == 1, tail, left)),
            "seq", [(0, 1), (1, 0), (3, 2)],
        )
        shard1 = jnp.where(at.seq == 0, head, jnp.where(at.seq == 1, core_got[:, :half], side_got))
        shard1, biases, attn_weight, out_weight, down_weight, ada_weight = lax.optimization_barrier(
            (shard1, biases, attn_weight, out_weight, down_weight, ada_weight)
        )
        far_got = lax.ppermute(ada_weight[:, :D], "seq", [(2, 1)])
        merged = jnp.concatenate([ada_weight[:, D:], core_got[:, :half]], axis=1)
        shard2 = jnp.where(
            at.seq == 0, core_got,
            jnp.where(at.seq == 1, far_got, jnp.where(at.seq == 2, merged, ada_weight[:, half:])),
        )
        both = at.gather_seq(jnp.concatenate([attn_weight, out_weight], axis=1))
    else:
        both = lax.all_gather(
            jnp.concatenate([attn_weight, out_weight, ada_weight], axis=1), "seq", axis=0
        )
        ada_rows = both[:, :, attn_weight.shape[1] + out_weight.shape[1] :]
        ada_rows = ada_rows.transpose(1, 0, 2).reshape(r, 6 * D)
        shard1 = lax.dynamic_slice_in_dim(ada_rows, at.seq * (n2 // 2), n2 // 2, 1)
        shard2 = lax.dynamic_slice_in_dim(ada_rows, 2 * D + at.seq * n2, n2, 1)
    cut = attn_weight.shape[1]
    attn_rows = both[:, :, :cut].transpose(1, 0, 2).reshape(r, 3 * D)
    out_rows = both[:, :, cut : cut + out_weight.shape[1]].transpose(1, 0, 2).reshape(r, D)
    every = [range(seqs)]
    ada1 = at.gather_by(shard1, every)
    ada1 = ada1.reshape(4, seqs // 4, D, n2 // 2).transpose(0, 2, 1, 3).reshape(4, D, half)
    mine = lax.dynamic_slice_in_dim(attn_rows.reshape(r, 3, seqs, w), at.seq, 1, 2)
    attn_blocks = at.ring_blocks(mine.reshape(r, 3 * w))
    lined = jnp.pad(biases, (0, padded - bias_len)).reshape(-1, 128)
    offsets = at.gather_pack(at.gather_seq(lined)).reshape(packs, seqs, padded)
    offsets = offsets[:, :, :bias_len].reshape(-1)

    ada2 = at.gather_by(shard2, every)
    ada2 = ada2.reshape(4, seqs // 4, D, n2).transpose(0, 2, 1, 3).reshape(4, D, D)
    rq = rf // seqs
    down_rows = lax.all_to_all(down_weight, "seq", 0, 1, tiled=True)
    down_rows, up_weight, ada1 = lax.optimization_barrier((down_rows, up_weight, ada1))
    down_mat = lax.all_gather(down_rows, ("pack", "seq"), axis=0, tiled=True)
    down_mats = down_mat.reshape(seqs, nf, D)
    up_mats = at.gather_by(up_weight, every).reshape(seqs, D, nf)

    query_offset = offsets[6 * D : 7 * D]
    value_offset = offsets[7 * D : 8 * D]
    out_offset = offsets[8 * D : 9 * D]
    up_offset = offsets[9 * D : 9 * D + FF]
    down_offset = offsets[9 * D + FF :]

    x = tokens.reshape(count, D).astype(F32)
    cond_act, attn_input, scale_mix = mix_input(
        condition.reshape(count, D), tokens.reshape(count, D), ada1,
        offsets[: 2 * D].astype(F32).reshape(2, 1, D),
    )
    attn_input = attn_input.reshape(rows, own, D)
    head_offset = jnp.concatenate(
        [
            lax.dynamic_slice_in_dim(query_offset, at.seq * w, w),
            jnp.zeros((w,), BF),
            lax.dynamic_slice_in_dim(value_offset, at.seq * w, w),
        ]
    )

    wide = 640
    out_half = jnp.where(at.c == 0, out_rows[:, :wide], out_rows[:, D - wide :])
    attn_input, attn_blocks, out_half = lax.optimization_barrier((attn_input, attn_blocks, out_half))
    starts = [lax.dynamic_index_in_dim(attn_input, row, 0, False) for row in row_order]
    attn_part = at.ring_join(attn_blocks)
    attn_mat = at.cross_join(attn_part, at.cross(attn_part)).reshape(D, 3 * w)
    out_blocks = at.ring_blocks(out_half)

    inputs, qkvs, heads, lses, outs = [], [], [], [], []
    id_rows = [lax.dynamic_slice_in_dim(ids, row, 1, 0) for row in row_order]
    for row in range(rows):
        start = starts[row]
        blocks = []
        for k in range(at.sides):
            block = start if k == 0 else at.side(start, k)
            if k and row + 1 < rows:
                starts[row + 1], block = after(starts[row + 1], block)
            if k and row:
                block, heads[row - 1] = after(block, heads[row - 1])
            side = (at.y - k + at.sides) % at.sides
            blocks += [(side * 2 + at.c, block), (side * 2 + 1 - at.c, at.core(block))]
        inputs.append(blocks)
        qkv = jnp.zeros((seqs, own, 3 * w), BF)
        for place, block in blocks:
            part = (dot(block, attn_mat) + head_offset).astype(BF)
            qkv = lax.dynamic_update_slice(qkv, part[None], (place, 0, 0))
        qkvs.append(qkv.reshape(1, length, 3 * w))
        if row == 0:
            qkvs[0], out_blocks = after(qkvs[0], out_blocks)
            out_part = at.ring_join(out_blocks)
            out_other = at.cross(out_part)
        if row == 1:
            qkvs[1], out_other = after(qkvs[1], out_other)
            out_own = at.cross_join(out_part, out_other).reshape(D, wide)
            out_far = at.core(out_own)
        head, lse = attend_forward(qkvs[row], id_rows[row], hpd, 256, 768)
        heads.append(head)
        lses.append(lse)
    for row in range(rows):
        outs.append(lax.all_to_all(heads[row][0], "seq", 0, 1, tiled=True))
    out_left, out_right = at.two(out_own, out_far)
    out_mat = jnp.concatenate([out_left, out_right[:, 2 * wide - D :]], axis=1)

    def line(values, parts):
        return values.astype(F32).reshape(parts + (1, -1))

    attn_out = in_order(outs)
    gates, branch_mix, middle, feed_input, feed_out_grad = before_feed(
        cond_act, attn_out, tokens.reshape(count, D), cotangent.reshape(count, D), ada2, out_mat,
        line(offsets[2 * D : 6 * D], (4,)), line(out_offset, ()),
    )
    branch_feed, shift_sum, up_whole, down_whole, up_sums = feed(
        feed_input, feed_out_grad, up_mats, down_mats, line(up_offset, (seqs,))
    )
    block_out, late, mix_out_grad, attn_out_grad, middle_grad = after_feed(
        branch_feed, shift_sum, middle, gates, branch_mix, cotangent.reshape(count, D), out_mat,
        line(down_offset, ()),
    )

    attn_out_grad = attn_out_grad.reshape(rows, own, D)
    down_part = lax.psum_scatter(
        down_whole.reshape(FF, D), ("pack", "seq"), scatter_dimension=0, tiled=True
    )
    up_grad = at.scatter_all(up_whole.reshape(seqs, packs, r, nf)).astype(F32)
    grad_heads = [
        lax.all_to_all(
            lax.dynamic_index_in_dim(attn_out_grad, row, 0, False), "seq", 1, 0, tiled=True
        )
        for row in row_order
    ]
    out_whole = dot(attn_out, mix_out_grad, TN).astype(BF).reshape(packs, 2, r // 2, D)
    if seqs == 4:
        turn = jnp.stack([y * 2 + core for core in (1 - at.c, at.c) for y in range(2)])
        late_whole, late_sums = token_products(turn.astype(jnp.int32), cond_act, late)
        late_whole = late_whole.reshape(2, 2, packs, r, D)
        late_core = add(late_whole[1], at.core(late_whole[0]))
        out_core = at.reduce_core(out_whole)
        grad_heads[0], late_core, out_core = lax.optimization_barrier(
            (grad_heads[0], late_core, out_core)
        )
        late_pair = at.reduce_cross(late_core)
    else:
        late_whole, late_sums = token_products(jnp.arange(4, dtype=jnp.int32), cond_act, late)
        late_whole = late_whole.reshape(4, packs, r, seqs // 4, n2).transpose(0, 3, 1, 2, 4)
        ada_late = at.scatter_all(late_whole.reshape(seqs, packs, r, n2))
        out_core = at.reduce_core(out_whole)
    out_pair = at.reduce_cross(out_core[None])

    input_grads, flat_grads = [], []
    for row in range(rows):
        if row == 1 and seqs == 4:
            grad_heads[1], late_pair = after(grad_heads[1], late_pair)
            late_ring = at.reduce_ring(late_pair).astype(BF)
        if row == 1:
            grad_heads[1], out_pair = after(grad_heads[1], out_pair)
            out_ring = at.reduce_ring(out_pair)[0].astype(BF)
        grad = attend_backward(
            qkvs[row], grad_heads[row][None], heads[row], lses[row], id_rows[row], hpd, 256, 768
        )[0]
        flat_grads.append(grad)
        part = dot(grad, attn_mat, NT).astype(BF).reshape(at.sides, 2, own, D)
        input_grads.append(at.reduce_side(at.reduce_core(part)))
    late, flat_grads = after(late, flat_grads)
    cond_part = to_condition(late, ada2)
    input_grad = in_order(input_grads)
    out_side = at.reduce_side(out_ring.reshape(r // 2, at.sides, -1).transpose(1, 0, 2))
    out_side = out_side.reshape(r // 2, 2, -1).transpose(1, 0, 2)
    out_far = at.core(lax.dynamic_index_in_dim(out_side, 1 - at.c, 0, False))
    out_near = lax.dynamic_index_in_dim(out_side, at.c, 0, False)
    out_grad = jnp.concatenate(at.two(out_near, out_far)).astype(F32)
    if seqs == 4:
        ada_late = at.reduce_side(late_ring)
    attn_whole = 0.0
    for row in range(rows):
        for place, block in inputs[row]:
            piece = lax.dynamic_slice_in_dim(flat_grads[row], place * own, own, 0)
            attn_whole = attn_whole + dot(block, piece, TN)
    attn_part = at.reduce_pack(attn_whole.astype(BF).reshape(packs, r, 3 * w)).astype(BF)
    norm_x, inverse_x = norm_of(x)
    scale_mix_grad = (input_grad * norm_x).astype(BF)
    tokens_grad = middle_grad + norm_back(input_grad * (1.0 + scale_mix.astype(F32)), norm_x, inverse_x)
    shift_mix_grad = input_grad.astype(BF)
    early = jnp.stack([shift_mix_grad, scale_mix_grad])
    early_whole, early_sums = token_products(
        jnp.stack([1 - at.c, at.c]).astype(jnp.int32), cond_act, early
    )
    early_whole = early_whole.reshape(2, packs, r, D)
    early_core = add(early_whole[1], at.core(early_whole[0]))
    early_pack = at.reduce_pack(early_core).astype(BF)
    early_side = add(early_pack, *[at.side(early_pack, k) for k in range(1, at.sides)])
    ada1_parts = ada1.reshape(2, 2, D, half).transpose(0, 2, 1, 3).reshape(2, D, D)
    condition_grad = to_condition(early, ada1_parts, cond_part, condition.reshape(count, D))

    def own_columns(whole):
        n = whole.shape[1] // seqs
        return lax.dynamic_slice_in_dim(whole, at.seq * n, n, 1).astype(F32)

    if seqs == 4:
        early_half = lax.ppermute(early_side[:, :half], "seq", [(1, 0)])
        swapped = lax.ppermute(ada_late, "seq", [(0, 1), (1, 2)])
        late_half = lax.ppermute(ada_late[:, half:], "seq", [(2, 3)])
        whole_part = jnp.where(
            at.seq == 0, early_side, jnp.where(at.seq == 3, ada_late, swapped)
        )
        half_part = jnp.where(
            at.seq == 1, early_side[:, half:],
            jnp.where(at.seq == 2, ada_late[:, :half], early_half + late_half),
        )
        ada_grad = jnp.where(
            at.c == 0,
            jnp.concatenate([whole_part, half_part], axis=1),
            jnp.concatenate([half_part, whole_part], axis=1),
        ).astype(F32)
    else:
        early_all = jnp.concatenate(at.two(early_side, at.core(early_side)), axis=1)
        late_all = at.gather_seq(ada_late).transpose(1, 0, 2).reshape(r, 4 * D)
        ada_grad = own_columns(jnp.concatenate([early_all, late_all], axis=1))
    attn_all = at.gather_seq(attn_part).reshape(seqs, r, 3, w).transpose(1, 2, 0, 3).reshape(r, 3 * D)

    down_grad = lax.all_to_all(down_part, "seq", 1, 0, tiled=True).astype(F32)

    head_sum = sum(token_sum(g) for g in flat_grads).reshape(3, w)
    zero = jnp.zeros((D,), F32)
    head_sums = [
        lax.dynamic_update_slice_in_dim(zero, head_sum[i], at.seq * w, 0) for i in (0, 2)
    ]
    bias_whole = jnp.concatenate(
        [early_sums.reshape(-1), late_sums.reshape(-1)]
        + head_sums
        + [token_sum(mix_out_grad)]
        + [up_sums.reshape(-1)]
        + [token_sum(feed_out_grad)]
    )
    bias_whole = jnp.pad(bias_whole.reshape(packs, seqs, bias_len), ((0, 0), (0, 0), (0, padded - bias_len)))
    bias_whole = bias_whole.transpose(1, 0, 2).reshape(at.sides, 2, packs, padded // 128, 128)
    bias_part = at.reduce_side(at.reduce_core(bias_whole))
    bias_grad = at.reduce_pack(bias_part).reshape(-1)[:bias_len]
    return (
        block_out.reshape(tokens.shape),
        tokens_grad.reshape(tokens.shape),
        condition_grad.reshape(tokens.shape),
        ada_grad,
        own_columns(attn_all),
        out_grad,
        up_grad,
        down_grad,
        bias_grad,
    )


def solution(mesh):
    acts = P("pack", "seq", None)
    mats = P("pack", "seq")
    vec = P(("pack", "seq"))
    return jax.shard_map(
        partial(per_device, mesh.shape["pack"], mesh.shape["seq"]),
        mesh=mesh,
        in_specs=(acts, acts, mats, mats, mats, mats, mats, mats, vec, acts),
        out_specs=(acts, acts, acts, mats, mats, mats, mats, mats, vec),
        check_vma=False,
    )
```

time: 3720 us -> 1180 us (0.32)
  waiting for transfers between devices: 2240 us -> 179 us
  matrix products: 857 us -> 89.5 us
  Pallas kernels: 0 us -> 486 us
  other arithmetic: 311 us -> 101 us
  starting transfers between devices: 0.9 us -> 136 us
  blocking collectives: 102 us -> 9.64 us
    reduce_scatter x8 -> x2, waiting for transfers between devices: 1720 us -> 0.02 us  [the longest x1 0.02 us: per_device(): lax.psum_scatter(down_whole.reshape(FF, D), ('pack', 'seq'), scatter_dime...]
    dot_general x43 -> x19, matrix products: 857 us -> 89.5 us  [dot(): return lax.dot_general(a, b, dims, preferred_element_type=F32)]
    pallas_call x0 -> x12, Pallas kernels: none -> 486 us  [the longest x2 151 us: attend_backward(): pl.pallas_call(partial(backward_kernel, hpd, tq, tk), grid_spec=pltpu.Pre...]
    all_gather x10 -> x4, waiting for transfers between devices: 415 us -> 49.2 us  [the longest x3 49.2 us: gather_by(): lax.all_gather(shard, ('pack', 'seq'), axis=0, tiled=True, axis_index_gro...]
    convert_element_type x9 -> x23, other arithmetic: 143 us -> 46 us  [the longest x13 33.3 us: add(): return total.astype(kind)]
    unnamed x26 -> x6, waiting for transfers between devices: 97.5 us -> 0.1 us
    reduce_sum x12 -> x20, other arithmetic: 115 us -> 24.2 us  [the longest x4 6.87 us: token_sum(): return jnp.sum(gradient.astype(F32), axis=0)]
    ppermute x0 -> x55, starting transfers between devices: none -> 88.8 us  [the longest x9 41.6 us: ring(): return lax.ppermute(value, 'pack', pairs)]
  transfers between devices with their start and end apart: 22 -> 71, of which waited for: 17 -> 21; matrix products, arithmetic and copies ran while one was open for 18% -> 28% of each run, Pallas kernels for 0% -> 33%
where the time goes in v1:
time: 1180 us; the launch traced here: 1170 us
  Pallas kernels  486 us (41%)
  waiting for transfers between devices  179 us (15%)
  local copies, waits for them, and re-layouts  153 us (13%)
  starting transfers between devices  136 us (12%)
  other arithmetic  101 us (9%)
  matrix products  89.5 us (8%)
  between operations  16.9 us (1%)
    pallas_call x2, Pallas kernels, attend_backward(): pl.pallas_call(partial(backward_kernel, hpd, tq, tk), grid_spec=pltpu.Pre...  151 us
    pallas_call x1, Pallas kernels, feed(): pl.pallas_call(partial(feed_kernel, tm), grid_spec=pltpu.PrefetchScalarGr...  104 us
    pallas_call x2, Pallas kernels, attend_forward(): pl.pallas_call(partial(forward_kernel, hpd, tq, tk), grid_spec=pltpu.Pref...  91.8 us
    dot_general x19, matrix products, dot(): return lax.dot_general(a, b, dims, preferred_element_type=F32)  89.5 us
    all_to_all x5, waiting for transfers between devices, reduce_ring(): lax.all_to_all(part, 'pack', 1, 1, axis_index_groups=groups, tiled=True)  50.4 us
    all_gather x3, waiting for transfers between devices, gather_by(): lax.all_gather(shard, ('pack', 'seq'), axis=0, tiled=True, axis_index_gro...  49.2 us
    ppermute x9, starting transfers between devices, ring(): return lax.ppermute(value, 'pack', pairs)  41.6 us
    pallas_call x2, Pallas kernels, to_condition(): pl.pallas_call(partial(to_condition_kernel, parts, len(rest) > 0), grid=(...  40.5 us
  transfers between devices with their start and end apart: 71, of which 21 were waited for; matrix products, arithmetic and copies ran while one was open for 28% of the time, Pallas kernels for 33%

profile of v1, /device:TPU:1, one launch (start us, length us, event | category | flops | bytes accessed | tf_op | source)
XLA Modules:
  0.0 1169.8 jit_solution(13924758279831016185)
XLA Ops:
  12.0 4.6 collective-permute-start.1
  24.0 7.1 collective-permute-done.29
  32.6 9.6 all_to_all.133
  43.4 49.2 %all-gather.5.cloned.1.call-done = bf16[4608,576]{1,0:T(8,128)(2,1)} async-done(((bf16[144,576]{1,0:T(8,128)(2,1)}), bf16[4608,576]{1,0:T(8,128)(2,1)}) %all-gather.5.cloned.1.call-update) | async-done | bytes 5308432 | tf_op jit(solution)/shard_map/all_gather | solution.py:664
  151.9 15.0 %mix_input.1 = (bf16[1152,1152]{1,0:T(8,128)(2,1)}, bf16[1152,1152]{1,0:T(8,128)(2,1)}, bf16[1152,1152]{1,0:T(8,128)(2,1)}) custom-call(bf16[1152,1152]{1,0:T(8,128)(2,1)} %bitcast.386, bf16[1152,1152]{1,0:T(8,128)(2,1)} %bitcast.334, bf16[4,1152,576]{2,1,0:T(8,128)(2,1)} %bitcast.360, f32[2,1,1152]{2,1,0:T(1,128)} %slice_convert_fusion.2.bias_ref), custom_call_target="tpu_custom_call" | custom-call | flops 6115295232 | bytes 18579456 | tf_op jit(solution)/shard_map/mix_input/pallas_call | solution.py:378
  166.9 15.0 %collective-permute-done.16 = bf16[144,864]{1,0:T(8,128)(2,1)S(1)} collective-permute-done((bf16[144,864]{1,0:T(8,128)(2,1)S(1)}, bf16[144,864]{1,0:T(8,128)(2,1)S(1)}, u32[]{:S(2)}, u32[]{:S(2)}) %collective-permute-start.16) | collective-permute-done | bytes 248864 | tf_op jit(solution)/shard_map/ppermute | solution.py:649
  192.8 18.1 %collective-permute-start.23 = (bf16[144,640]{1,0:T(8,128)(2,1)S(1)}, bf16[144,640]{1,0:T(8,128)(2,1)S(1)}, u32[]{:S(2)}, u32[]{:S(2)}) collective-permute-start(bf16[144,640]{1,0:T(8,128)(2,1)S(1)} %slice_select_fusion.2), channel_id=1, source_target_pairs={{0,8},{4,12},{8,16},{12,20},{16,24},{20,28},{24,0},{28,4},{1,9},{5... | collective-permute-start | bytes 552968 | tf_op jit(solution)/shard_map/ppermute | solution.py:649
  211.8 14.3 %collective-permute-start.25 = (bf16[144,640]{1,0:T(8,128)(2,1)S(1)}, bf16[144,640]{1,0:T(8,128)(2,1)S(1)}, u32[]{:S(2)}, u32[]{:S(2)}) collective-permute-start(bf16[144,640]{1,0:T(8,128)(2,1)S(1)} %slice_select_fusion.2), channel_id=1, source_target_pairs={{0,24},{4,28},{8,0},{12,4},{16,8},{20,12},{24,16},{28,20},{1,25},{... | collective-permute-start | bytes 552968 | tf_op jit(solution)/shard_map/ppermute | solution.py:649
  246.2 53.9 %attend_forward.2 = (bf16[1,2304,288]{2,1,0:T(8,128)(2,1)}, f32[1,2304,128]{2,1,0:T(8,128)}) custom-call(s32[1,9]{1,0:T(1,128)} %bitcast.437, s32[1,9]{1,0:T(1,128)} %bitcast.438, bf16[1,2304,864]{2,1,0:T(8,128)(2,1)} %bitcast.379, bf16[1,2304,864]{2,1,0:T(8,128)(2,1)} %bitcast.380, s32[1,2304,1]{2,1,0:T(8,128)} %copy.309.ids_q.ids_ref, ...), custom_call_target="tpu_custom_call" | custom-call | flops 18345885696 | bytes 5308416 | tf_op jit(solution)/shard_map/attend_forward/pallas_call | solution.py:164
  304.0 4.6 all-to-all-start.1
  308.5 4.7 fusion.31
  321.2 37.9 %attend_forward.3 = (bf16[1,2304,288]{2,1,0:T(8,128)(2,1)}, f32[1,2304,128]{2,1,0:T(8,128)}) custom-call(s32[1,9]{1,0:T(1,128)} %bitcast.434, s32[1,9]{1,0:T(1,128)} %bitcast.433, bf16[1,2304,864]{2,1,0:T(8,128)(2,1)} %bitcast.382, bf16[1,2304,864]{2,1,0:T(8,128)(2,1)} %bitcast.383, s32[1,2304,1]{2,1,0:T(8,128)} %copy.312.ids_q.ids_ref, ...), custom_call_target="tpu_custom_call" | custom-call | flops 18345885696 | bytes 5308416 | tf_op jit(solution)/shard_map/attend_forward/pallas_call | solution.py:164
  362.8 4.4 all-to-all-start.2
  373.0 26.9 %all-to-all-done.2 = bf16[4,576,288]{1,2,0:T(8,128)(2,1)} async-done(((bf16[4,576,288]{1,2,0:T(8,128)(2,1)}), bf16[4,576,288]{1,2,0:T(8,128)(2,1)}, u32[]{:S(2)}, u32[]{:S(2)}) %all-to-all-start.2) | async-done | bytes 1327136 | tf_op jit(solution)/shard_map/all_to_all | solution.py:887
  411.6 28.2 %before_feed.1 = (bf16[3,1152,1152]{2,1,0:T(8,128)(2,1)}, bf16[1152,1152]{1,0:T(8,128)(2,1)}, f32[1152,1152]{1,0:T(8,128)}, bf16[1152,1152]{1,0:T(8,128)(2,1)}, bf16[1152,1152]{1,0:T(8,128)(2,1)}) custom-call(bf16[1152,1152]{1,0:T(8,128)(2,1)} %get-tuple-element.75.act_ref, bf16[1152,1152]{1,0:T(8,128)(2,1)} %maximum_select_fusion.attn_ref, ...), custom_call_target="tpu_custom_call" | custom-call | flops 15288238080 | bytes 45121536 | tf_op jit(solution)/shard_map/before_feed/pallas_call | solution.py:416
  439.9 104.3 %feed.1 = (f32[1152,1152]{1,0:T(8,128)}, f32[1152,1152]{1,0:T(8,128)}, bf16[4,1152,1152]{2,1,0:T(8,128)(2,1)}, bf16[4,1152,1152]{2,1,0:T(8,128)(2,1)}, f32[4,1,1152]{2,1,0:T(1,128)}) custom-call(bf16[1152,1152]{1,0:T(8,128)(2,1)} %get-tuple-element.99.input_ref, bf16[1152,1152]{1,0:T(8,128)(2,1)} %get-tuple-element.100.grad_ref, ...), custom_call_target="tpu_custom_call" | custom-call | flops 73383542784 | bytes 63700992 | tf_op jit(solution)/shard_map/feed/pallas_call | solution.py:489
  545.5 21.1 %after_feed.1 = (bf16[1152,1152]{1,0:T(8,128)(2,1)}, bf16[4,1152,1152]{2,1,0:T(8,128)(2,1)}, bf16[1152,1152]{1,0:T(8,128)(2,1)}, bf16[1152,1152]{1,0:T(8,128)(2,1)}, f32[1152,1152]{1,0:T(8,128)}) custom-call(f32[1152,1152]{1,0:T(8,128)} %get-tuple-element.103.branch_ref, f32[1152,1152]{1,0:T(8,128)} %get-tuple-element.104.shift_ref, ...), custom_call_target="tpu_custom_call" | custom-call | flops 3057647616 | bytes 58392576 | tf_op jit(solution)/shard_map/after_feed/pallas_call | solution.py:549
  566.6 21.0 %token_products.2 = (bf16[4,1152,1152]{2,1,0:T(8,128)(2,1)}, f32[4,1,1152]{2,1,0:T(1,128)}) custom-call(s32[4]{0:T(128)} %pad_add_fusion.order, bf16[1152,1152]{1,0:T(8,128)(2,1)} %get-tuple-element.75.act_ref, bf16[4,1152,1152]{2,1,0:T(8,128)(2,1)} %get-tuple-element.122.grad_ref.grads_ref), custom_call_target="tpu_custom_call" | custom-call | flops 12230590464 | bytes 23887872 | tf_op jit(solution)/shard_map/token_products/pallas_call | solution.py:576
  587.6 9.1 fusion.85
  603.1 4.5 all-to-all-start.3
  607.7 6.5 convolution_convert_fusion.2
  627.7 5.3 all-to-all-start.4
  636.7 8.9 copy.331
  645.6 8.8 copy.332.ada_ref
  669.3 5.9 fusion
  678.6 89.7 %attend_backward.2 = bf16[1,2304,864]{2,1,0:T(8,128)(2,1)} custom-call(s32[1,3]{1,0:T(1,128)} %bitcast.439, s32[1,3]{1,0:T(1,128)} %bitcast.440, bf16[1,2304,864]{2,1,0:T(8,128)(2,1)} %bitcast.381, bf16[1,2304,288]{2,1,0:T(8,128)(2,1)} %bitcast.408, bf16[1,2304,288]{2,1,0:T(8,128)(2,1)} %get-tuple-element.89.o_ref, ...), custom_call_target="tpu_custom_call" | custom-call | flops 45864714240 | bytes 11943936 | tf_op jit(solution)/shard_map/attend_backward/pallas_call | solution.py:288
  768.2 8.8 convolution_convert_fusion.1
  787.0 61.1 %attend_backward.3 = bf16[1,2304,864]{2,1,0:T(8,128)(2,1)} custom-call(s32[1,3]{1,0:T(1,128)} %bitcast.435, s32[1,3]{1,0:T(1,128)} %bitcast.436, bf16[1,2304,864]{2,1,0:T(8,128)(2,1)} %bitcast.384, bf16[1,2304,288]{2,1,0:T(8,128)(2,1)} %bitcast.407, bf16[1,2304,288]{2,1,0:T(8,128)(2,1)} %get-tuple-element.96.o_ref, ...), custom_call_target="tpu_custom_call" | custom-call | flops 45864714240 | bytes 11943936 | tf_op jit(solution)/shard_map/attend_backward/pallas_call | solution.py:288
  848.1 8.0 convolution_convert_fusion
  866.6 8.2 all-to-all-start.8
  878.5 5.2 fusion.45
  883.7 5.2 fusion.41
  892.7 5.1 fusion.39
  897.9 5.3 fusion.43
  905.4 10.7 fusion.14
  926.8 23.5 %to_condition.2.refs_0_ = f32[1152,1152]{1,0:T(8,128)} custom-call(bf16[4,1152,1152]{2,1,0:T(8,128)(2,1)} %get-tuple-element.122.grad_ref.grads_ref, bf16[4,1152,1152]{2,1,0:T(8,128)(2,1)} %bitcast.429), custom_call_target="tpu_custom_call" | custom-call | flops 12230590464 | bytes 26542080 | tf_op jit(solution)/shard_map/to_condition/pallas_call | solution.py:623
  964.7 12.9 %token_products.3 = (bf16[2,1152,1152]{2,1,0:T(8,128)(2,1)}, f32[2,1,1152]{2,1,0:T(1,128)}) custom-call(s32[2]{0:T(128)} %pad_add_fusion.1.order, bf16[1152,1152]{1,0:T(8,128)(2,1)} %get-tuple-element.75.act_ref, bf16[2,1152,1152]{2,1,0:T(8,128)(2,1)} %pad_maximum_fusion.grads_ref.grad_ref), custom_call_target="tpu_custom_call" | custom-call | flops 6115295232 | bytes 13271040 | tf_op jit(solution)/shard_map/token_products/pallas_call | solution.py:576
  981.9 5.5 fusion.86
  993.6 13.2 %all-to-all-done.7 = bf16[1,4,144,864]{3,2,0,1:T(8,128)(2,1)} async-done(((bf16[1,4,144,864]{3,2,0,1:T(8,128)(2,1)}), bf16[1,4,144,864]{3,2,0,1:T(8,128)(2,1)}, u32[]{:S(2)}, u32[]{:S(2)}) %all-to-all-start.7) | async-done | bytes 995360 | tf_op jit(solution)/shard_map/all_to_all | solution.py:727
  1017.9 5.0 collective-permute-done.48
  1026.0 5.0 reshape.1035
  1048.0 22.1 %all-to-all-done.6 = bf16[2,4,144,1152]{3,2,0,1:T(8,128)(2,1)S(1)} async-done(((bf16[2,4,144,1152]{3,2,0,1:T(8,128)(2,1)}), bf16[2,4,144,1152]{3,2,0,1:T(8,128)(2,1)S(1)}, u32[]{:S(2)}, u32[]{:S(2)}) %all-to-all-start.6) | async-done | bytes 2654240 | tf_op jit(solution)/shard_map/all_to_all | solution.py:727
  1078.2 4.8 all-to-all-start.5
  1083.0 6.3 fusion.13
  1094.7 4.4 collective-permute-start.43
  1099.2 15.1 %all-to-all-done.5 = bf16[1,4,144,1152]{3,2,0,1:T(8,128)(2,1)} async-done(((bf16[1,4,144,1152]{3,2,0,1:T(8,128)(2,1)}), bf16[1,4,144,1152]{3,2,0,1:T(8,128)(2,1)}, u32[]{:S(2)}, u32[]{:S(2)}) %all-to-all-start.5) | async-done | bytes 1327136 | tf_op jit(solution)/shard_map/all_to_all | solution.py:727
  1116.1 8.7 multiply_add_fusion
  1140.5 16.9 %to_condition.3 = f32[1152,1152]{1,0:T(8,128)} custom-call(bf16[2,1152,1152]{2,1,0:T(8,128)(2,1)} %pad_maximum_fusion.grads_ref.grad_ref, bf16[2,1152,1152]{2,1,0:T(8,128)(2,1)} %copy.332.ada_ref, f32[1152,1152]{1,0:T(8,128)} %to_condition.2.refs_0_, bf16[1152,1152]{1,0:T(8,128)(2,1)} %bitcast.387), custom_call_target="tpu_custom_call" | custom-call | flops 6115295232 | bytes 21233664 | tf_op jit(solution)/shard_map/to_condition/pallas_call | solution.py:623
  (496 shorter events, 313.2 us)
Async XLA Ops:
  7.2 85.4 %all-gather.5.cloned.1.call-start = ((), (), s32[]{:S(2)}) async-start(), calls=%async_computation.13 | async-start | bytes 6082560 | tf_op jit(solution)/shard_map/all_gather | solution.py:664
  22.6 389.1 %all-gather.7.cloned.1.call-start = ((), (), s32[]{:S(2)}) async-start(), calls=%async_computation.14 | async-start | bytes 10948608 | tf_op jit(solution)/shard_map/all_gather | solution.py:664
  32.3 407.6 %all-gather.9.cloned.1.call-start = ((), (), s32[]{:S(2)}) async-start(), calls=%async_computation.15 | async-start | bytes 10948608 | tf_op jit(solution)/shard_map/all_gather | solution.py:664
  92.6 347.3 %all-gather.11.cloned.1.call-start = ((), (), s32[]{:S(2)}) async-start(), calls=%async_computation.16 | async-start | bytes 10948608 | tf_op jit(solution)/shard_map/all_gather | solution.py:824
  99.6 25.6 %collective-permute-start.12 = (bf16[144,1152]{1,0:T(8,128)(2,1)S(1)}, bf16[144,1152]{1,0:T(8,128)(2,1)S(1)}, u32[]{:S(2)}, u32[]{:S(2)}) collective-permute-start(bf16[144,1152]{1,0:T(8,128)(2,1)S(1)} %pad_maximum_fusion.2), channel_id=1, source_target_pairs={{0,1},{1,0},{2,3},{3,2},{4,5},{5,4},{6,7},{7,6},{8,9},{9,8},{10,11... | collective-permute-start | bytes 995336 | tf_op jit(solution)/shard_map/ppermute | solution.py:660
  100.0 21.7 %collective-permute-start.13 = (bf16[144,1152]{1,0:T(8,128)(2,1)S(1)}, bf16[144,1152]{1,0:T(8,128)(2,1)S(1)}, u32[]{:S(2)}, u32[]{:S(2)}) collective-permute-start(bf16[144,1152]{1,0:T(8,128)(2,1)S(1)} %pad_maximum_fusion.2), channel_id=1, source_target_pairs={{0,2},{1,3},{2,0},{3,1},{4,6},{5,7},{6,4},{7,5},{8,10},{9,11},{10,... | collective-permute-start | bytes 995336 | tf_op jit(solution)/shard_map/ppermute | solution.py:657
  147.1 19.9 %collective-permute-start.15 = (bf16[144,864]{1,0:T(8,128)(2,1)S(1)}, bf16[144,864]{1,0:T(8,128)(2,1)S(1)}, u32[]{:S(2)}, u32[]{:S(2)}) collective-permute-start(bf16[144,864]{1,0:T(8,128)(2,1)S(1)} %reshape.1010), channel_id=1, source_target_pairs={{0,8},{4,12},{8,16},{12,20},{16,24},{20,28},{24,0},{28,4},{1,9},{5... | collective-permute-start | bytes 746504 | tf_op jit(solution)/shard_map/ppermute | solution.py:649
  148.3 33.6 %collective-permute-start.16 = (bf16[144,864]{1,0:T(8,128)(2,1)S(1)}, bf16[144,864]{1,0:T(8,128)(2,1)S(1)}, u32[]{:S(2)}, u32[]{:S(2)}) collective-permute-start(bf16[144,864]{1,0:T(8,128)(2,1)S(1)} %reshape.1010), channel_id=1, source_target_pairs={{0,16},{4,20},{8,24},{12,28},{16,0},{20,4},{24,8},{28,12},{1,17},{... | collective-permute-start | bytes 746504 | tf_op jit(solution)/shard_map/ppermute | solution.py:649
  151.2 30.7 %collective-permute-start.17 = (bf16[144,864]{1,0:T(8,128)(2,1)S(1)}, bf16[144,864]{1,0:T(8,128)(2,1)S(1)}, u32[]{:S(2)}, u32[]{:S(2)}) collective-permute-start(bf16[144,864]{1,0:T(8,128)(2,1)S(1)} %reshape.1010), channel_id=1, source_target_pairs={{0,24},{4,28},{8,0},{12,4},{16,8},{20,12},{24,16},{28,20},{1,25},{... | collective-permute-start | bytes 746504 | tf_op jit(solution)/shard_map/ppermute | solution.py:649
  182.2 29.6 %collective-permute-start.20 = (bf16[4,144,864]{2,1,0:T(8,128)(2,1)S(1)}, bf16[4,144,864]{2,1,0:T(8,128)(2,1)}, u32[]{:S(2)}, u32[]{:S(2)}) collective-permute-start(bf16[4,144,864]{2,1,0:T(8,128)(2,1)S(1)} %bitcast_dynamic-update-slice_fusion.8), channel_id=1, source_target_pairs={{0,4},{4,0},{8,12},{12,8},{16,20},{20,16},{24,28},{28,24},{1,5},{5... | collective-permute-start | bytes 2985992 | tf_op jit(solution)/shard_map/ppermute | solution.py:652
  185.1 42.3 %collective-permute-start.18 = (bf16[576,1152]{1,0:T(8,128)(2,1)}, bf16[576,1152]{1,0:T(8,128)(2,1)}, u32[]{:S(2)}, u32[]{:S(2)}) collective-permute-start(bf16[576,1152]{1,0:T(8,128)(2,1)} %get-tuple-element.218), channel_id=1, source_target_pairs={{0,2},{1,3},{2,0},{3,1},{4,6},{5,7},{6,4},{7,5},{8,10},{9,11},{10,... | collective-permute-start | bytes 3981320 | tf_op jit(solution)/shard_map/ppermute | solution.py:657
  187.2 45.0 %collective-permute-start.21 = (bf16[576,1152]{1,0:T(8,128)(2,1)}, bf16[576,1152]{1,0:T(8,128)(2,1)S(1)}, u32[]{:S(2)}, u32[]{:S(2)}) collective-permute-start(bf16[576,1152]{1,0:T(8,128)(2,1)} %get-tuple-element.218), channel_id=1, source_target_pairs={{0,1},{1,0},{2,3},{3,2},{4,5},{5,4},{6,7},{7,6},{8,9},{9,8},{10,11... | collective-permute-start | bytes 3981320 | tf_op jit(solution)/shard_map/ppermute | solution.py:660
  192.8 51.4 %collective-permute-start.23 = (bf16[144,640]{1,0:T(8,128)(2,1)S(1)}, bf16[144,640]{1,0:T(8,128)(2,1)S(1)}, u32[]{:S(2)}, u32[]{:S(2)}) collective-permute-start(bf16[144,640]{1,0:T(8,128)(2,1)S(1)} %slice_select_fusion.2), channel_id=1, source_target_pairs={{0,8},{4,12},{8,16},{12,20},{16,24},{20,28},{24,0},{28,4},{1,9},{5... | collective-permute-start | bytes 552968 | tf_op jit(solution)/shard_map/ppermute | solution.py:649
  210.9 33.3 %collective-permute-start.24 = (bf16[144,640]{1,0:T(8,128)(2,1)S(1)}, bf16[144,640]{1,0:T(8,128)(2,1)S(1)}, u32[]{:S(2)}, u32[]{:S(2)}) collective-permute-start(bf16[144,640]{1,0:T(8,128)(2,1)S(1)} %slice_select_fusion.2), channel_id=1, source_target_pairs={{0,16},{4,20},{8,24},{12,28},{16,0},{20,4},{24,8},{28,12},{1,17},{... | collective-permute-start | bytes 552968 | tf_op jit(solution)/shard_map/ppermute | solution.py:649
  211.8 32.4 %collective-permute-start.25 = (bf16[144,640]{1,0:T(8,128)(2,1)S(1)}, bf16[144,640]{1,0:T(8,128)(2,1)S(1)}, u32[]{:S(2)}, u32[]{:S(2)}) collective-permute-start(bf16[144,640]{1,0:T(8,128)(2,1)S(1)} %slice_select_fusion.2), channel_id=1, source_target_pairs={{0,24},{4,28},{8,0},{12,4},{16,8},{20,12},{24,16},{28,20},{1,25},{... | collective-permute-start | bytes 552968 | tf_op jit(solution)/shard_map/ppermute | solution.py:649
  232.2 67.9 %collective-permute-start.19 = (bf16[576,1152]{1,0:T(8,128)(2,1)}, bf16[576,1152]{1,0:T(8,128)(2,1)}, u32[]{:S(2)}, u32[]{:S(2)}) collective-permute-start(bf16[576,1152]{1,0:T(8,128)(2,1)} %get-tuple-element.80), channel_id=1, source_target_pairs={{0,2},{1,3},{2,0},{3,1},{4,6},{5,7},{6,4},{7,5},{8,10},{9,11},{10,... | collective-permute-start | bytes 3981320 | tf_op jit(solution)/shard_map/ppermute | solution.py:657
  241.8 66.7 %collective-permute-start.26 = (bf16[576,1152]{1,0:T(8,128)(2,1)}, bf16[576,1152]{1,0:T(8,128)(2,1)}, u32[]{:S(2)}, u32[]{:S(2)}) collective-permute-start(bf16[576,1152]{1,0:T(8,128)(2,1)} %get-tuple-element.80), channel_id=1, source_target_pairs={{0,1},{1,0},{2,3},{3,2},{4,5},{5,4},{6,7},{7,6},{8,9},{9,8},{10,11... | collective-permute-start | bytes 3981320 | tf_op jit(solution)/shard_map/ppermute | solution.py:660
  301.0 20.2 %collective-permute-start.28 = (bf16[4,144,640]{2,1,0:T(8,128)(2,1)S(1)}, bf16[4,144,640]{2,1,0:T(8,128)(2,1)}, u32[]{:S(2)}, u32[]{:S(2)}) collective-permute-start(bf16[4,144,640]{2,1,0:T(8,128)(2,1)S(1)} %bitcast_dynamic-update-slice_fusion.12), channel_id=1, source_target_pairs={{0,4},{4,0},{8,12},{12,8},{16,20},{20,16},{24,28},{28,24},{1,5},{5... | collective-permute-start | bytes 2211848 | tf_op jit(solution)/shard_map/ppermute | solution.py:652
  304.0 58.8 %all-to-all-start.1 = ((bf16[4,576,288]{1,2,0:T(8,128)(2,1)}), bf16[4,576,288]{1,2,0:T(8,128)(2,1)S(1)}, u32[]{:S(2)}, u32[]{:S(2)}) async-start(bf16[4,576,288]{1,2,0:T(8,128)(2,1)} %copy.311), calls=%async_computation.1 | async-start | bytes 2949120 | tf_op jit(solution)/shard_map/all_to_all | solution.py:887
  362.8 37.1 %all-to-all-start.2 = ((bf16[4,576,288]{1,2,0:T(8,128)(2,1)}), bf16[4,576,288]{1,2,0:T(8,128)(2,1)}, u32[]{:S(2)}, u32[]{:S(2)}) async-start(bf16[4,576,288]{1,2,0:T(8,128)(2,1)} %copy.314), calls=%async_computation.2 | async-start | bytes 2949120 | tf_op jit(solution)/shard_map/all_to_all | solution.py:887
  367.2 762.3 %reduce-scatter.5.cloned.1.call-start = ((), (), s32[]{:S(2)}) async-start(), calls=%async_computation.18 | async-start | bytes 10948608 | tf_op jit(solution)/shard_map/reduce_scatter | solution.py:908
  369.8 37.0 %collective-permute-start.30 = (bf16[1152,640]{1,0:T(8,128)(2,1)S(1)}, bf16[1152,640]{1,0:T(8,128)(2,1)}, u32[]{:S(2)}, u32[]{:S(2)}) collective-permute-start(bf16[1152,640]{1,0:T(8,128)(2,1)S(1)} %bitcast.345), channel_id=1, source_target_pairs={{0,1},{1,0},{2,3},{3,2},{4,5},{5,4},{6,7},{7,6},{8,9},{9,8},{10,11... | collective-permute-start | bytes 4423688 | tf_op jit(solution)/shard_map/ppermute | solution.py:660
  596.7 72.6 %collective-permute-start.31 = (bf16[2,8,144,1152]{3,2,1,0:T(8,128)(2,1)}, bf16[2,8,144,1152]{3,2,1,0:T(8,128)(2,1)}, u32[]{:S(2)}, u32[]{:S(2)}) collective-permute-start(bf16[2,8,144,1152]{3,2,1,0:T(8,128)(2,1)} %bitcast.365), channel_id=1, source_target_pairs={{0,1},{1,0},{2,3},{3,2},{4,5},{5,4},{6,7},{7,6},{8,9},{9,8},{10,11... | collective-permute-start | bytes 15925256 | tf_op jit(solution)/shard_map/ppermute | solution.py:660
  603.1 24.6 %all-to-all-start.3 = ((bf16[576,4,288]{0,2,1:T(8,128)(2,1)}), bf16[576,4,288]{0,2,1:T(8,128)(2,1)}, u32[]{:S(2)}, u32[]{:S(2)}) async-start(bf16[576,4,288]{0,2,1:T(8,128)(2,1)} %bitcast.362), calls=%async_computation.3 | async-start | bytes 2949120 | tf_op jit(solution)/shard_map/all_to_all | solution.py:913
  616.8 50.4 %collective-permute-start.32 = (bf16[8,72,1152]{2,1,0:T(8,128)(2,1)}, bf16[8,72,1152]{2,1,0:T(8,128)(2,1)}, u32[]{:S(2)}, u32[]{:S(2)}) collective-permute-start(bf16[8,72,1152]{2,1,0:T(8,128)(2,1)} %dynamic-slice_bitcast_fusion.6), channel_id=1, source_target_pairs={{0,1},{1,0},{2,3},{3,2},{4,5},{5,4},{6,7},{7,6},{8,9},{9,8},{10,11... | collective-permute-start | bytes 3981320 | tf_op jit(solution)/shard_map/ppermute | solution.py:660
  627.7 37.1 %all-to-all-start.4 = ((bf16[576,4,288]{0,2,1:T(8,128)(2,1)}), bf16[576,4,288]{0,2,1:T(8,128)(2,1)S(1)}, u32[]{:S(2)}, u32[]{:S(2)}) async-start(bf16[576,4,288]{0,2,1:T(8,128)(2,1)} %bitcast.102), calls=%async_computation.4 | async-start | bytes 2949120 | tf_op jit(solution)/shard_map/all_to_all | solution.py:913
  633.0 525.0 %reduce-scatter.3.cloned.1.call-start = ((), (), s32[]{:S(2)}) async-start(), calls=%async_computation.17 | async-start | bytes 10948608 | tf_op jit(solution)/shard_map/reduce_scatter | solution.py:709
  675.2 105.6 %collective-permute-start.36 = (bf16[1,4,72,1152]{3,2,1,0:T(8,128)(2,1)S(1)}, bf16[1,4,72,1152]{3,2,1,0:T(8,128)(2,1)}, u32[]{:S(2)}, u32[]{:S(2)}) collective-permute-start(bf16[1,4,72,1152]{3,2,1,0:T(8,128)(2,1)S(1)} %dynamic-slice_bitcast_fusion.10), channel_id=1, source_target_pairs={{0,4},{4,0},{8,12},{12,8},{16,20},{20,16},{24,28},{28,24},{1,5},{5... | collective-permute-start | bytes 1990664 | tf_op jit(solution)/shard_map/ppermute | solution.py:652
  678.5 104.4 %collective-permute-start.35 = (bf16[2,4,144,1152]{3,2,1,0:T(8,128)(2,1)}, bf16[2,4,144,1152]{3,2,1,0:T(8,128)(2,1)}, u32[]{:S(2)}, u32[]{:S(2)}) collective-permute-start(bf16[2,4,144,1152]{3,2,1,0:T(8,128)(2,1)} %dynamic-slice_bitcast_fusion.1), channel_id=1, source_target_pairs={{0,4},{4,0},{8,12},{12,8},{16,20},{20,16},{24,28},{28,24},{1,5},{5... | collective-permute-start | bytes 7962632 | tf_op jit(solution)/shard_map/ppermute | solution.py:652
  780.2 79.8 %collective-permute-start.33 = (bf16[2,576,1152]{2,1,0:T(8,128)(2,1)}, bf16[2,576,1152]{2,1,0:T(8,128)(2,1)}, u32[]{:S(2)}, u32[]{:S(2)}) collective-permute-start(bf16[2,576,1152]{2,1,0:T(8,128)(2,1)} %dynamic-slice_bitcast_fusion.2), channel_id=1, source_target_pairs={{0,1},{1,0},{2,3},{3,2},{4,5},{5,4},{6,7},{7,6},{8,9},{9,8},{10,11... | collective-permute-start | bytes 7962632 | tf_op jit(solution)/shard_map/ppermute | solution.py:660
  860.0 62.4 %collective-permute-start.37 = (bf16[2,576,1152]{2,1,0:T(8,128)(2,1)}, bf16[2,576,1152]{2,1,0:T(8,128)(2,1)}, u32[]{:S(2)}, u32[]{:S(2)}) collective-permute-start(bf16[2,576,1152]{2,1,0:T(8,128)(2,1)} %dynamic-slice_bitcast_fusion), channel_id=1, source_target_pairs={{0,1},{1,0},{2,3},{3,2},{4,5},{5,4},{6,7},{7,6},{8,9},{9,8},{10,11... | collective-permute-start | bytes 7962632 | tf_op jit(solution)/shard_map/ppermute | solution.py:660
  865.0 88.2 %collective-permute-start.34 = (bf16[576,1152]{1,0:T(8,128)(2,1)}, bf16[576,1152]{1,0:T(8,128)(2,1)}, u32[]{:S(2)}, u32[]{:S(2)}) collective-permute-start(bf16[576,1152]{1,0:T(8,128)(2,1)} %dynamic-slice_bitcast_fusion.5), channel_id=1, source_target_pairs={{0,2},{1,3},{2,0},{3,1},{4,6},{5,7},{6,4},{7,5},{8,10},{9,11},{10,... | collective-permute-start | bytes 3981320 | tf_op jit(solution)/shard_map/ppermute | solution.py:657
  866.6 111.0 %all-to-all-start.8 = ((bf16[1,4,72,1152]{3,2,0,1:T(8,128)(2,1)}), bf16[1,4,72,1152]{3,2,0,1:T(8,128)(2,1)S(1)}, u32[]{:S(2)}, u32[]{:S(2)}) async-start(bf16[1,4,72,1152]{3,2,0,1:T(8,128)(2,1)} %bitcast.392), calls=%async_computation.8 | async-start | bytes 1327104 | tf_op jit(solution)/shard_map/all_to_all | solution.py:727
  922.4 27.9 %collective-permute-start.46 = (bf16[1,4,144,864]{3,2,1,0:T(8,128)(2,1)}, bf16[1,4,144,864]{3,2,1,0:T(8,128)(2,1)}, u32[]{:S(2)}, u32[]{:S(2)}) collective-permute-start(bf16[1,4,144,864]{3,2,1,0:T(8,128)(2,1)} %dynamic-slice_bitcast_fusion.9), channel_id=1, source_target_pairs={{0,4},{4,0},{8,12},{12,8},{16,20},{20,16},{24,28},{28,24},{1,5},{5... | collective-permute-start | bytes 2985992 | tf_op jit(solution)/shard_map/ppermute | solution.py:652
  926.8 30.3 %collective-permute-start.38 = (bf16[576,1152]{1,0:T(8,128)(2,1)}, bf16[576,1152]{1,0:T(8,128)(2,1)}, u32[]{:S(2)}, u32[]{:S(2)}) collective-permute-start(bf16[576,1152]{1,0:T(8,128)(2,1)} %dynamic-slice_bitcast_fusion.4), channel_id=1, source_target_pairs={{0,2},{1,3},{2,0},{3,1},{4,6},{5,7},{6,4},{7,5},{8,10},{9,11},{10,... | collective-permute-start | bytes 3981320 | tf_op jit(solution)/shard_map/ppermute | solution.py:657
  977.6 29.2 %all-to-all-start.7 = ((bf16[1,4,144,864]{3,2,0,1:T(8,128)(2,1)}), bf16[1,4,144,864]{3,2,0,1:T(8,128)(2,1)}, u32[]{:S(2)}, u32[]{:S(2)}) async-start(bf16[1,4,144,864]{3,2,0,1:T(8,128)(2,1)} %fusion.38), calls=%async_computation.7 | async-start | bytes 2064384 | tf_op jit(solution)/shard_map/all_to_all | solution.py:727
  987.4 50.8 %collective-permute-start.39 = (bf16[8,144,1152]{2,1,0:T(8,128)(2,1)}, bf16[8,144,1152]{2,1,0:T(8,128)(2,1)}, u32[]{:S(2)}, u32[]{:S(2)}) collective-permute-start(bf16[8,144,1152]{2,1,0:T(8,128)(2,1)} %bitcast.127), channel_id=1, source_target_pairs={{0,1},{1,0},{2,3},{3,2},{4,5},{5,4},{6,7},{7,6},{8,9},{9,8},{10,11... | collective-permute-start | bytes 7962632 | tf_op jit(solution)/shard_map/ppermute | solution.py:660
  991.5 19.0 %collective-permute-start.50 = (bf16[72,576]{1,0:T(8,128)(2,1)S(1)}, bf16[72,576]{1,0:T(8,128)(2,1)S(1)}, u32[]{:S(2)}, u32[]{:S(2)}) collective-permute-start(bf16[72,576]{1,0:T(8,128)(2,1)S(1)} %bitcast.418), channel_id=1, source_target_pairs={{0,2},{1,3},{2,0},{3,1},{4,6},{5,7},{6,4},{7,5},{8,10},{9,11},{10,... | collective-permute-start | bytes 248840 | tf_op jit(solution)/shard_map/ppermute | solution.py:657
  1006.8 63.3 %all-to-all-start.6 = ((bf16[2,4,144,1152]{3,2,0,1:T(8,128)(2,1)}), bf16[2,4,144,1152]{3,2,0,1:T(8,128)(2,1)S(1)}, u32[]{:S(2)}, u32[]{:S(2)}) async-start(bf16[2,4,144,1152]{3,2,0,1:T(8,128)(2,1)} %copy.334), calls=%async_computation.6 | async-start | bytes 5308416 | tf_op jit(solution)/shard_map/all_to_all | solution.py:727
  1044.1 31.0 %collective-permute-start.40 = (bf16[1,4,144,1152]{3,2,1,0:T(8,128)(2,1)}, bf16[1,4,144,1152]{3,2,1,0:T(8,128)(2,1)}, u32[]{:S(2)}, u32[]{:S(2)}) collective-permute-start(bf16[1,4,144,1152]{3,2,1,0:T(8,128)(2,1)} %dynamic-slice_bitcast_fusion.3), channel_id=1, source_target_pairs={{0,4},{4,0},{8,12},{12,8},{16,20},{20,16},{24,28},{28,24},{1,5},{5... | collective-permute-start | bytes 3981320 | tf_op jit(solution)/shard_map/ppermute | solution.py:652
  1047.6 41.7 %collective-permute-start.52 = (f32[2,8,4,128]{3,1,2,0:T(8,128)S(1)}, f32[2,8,4,128]{3,1,2,0:T(8,128)S(1)}, u32[]{:S(2)}, u32[]{:S(2)}) collective-permute-start(f32[2,8,4,128]{3,1,2,0:T(8,128)S(1)} %dynamic-slice_bitcast_fusion.12), channel_id=1, source_target_pairs={{0,1},{1,0},{2,3},{3,2},{4,5},{5,4},{6,7},{7,6},{8,9},{9,8},{10,11... | collective-permute-start | bytes 98312 | tf_op jit(solution)/shard_map/ppermute | solution.py:660
  1071.7 22.0 %collective-permute-start.42 = (bf16[144,1152]{1,0:T(8,128)(2,1)}, bf16[144,1152]{1,0:T(8,128)(2,1)}, u32[]{:S(2)}, u32[]{:S(2)}) collective-permute-start(bf16[144,1152]{1,0:T(8,128)(2,1)} %dynamic-slice_bitcast_fusion.11), channel_id=1, source_target_pairs={{0,2},{1,3},{2,0},{3,1},{4,6},{5,7},{6,4},{7,5},{8,10},{9,11},{10,... | collective-permute-start | bytes 995336 | tf_op jit(solution)/shard_map/ppermute | solution.py:657
  1078.2 36.1 %all-to-all-start.5 = ((bf16[1,4,144,1152]{3,2,0,1:T(8,128)(2,1)}), bf16[1,4,144,1152]{3,2,0,1:T(8,128)(2,1)}, u32[]{:S(2)}, u32[]{:S(2)}) async-start(bf16[1,4,144,1152]{3,2,0,1:T(8,128)(2,1)} %fusion.36), calls=%async_computation.5 | async-start | bytes 2654208 | tf_op jit(solution)/shard_map/all_to_all | solution.py:727
  1092.4 32.4 %collective-permute-start.54 = (f32[1,4,4,128]{3,2,1,0:T(4,128)S(1)}, f32[1,4,4,128]{3,2,1,0:T(4,128)S(1)}, u32[]{:S(2)}, u32[]{:S(2)}) collective-permute-start(f32[1,4,4,128]{3,2,1,0:T(4,128)S(1)} %bitcast.422), channel_id=1, source_target_pairs={{0,4},{4,0},{8,12},{12,8},{16,20},{20,16},{24,28},{28,24},{1,5},{5... | collective-permute-start | bytes 24584 | tf_op jit(solution)/shard_map/ppermute | solution.py:652
  1094.7 37.0 %collective-permute-start.43 = (bf16[144,1152]{1,0:T(8,128)(2,1)S(1)}, bf16[144,1152]{1,0:T(8,128)(2,1)}, u32[]{:S(2)}, u32[]{:S(2)}) collective-permute-start(bf16[144,1152]{1,0:T(8,128)(2,1)S(1)} %fusion.53), channel_id=1, source_target_pairs={{0,1},{1,2},{4,5},{5,6},{8,9},{9,10},{12,13},{13,14},{16,17},{17,1... | collective-permute-start | bytes 995336 | tf_op jit(solution)/shard_map/ppermute | solution.py:987
  1128.8 32.3 %collective-permute-start.45 = (bf16[144,576]{1,0:T(8,128)(2,1)S(1)}, bf16[144,576]{1,0:T(8,128)(2,1)S(1)}, u32[]{:S(2)}, u32[]{:S(2)}) collective-permute-start(bf16[144,576]{1,0:T(8,128)(2,1)S(1)} %slice.222), channel_id=1, source_target_pairs={{2,3},{6,7},{10,11},{14,15},{18,19},{22,23},{26,27},{30,31}} | collective-permute-start | bytes 497672 | tf_op jit(solution)/shard_map/ppermute | solution.py:988
  1133.0 28.1 %collective-permute-start.44 = (bf16[144,576]{1,0:T(8,128)(2,1)S(1)}, bf16[144,576]{1,0:T(8,128)(2,1)S(1)}, u32[]{:S(2)}, u32[]{:S(2)}) collective-permute-start(bf16[144,576]{1,0:T(8,128)(2,1)S(1)} %slice.221), channel_id=1, source_target_pairs={{1,0},{5,4},{9,8},{13,12},{17,16},{21,20},{25,24},{29,28}} | collective-permute-start | bytes 497672 | tf_op jit(solution)/shard_map/ppermute | solution.py:986
  1136.7 23.2 %all-to-all-start.9 = ((bf16[144,4,288]{2,0,1:T(8,128)(2,1)}), bf16[144,4,288]{2,0,1:T(8,128)(2,1)S(1)}, u32[]{:S(2)}, u32[]{:S(2)}) async-start(bf16[144,4,288]{2,0,1:T(8,128)(2,1)} %copy.339), calls=%async_computation.11 | async-start | bytes 884736 | tf_op jit(solution)/shard_map/all_to_all | solution.py:1007
  (94 other events, 1668.9 us)
Sparse Core Ops, SparseCore 0:
  22.7 69.8 all-gather.4
  96.1 107.5 all-gather.6
  206.7 101.0 all-gather.8
  311.2 98.0 all-gather.10
  544.4 148.3 reduce-scatter.4
  698.7 139.7 reduce-scatter.2

commit v2 on v1

--- a/solution.py
+++ b/solution.py
@@ -33,13 +33,33 @@
     return lax.broadcasted_iota(jnp.int32, (n, w), 1)
 
 
-def pick(width, out_width, offset, copies):
-    r = lax.broadcasted_iota(jnp.int32, (width, out_width), 0) - offset
-    c = lax.broadcasted_iota(jnp.int32, (width, out_width), 1)
+def window(first, limit):
+    lo = first // 128 * 128
+    return lo, min(lo + 256, limit)
+
+
+def pickers(hpd, parts, limit, out_width, copies):
+    firsts = [part * hpd * HD + h * HD for part in parts for h in range(hpd)]
+    offsets = jnp.array([f - window(f, limit)[0] for f in firsts], jnp.int32)[:, None, None]
+    shape = (len(firsts), 256, out_width)
+    r = lax.broadcasted_iota(jnp.int32, shape, 1) - offsets
+    c = lax.broadcasted_iota(jnp.int32, shape, 2)
     hit = (r == c) & (c < HD)
     if copies == 2:
         hit = hit | ((r == c - HD) & (c >= HD) & (c < 2 * HD))
     return jnp.where(hit, 1.0, 0.0).astype(BF)
+
+
+def placer(hpd):
+    r = lax.broadcasted_iota(jnp.int32, (hpd * 128, hpd * HD), 0)
+    c = lax.broadcasted_iota(jnp.int32, (hpd * 128, hpd * HD), 1)
+    hit = (r % 128 < HD) & (c == r // 128 * HD + r % 128)
+    return jnp.where(hit, 1.0, 0.0).astype(BF)
+
+
+def chosen(ref, rows, first, e):
+    lo, hi = window(first, ref.shape[2])
+    return dot(ref[0, rows, lo:hi], e[: hi - lo])
 
 
 def split3(v):
@@ -49,38 +69,39 @@
     return a, b, r - b
 
 
-def aug_query(q_block, h, ids, extra=None):
-    n, w = q_block.shape
-    q = dot(q_block, pick(w, 256, h * HD, 2)) * C2
+def query_tags(n, ids):
     lane = lanes(n, 256)
-    hi = q.astype(BF).astype(F32)
-    out = jnp.where(lane < HD, hi, q - hi)
-    out = jnp.where(lane == 2 * HD + ids, BIG, out)
-    if extra is not None:
-        for t, part in enumerate(split3(extra)):
-            out = jnp.where(lane == 2 * HD + IMAGES + t, part, out)
-    return out.astype(BF)
-
-
-def aug_key(k_block, h, ids):
-    n, w = k_block.shape
-    k = dot(k_block, pick(w, 256, h * HD, 2))
+    return jnp.where(lane == 2 * HD + ids, BIG, 0.0)
+
+
+def key_tags(n, ids):
     lane = lanes(n, 256)
     tag = (lane >= 2 * HD) & (lane < 2 * HD + IMAGES) & (lane != 2 * HD + ids)
-    out = jnp.where(tag, -1.0, k)
-    out = jnp.where((lane >= 2 * HD + IMAGES) & (lane < 2 * HD + IMAGES + 3), 1.0, out)
-    return out.astype(BF)
-
-
-def aug_value(v_block, h, ones):
-    n, w = v_block.shape
-    v = dot(v_block, pick(w, 128, h * HD, 1))
-    lane = lanes(n, 128)
-    return jnp.where((lane >= HD) & (lane < HD + ones), 1.0, v).astype(BF)
+    ones = (lane >= 2 * HD + IMAGES) & (lane < 2 * HD + IMAGES + 3)
+    return jnp.where(tag, -1.0, jnp.where(ones, 1.0, 0.0))
+
+
+def in_lanes(n, width, start, parts):
+    lane = lanes(n, width)
+    out = 0.0
+    for t, part in enumerate(parts):
+        out = jnp.where(lane == start + t, part, out)
+    return out
+
+
+def aug_query(q, tags):
+    q = q * C2
+    hi = q.astype(BF).astype(F32)
+    out = jnp.where(lanes(q.shape[0], 256) < HD, hi, q - hi)
+    return (out + tags).astype(BF)
+
+
+def once(shape, index):
+    return pl.BlockSpec(shape, index, pipeline_mode=pl.Buffered(1))
 
 
 def forward_kernel(
-    hpd, tq, tk, lo_ref, hi_ref, qkv_q, qkv_ref, ids_q, ids_ref, o_ref, lse_ref,
+    hpd, tq, tk, lo_ref, hi_ref, qkv_q, qkv_ref, ids_q, ids_ref, e2_ref, e1_ref, put_ref, o_ref, lse_ref,
     kaug, vaug, s_scr, qa_scr, best_scr, acc_scr,
 ):
     r = pl.program_id(0)
@@ -93,22 +114,24 @@
         def build(j, _):
             rows = pl.ds(pl.multiple_of(j * tk, tk), tk)
             ids = ids_ref[0, rows, :]
-            kb = qkv_ref[0, rows, w : 2 * w]
-            vb = qkv_ref[0, rows, 2 * w : 3 * w]
+            tags = key_tags(tk, ids)
+            ones = in_lanes(tk, 128, HD, [1.0])
             for h in range(hpd):
-                kaug[h, rows, :] = aug_key(kb, h, ids)
-                vaug[h, rows, :] = aug_value(vb, h, 1)
+                k = chosen(qkv_ref, rows, w + h * HD, e2_ref[hpd + h])
+                kaug[h, rows, :] = (k + tags).astype(BF)
+                v = chosen(qkv_ref, rows, 2 * w + h * HD, e1_ref[h])
+                vaug[h, rows, :] = (v + ones).astype(BF)
             return 0
 
         lax.fori_loop(0, length // tk, build, 0)
 
     lo = lo_ref[r, i]
     hi = hi_ref[r, i]
-    qb = qkv_q[0, :, 0:w]
     ids = ids_q[0]
     lane = lanes(tq, 128)
+    tags = query_tags(tq, ids)
     for h in range(hpd):
-        qa_scr[h] = aug_query(qb, h, ids)
+        qa_scr[h] = aug_query(chosen(qkv_q, slice(None), h * HD, e2_ref[h]), tags)
     best_scr[...] = jnp.full((hpd, tq, 128), -3e38, F32)
     acc_scr[...] = jnp.zeros((hpd, tq, 128), F32)
 
@@ -143,16 +166,15 @@
         return 0
 
     lax.fori_loop(lo, hi, second, 0)
-    out = jnp.zeros((tq, w), F32)
+    outs = []
     lse_all = jnp.zeros((tq, 128), F32)
     for h in range(hpd):
         acc = acc_scr[h]
         total = acc[:, HD : HD + 1]
         o = (acc / total).astype(BF)
-        o = jnp.where(lane < HD, o, 0).astype(BF)
-        out = out + dot(o, pick(w, 128, h * HD, 1), NT)
+        outs.append(jnp.where(lane < HD, o, 0).astype(BF))
         lse_all = jnp.where(lane == h, best_scr[h] + jnp.log2(total), lse_all)
-    o_ref[0] = out.astype(BF)
+    o_ref[0] = dot(jnp.concatenate(outs, axis=1), put_ref[...]).astype(BF)
     lse_ref[0] = lse_all
 
 
@@ -171,6 +193,9 @@
                 pl.BlockSpec((1, length, 3 * w), lambda r, i, *_: (r, 0, 0)),
                 pl.BlockSpec((1, tq, 1), lambda r, i, *_: (r, i, 0)),
                 pl.BlockSpec((1, length, 1), lambda r, i, *_: (r, 0, 0)),
+                once((2 * hpd, 256, 256), lambda r, i, *_: (0, 0, 0)),
+                once((hpd, 256, 128), lambda r, i, *_: (0, 0, 0)),
+                once((hpd * 128, w), lambda r, i, *_: (0, 0)),
             ],
             out_specs=[
                 pl.BlockSpec((1, tq, w), lambda r, i, *_: (r, i, 0)),
@@ -191,16 +216,19 @@
         ],
         compiler_params=pltpu.CompilerParams(vmem_limit_bytes=58 << 20),
         cost_estimate=pl.CostEstimate(
-            flops=12 * length * length * rows * w,
+            flops=40 * length * length * rows * w,
             bytes_accessed=8 * rows * length * w,
             transcendentals=rows * length * length * hpd,
         ),
         name="attend_forward",
-    )(lo, hi, qkv, qkv, column, column)
+    )(
+        lo, hi, qkv, qkv, column, column, pickers(hpd, (0, 1), 3 * w, 256, 2),
+        pickers(hpd, (2,), 3 * w, 128, 1), placer(hpd),
+    )
 
 
 def backward_kernel(
-    hpd, tq, tk, lo_ref, hi_ref, qkv_ref, g_ref, o_ref, lse_ref, ids_ref, dp_ref,
+    hpd, tq, tk, lo_ref, hi_ref, qkv_ref, g_ref, o_ref, lse_ref, ids_ref, e2_ref, e1_ref, eg_ref, put_ref, dp_ref,
     qaug, qraw, gaug, dq, kaug, vaug, dka, dva,
 ):
     r = pl.program_id(0)
@@ -212,22 +240,23 @@
         rows = pl.ds(pl.multiple_of(i * step, step), step)
         ids = ids_ref[0, rows, :]
         lane = lanes(step, 128)
-        qb = qkv_ref[0, rows, 0:w]
-        kb = qkv_ref[0, rows, w : 2 * w]
-        vb = qkv_ref[0, rows, 2 * w : 3 * w]
+        q_tags = query_tags(step, ids)
+        k_tags = key_tags(step, ids)
+        ones = in_lanes(step, 128, HD, [1.0] * 3)
         for h in range(hpd):
             lse = lse_ref[0, rows, h : h + 1]
-            qaug[h, rows, :] = aug_query(qb, h, ids, -lse)
-            e = pick(w, 128, h * HD, 1)
-            qraw[h, rows, :] = dot(qb, e).astype(BF)
-            g = dot(g_ref[0, rows, :], e)
-            o = dot(o_ref[0, rows, :], e)
+            tags = q_tags + in_lanes(step, 256, 2 * HD + IMAGES, split3(-lse))
+            q = chosen(qkv_ref, rows, h * HD, e2_ref[h])
+            qaug[h, rows, :] = aug_query(q, tags)
+            qraw[h, rows, :] = jnp.where(lane < HD, q[:, :128], 0.0).astype(BF)
+            g = chosen(g_ref, rows, h * HD, eg_ref[h])
+            o = chosen(o_ref, rows, h * HD, eg_ref[h])
             delta = jnp.sum(g * o, axis=1, keepdims=True)
-            for t, part in enumerate(split3(-delta)):
-                g = jnp.where(lane == HD + t, part, g)
-            gaug[h, rows, :] = g.astype(BF)
-            kaug[h, rows, :] = aug_key(kb, h, ids)
-            vaug[h, rows, :] = aug_value(vb, h, 3)
+            gaug[h, rows, :] = (g + in_lanes(step, 128, HD, split3(-delta))).astype(BF)
+            k = chosen(qkv_ref, rows, w + h * HD, e2_ref[hpd + h])
+            kaug[h, rows, :] = (k + k_tags).astype(BF)
+            v = chosen(qkv_ref, rows, 2 * w + h * HD, e1_ref[h])
+            vaug[h, rows, :] = (v + ones).astype(BF)
             dq[h, rows, :] = jnp.zeros((step, 128), F32)
         return 0
 
@@ -235,13 +264,8 @@
 
     def put(values, n):
         lane = lanes(n, 128)
-        full = None
-        for h in range(hpd):
-            part = dot(
-                jnp.where(lane < HD, values[h], 0).astype(BF), pick(w, 128, h * HD, 1), NT
-            )
-            full = part if full is None else full + part
-        return full.astype(BF)
+        parts = [jnp.where(lane < HD, values[h], 0).astype(BF) for h in range(hpd)]
+        return dot(jnp.concatenate(parts, axis=1), put_ref[...]).astype(BF)
 
     def per_key(j, _):
         krows = pl.ds(pl.multiple_of(j * tk, tk), tk)
@@ -290,7 +314,13 @@
         grid_spec=pltpu.PrefetchScalarGridSpec(
             num_scalar_prefetch=2,
             grid=(rows,),
-            in_specs=[spec(3 * w), spec(w), spec(w), spec(128), spec(1)],
+            in_specs=[
+                spec(3 * w), spec(w), spec(w), spec(128), spec(1),
+                once((2 * hpd, 256, 256), lambda r, *_: (0, 0, 0)),
+                once((hpd, 256, 128), lambda r, *_: (0, 0, 0)),
+                once((hpd, 256, 128), lambda r, *_: (0, 0, 0)),
+                once((hpd * 128, w), lambda r, *_: (0, 0)),
+            ],
             out_specs=spec(3 * w),
             scratch_shapes=[
                 pltpu.VMEM((hpd, length, 256), BF),
@@ -306,12 +336,15 @@
         out_shape=jax.ShapeDtypeStruct((rows, length, 3 * w), BF),
         compiler_params=pltpu.CompilerParams(vmem_limit_bytes=58 << 20),
         cost_estimate=pl.CostEstimate(
-            flops=30 * length * length * rows * w,
+            flops=60 * length * length * rows * w,
             bytes_accessed=18 * rows * length * w,
             transcendentals=rows * length * length * hpd,
         ),
         name="attend_backward",
-    )(lo, hi, qkv, g, o, lse, ids[..., None])
+    )(
+        lo, hi, qkv, g, o, lse, ids[..., None], pickers(hpd, (0, 1), 3 * w, 256, 2),
+        pickers(hpd, (2,), 3 * w, 128, 1), pickers(hpd, (0,), w, 128, 1), placer(hpd),
+    )
 
 
 def block_ranges(ids, mine, theirs):
@@ -334,10 +367,6 @@
     return pl.CostEstimate(
         flops=int(2 * units * count * D * D), bytes_accessed=int(moved), transcendentals=0
     )
-
-
-def once(shape, index):
-    return pl.BlockSpec(shape, index, pipeline_mode=pl.Buffered(1))
 
 
 def row_tile(count):
@@ -388,49 +417,59 @@
     )(cond, x, ada, bias)
 
 
+def gates_kernel(act_ref, ada_ref, bias_ref, out_ref):
+    out_ref[0] = (dot(act_ref[...], ada_ref[0]) + bias_ref[0]).astype(BF)
+
+
+def feed_gates(act, ada, bias):
+    count = act.shape[0]
+    return pl.pallas_call(
+        gates_kernel,
+        grid=(4,),
+        in_specs=[once((count, D), lambda i: (0, 0)), pl.BlockSpec((1, D, D), lambda i: (i, 0, 0)),
+                  pl.BlockSpec((1, 1, D), lambda i: (i, 0, 0))],
+        out_specs=pl.BlockSpec((1, count, D), lambda i: (i, 0, 0)),
+        out_shape=jax.ShapeDtypeStruct((4, count, D), BF),
+        compiler_params=params(),
+        cost_estimate=cost(4, count, 10 * count * D + 8 * D * D),
+        name="feed_gates",
+    )(act, ada, bias)
+
+
 def before_feed_kernel(
-    act_ref, attn_ref, x_ref, cot_ref, ada_ref, out_ref, ada_bias, out_bias,
-    gates_ref, mix_ref, middle_ref, input_ref, grad_ref,
+    attn_ref, x_ref, cot_ref, gates_ref, out_ref, out_bias, mix_ref, middle_ref, input_ref, grad_ref
 ):
-    act = act_ref[...]
-    gate_mix = dot(act, ada_ref[0]) + ada_bias[0]
-    gates_ref[0] = gate_mix.astype(BF)
     branch_mix = dot(attn_ref[...], out_ref[...]) + out_bias[...]
     mix_ref[...] = branch_mix.astype(BF)
-    middle = x_ref[...].astype(F32) + gate_mix * branch_mix
+    middle = x_ref[...].astype(F32) + gates_ref[0].astype(F32) * branch_mix
     middle_ref[...] = middle
     normed, _ = norm_of(middle)
-    scale_feed = dot(act, ada_ref[2]) + ada_bias[2]
-    gates_ref[1] = scale_feed.astype(BF)
-    shift_feed = dot(act, ada_ref[1]) + ada_bias[1]
-    input_ref[...] = (normed * (1.0 + scale_feed) + shift_feed).astype(BF)
-    gate_feed = dot(act, ada_ref[3]) + ada_bias[3]
-    gates_ref[2] = gate_feed.astype(BF)
-    grad_ref[...] = (cot_ref[...].astype(F32) * gate_feed).astype(BF)
-
-
-def before_feed(act, attn_out, x, cot, ada, out_mat, ada_bias, out_bias):
-    count = act.shape[0]
+    input_ref[...] = (
+        normed * (1.0 + gates_ref[2].astype(F32)) + gates_ref[1].astype(F32)
+    ).astype(BF)
+    grad_ref[...] = (cot_ref[...].astype(F32) * gates_ref[3].astype(F32)).astype(BF)
+
+
+def before_feed(attn_out, x, cot, gates, out_mat, out_bias):
+    count = x.shape[0]
     tm = row_tile(count)
     rows = pl.BlockSpec((tm, D), lambda i: (i, 0))
     return pl.pallas_call(
         before_feed_kernel,
         grid=(count // tm,),
-        in_specs=[rows, rows, rows, rows, once((4, D, D), lambda i: (0, 0, 0)),
-                  once((D, D), lambda i: (0, 0)), once((4, 1, D), lambda i: (0, 0, 0)),
-                  once((1, D), lambda i: (0, 0))],
-        out_specs=[pl.BlockSpec((3, tm, D), lambda i: (0, i, 0)), rows, rows, rows, rows],
+        in_specs=[rows, rows, rows, pl.BlockSpec((4, tm, D), lambda i: (0, i, 0)),
+                  once((D, D), lambda i: (0, 0)), once((1, D), lambda i: (0, 0))],
+        out_specs=[rows] * 4,
         out_shape=[
-            jax.ShapeDtypeStruct((3, count, D), BF),
             jax.ShapeDtypeStruct((count, D), BF),
             jax.ShapeDtypeStruct((count, D), F32),
             jax.ShapeDtypeStruct((count, D), BF),
             jax.ShapeDtypeStruct((count, D), BF),
         ],
         compiler_params=params(),
-        cost_estimate=cost(5, count, 24 * count * D + 10 * D * D),
+        cost_estimate=cost(1, count, 24 * count * D),
         name="before_feed",
-    )(act, attn_out, x, cot, ada, out_mat, ada_bias, out_bias)
+    )(attn_out, x, cot, gates, out_mat, out_bias)
 
 
 GELU_A = math.sqrt(2.0 / math.pi)
@@ -522,81 +561,198 @@
 
 
 def after_feed_kernel(
-    branch_ref, shift_ref, middle_ref, gates_ref, mix_ref, cot_ref, out_ref, bias_ref,
+    first, branch_ref, shift_ref, middle_ref, gates_ref, mix_ref, cot_ref, out_ref, bias_ref,
     block_ref, late_ref, mix_grad_ref, attn_grad_ref, middle_grad_ref,
 ):
     cot = cot_ref[...].astype(F32)
     middle = middle_ref[...]
     branch = branch_ref[...] + bias_ref[...]
-    block_ref[...] = (middle + gates_ref[2].astype(F32) * branch).astype(BF)
+    block_ref[...] = (middle + gates_ref[3].astype(F32) * branch).astype(BF)
     late_ref[3] = (cot * branch).astype(BF)
     shift = shift_ref[...]
     late_ref[1] = shift.astype(BF)
     normed, inverse = norm_of(middle)
     late_ref[2] = (shift * normed).astype(BF)
-    middle_grad = cot + norm_back(shift * (1.0 + gates_ref[1].astype(F32)), normed, inverse)
+    middle_grad = cot + norm_back(shift * (1.0 + gates_ref[2].astype(F32)), normed, inverse)
     middle_grad_ref[...] = middle_grad
     late_ref[0] = (middle_grad * mix_ref[...].astype(F32)).astype(BF)
     mix_grad = (middle_grad * gates_ref[0].astype(F32)).astype(BF)
     mix_grad_ref[...] = mix_grad
-    attn_grad_ref[...] = dot(mix_grad, out_ref[...], NT).astype(BF)
-
-
-def after_feed(branch, shift, middle, gates, mix, cot, out_mat, down_bias):
+    attn_grad = dot(mix_grad, out_ref[...], NT).astype(BF)
+    w = attn_grad_ref.shape[3]
+    for s in range(attn_grad_ref.shape[0]):
+        attn_grad_ref[s, 0] = attn_grad[:, s * w : (s + 1) * w]
+
+
+def after_feed(first, seqs, own, branch, shift, middle, gates, mix, cot, out_mat, down_bias):
     count = branch.shape[0]
-    tm = row_tile(count)
-    rows = pl.BlockSpec((tm, D), lambda i: (i, 0))
+    tm = 288 if own % 288 == 0 else own
+    steps = own // tm
+    rows = pl.BlockSpec((tm, D), lambda i, f: (i, 0))
     return pl.pallas_call(
         after_feed_kernel,
-        grid=(count // tm,),
-        in_specs=[rows, rows, rows, pl.BlockSpec((3, tm, D), lambda i: (0, i, 0)), rows, rows,
-                  once((D, D), lambda i: (0, 0)), once((1, D), lambda i: (0, 0))],
-        out_specs=[rows, pl.BlockSpec((4, tm, D), lambda i: (0, i, 0)), rows, rows, rows],
+        grid_spec=pltpu.PrefetchScalarGridSpec(
+            num_scalar_prefetch=1,
+            grid=(count // tm,),
+            in_specs=[rows, rows, rows, pl.BlockSpec((4, tm, D), lambda i, f: (0, i, 0)), rows, rows,
+                      once((D, D), lambda i, f: (0, 0)), once((1, D), lambda i, f: (0, 0))],
+            out_specs=[
+                rows, pl.BlockSpec((4, tm, D), lambda i, f: (0, i, 0)), rows,
+                pl.BlockSpec(
+                    (seqs, 1, tm, D // seqs),
+                    lambda i, f: (0, (i // steps + f[0]) % 2, i % steps, 0),
+                ),
+                rows,
+            ],
+        ),
         out_shape=[
             jax.ShapeDtypeStruct((count, D), BF),
             jax.ShapeDtypeStruct((4, count, D), BF),
             jax.ShapeDtypeStruct((count, D), BF),
-            jax.ShapeDtypeStruct((count, D), BF),
+            jax.ShapeDtypeStruct((seqs, count // own, own, D // seqs), BF),
             jax.ShapeDtypeStruct((count, D), F32),
         ],
         compiler_params=params(),
         cost_estimate=cost(1, count, 44 * count * D),
         name="after_feed",
-    )(branch, shift, middle, gates, mix, cot, out_mat, down_bias)
-
-
-def token_products_kernel(order, act_ref, grad_ref, out_ref, sum_ref):
+    )(first, branch, shift, middle, gates, mix, cot, out_mat, down_bias)
+
+
+def late_products_kernel(turns, order, act_ref, grad_ref, give_ref, keep_ref, sum_ref):
     grad = grad_ref[0]
-    out_ref[0] = dot(act_ref[...], grad, TN).astype(BF)
+    out = dot(act_ref[...], grad, TN).astype(BF)
+    t = pl.program_id(0)
+
+    @pl.when(t < turns)
+    def _():
+        give_ref[0] = out
+
+    @pl.when(t >= turns)
+    def _():
+        keep_ref[0] = out
+
     sum_ref[0] = jnp.sum(grad.astype(F32), axis=0, keepdims=True)
 
 
-def token_products(order, act, grads):
+def late_products(order, act, grads):
     parts, count, _ = grads.shape
+    turns = parts // 2
     return pl.pallas_call(
-        token_products_kernel,
+        partial(late_products_kernel, turns),
         grid_spec=pltpu.PrefetchScalarGridSpec(
             num_scalar_prefetch=1,
             grid=(parts,),
             in_specs=[once((count, D), lambda t, o: (0, 0)),
                       pl.BlockSpec((1, count, D), lambda t, o: (o[t], 0, 0))],
-            out_specs=[pl.BlockSpec((1, D, D), lambda t, o: (t, 0, 0)),
+            out_specs=[pl.BlockSpec((1, D, D), lambda t, o: (jnp.minimum(t, turns - 1), 0, 0)),
+                       pl.BlockSpec((1, D, D), lambda t, o: (jnp.maximum(t - turns, 0), 0, 0)),
                        pl.BlockSpec((1, 1, D), lambda t, o: (o[t], 0, 0))],
         ),
         out_shape=[
-            jax.ShapeDtypeStruct((parts, D, D), BF),
+            jax.ShapeDtypeStruct((turns, D, D), BF),
+            jax.ShapeDtypeStruct((turns, D, D), BF),
             jax.ShapeDtypeStruct((parts, 1, D), F32),
         ],
         compiler_params=params(),
         cost_estimate=cost(parts, count, 2 * (parts + 1) * count * D + 2 * parts * D * D),
-        name="token_products",
+        name="late_products",
     )(order, act, grads)
+
+
+def early_products_kernel(act_ref, grad_ref, out_ref, sum_ref):
+    grad = grad_ref[0]
+    out = dot(act_ref[...], grad, TN).astype(BF)
+    out_ref[0] = out[:, : D // 2]
+    out_ref[1] = out[:, D // 2 :]
+    sum_ref[0] = jnp.sum(grad.astype(F32), axis=0, keepdims=True)
+
+
+def early_products(act, grads):
+    parts, count, _ = grads.shape
+    return pl.pallas_call(
+        early_products_kernel,
+        grid=(parts,),
+        in_specs=[once((count, D), lambda t: (0, 0)),
+                  pl.BlockSpec((1, count, D), lambda t: (t, 0, 0))],
+        out_specs=[pl.BlockSpec((2, D, D // 2), lambda t: (t, 0, 0)),
+                   pl.BlockSpec((1, 1, D), lambda t: (t, 0, 0))],
+        out_shape=[
+            jax.ShapeDtypeStruct((2 * parts, D, D // 2), BF),
+            jax.ShapeDtypeStruct((parts, 1, D), F32),
+        ],
+        compiler_params=params(),
+        cost_estimate=cost(parts, count, 2 * (parts + 1) * count * D + 2 * parts * D * D),
+        name="early_products",
+    )(act, grads)
+
+
+def head_products_kernel(blocks, places, *refs):
+    own = refs[0].shape[0]
+    grad_ref, out_ref = refs[blocks], refs[-1]
+    for t in range(blocks):
+        rows = pl.ds(pl.multiple_of(places[t] * own, own), own)
+        part = dot(refs[t][...], grad_ref[rows, :], TN)
+        if t == 0:
+            out_ref[...] = part if len(refs) == blocks + 2 else part + refs[blocks + 1][...]
+        else:
+            out_ref[...] += part
+
+
+def head_products(places, blocks, grad, *start):
+    n = grad.shape[1]
+    vmem = pl.BlockSpec(memory_space=pltpu.VMEM)
+    return pl.pallas_call(
+        partial(head_products_kernel, len(blocks)),
+        grid_spec=pltpu.PrefetchScalarGridSpec(
+            num_scalar_prefetch=1,
+            grid=(),
+            in_specs=[vmem] * (len(blocks) + 1 + len(start)),
+            out_specs=vmem,
+        ),
+        out_shape=jax.ShapeDtypeStruct((D, n), F32),
+        compiler_params=params(),
+        cost_estimate=pl.CostEstimate(
+            flops=2 * grad.shape[0] * D * n, bytes_accessed=2 * grad.size + 8 * D * n, transcendentals=0
+        ),
+        name="head_products",
+    )(places, *blocks, grad, *start)
+
+
+def after_mix_kernel(grad_ref, x_ref, scale_ref, middle_grad_ref, early_ref, tokens_grad_ref):
+    grad = grad_ref[...].astype(F32)
+    normed, inverse = norm_of(x_ref[...].astype(F32))
+    early_ref[0] = grad.astype(BF)
+    early_ref[1] = (grad * normed).astype(BF)
+    back = norm_back(grad * (1.0 + scale_ref[...].astype(F32)), normed, inverse)
+    tokens_grad_ref[...] = middle_grad_ref[...] + back
+
+
+def after_mix(grad, x, scale, middle_grad):
+    count = x.shape[0]
+    tm = row_tile(count)
+    rows = pl.BlockSpec((tm, D), lambda i: (i, 0))
+    return pl.pallas_call(
+        after_mix_kernel,
+        grid=(count // tm,),
+        in_specs=[rows] * 4,
+        out_specs=[pl.BlockSpec((2, tm, D), lambda i: (0, i, 0)), rows],
+        out_shape=[
+            jax.ShapeDtypeStruct((2, count, D), BF),
+            jax.ShapeDtypeStruct((count, D), F32),
+        ],
+        compiler_params=params(),
+        cost_estimate=cost(0, count, 18 * count * D),
+        name="after_mix",
+    )(grad, x, scale, middle_grad)
 
 
 def to_condition_kernel(parts, last, grads_ref, ada_ref, *refs):
     out_ref, total = refs[-2:]
     t = pl.program_id(1)
-    part = dot(grads_ref[0], ada_ref[0], NT)
+    n = ada_ref.shape[2]
+    part = sum(
+        dot(grads_ref[0][:, k * n : (k + 1) * n], ada_ref[k], NT) for k in range(ada_ref.shape[0])
+    )
 
     @pl.when(t == 0)
     def _():
@@ -624,7 +780,8 @@
         partial(to_condition_kernel, parts, len(rest) > 0),
         grid=(count // tm, parts),
         in_specs=[pl.BlockSpec((1, tm, D), lambda m, t: (t, m, 0)),
-                  pl.BlockSpec((1, D, D), lambda m, t: (t, 0, 0))] + [rows] * len(rest),
+                  pl.BlockSpec((ada.shape[0] // parts, D, ada.shape[2]), lambda m, t: (t, 0, 0))]
+        + [rows] * len(rest),
         out_specs=rows,
         scratch_shapes=[pltpu.VMEM((tm, D), F32)],
         out_shape=jax.ShapeDtypeStruct((count, D), F32),
@@ -698,6 +855,16 @@
         whole = lax.dynamic_update_slice(whole, part[:, None], (0, self.b) + rest)
         whole = lax.dynamic_update_slice(whole, other[:, None], (0, 1 - self.b) + rest)
         return whole.reshape((self.packs,) + part.shape[1:])
+
+    def list_seq(self, value):
+        if self.seqs != 4:
+            whole = self.gather_seq(value)
+            return [whole[s] for s in range(self.seqs)]
+        far = self.side(value, 1)
+        near = self.two(value, self.core(value))
+        away = self.two(far, self.core(far))
+        pairs = [jnp.where(self.y == y, near[c], away[c]) for y in range(2) for c in range(2)]
+        return pairs
 
     def gather_pack(self, value):
         part = self.ring_join(self.ring_blocks(value))
@@ -770,12 +937,18 @@
     half = D // 2
     ids = at.gather_seq(image_ids).transpose(1, 0, 2).reshape(rows, length)
     first = jnp.where(ids[0, length - 1] == 0, 0, 1)
-    row_order = [first, 1 - first]
-
     def in_order(values):
         return jnp.where(
             first == 0, jnp.concatenate(values, axis=0), jnp.concatenate(values[::-1], axis=0)
         )
+
+    cut, nd = attn_weight.shape[1], down_weight.shape[1]
+    skip = cut + out_weight.shape[1]
+    rq = rf // seqs
+
+    def side_by_side():
+        downs = [down_weight[s * rq : (s + 1) * rq] for s in range(seqs)] if rq == r else []
+        return jnp.concatenate([attn_weight, out_weight] + downs, axis=1)
 
     if seqs == 4:
         left, right = ada_weight[:, :D], ada_weight[:, D:]
@@ -795,48 +968,63 @@
             at.seq == 0, core_got,
             jnp.where(at.seq == 1, far_got, jnp.where(at.seq == 2, merged, ada_weight[:, half:])),
         )
-        both = at.gather_seq(jnp.concatenate([attn_weight, out_weight], axis=1))
+        both = at.list_seq(side_by_side())
     else:
-        both = lax.all_gather(
-            jnp.concatenate([attn_weight, out_weight, ada_weight], axis=1), "seq", axis=0
-        )
-        ada_rows = both[:, :, attn_weight.shape[1] + out_weight.shape[1] :]
-        ada_rows = ada_rows.transpose(1, 0, 2).reshape(r, 6 * D)
+        both = at.list_seq(side_by_side())
+        ada_rows = jnp.concatenate(at.list_seq(ada_weight), axis=1)
         shard1 = lax.dynamic_slice_in_dim(ada_rows, at.seq * (n2 // 2), n2 // 2, 1)
         shard2 = lax.dynamic_slice_in_dim(ada_rows, 2 * D + at.seq * n2, n2, 1)
-    cut = attn_weight.shape[1]
-    attn_rows = both[:, :, :cut].transpose(1, 0, 2).reshape(r, 3 * D)
-    out_rows = both[:, :, cut : cut + out_weight.shape[1]].transpose(1, 0, 2).reshape(r, D)
+    attn_rows = jnp.concatenate([block[:, :cut] for block in both], axis=1)
+    out_rows = jnp.concatenate([block[:, cut:skip] for block in both], axis=1)
     every = [range(seqs)]
     ada1 = at.gather_by(shard1, every)
     ada1 = ada1.reshape(4, seqs // 4, D, n2 // 2).transpose(0, 2, 1, 3).reshape(4, D, half)
     mine = lax.dynamic_slice_in_dim(attn_rows.reshape(r, 3, seqs, w), at.seq, 1, 2)
-    attn_blocks = at.ring_blocks(mine.reshape(r, 3 * w))
+    wide = 640
+    out_half = jnp.where(at.c == 0, out_rows[:, :wide], out_rows[:, D - wide :])
+    packed = jnp.concatenate([out_half, mine.reshape(r, 3 * w)], axis=1)
     lined = jnp.pad(biases, (0, padded - bias_len)).reshape(-1, 128)
     offsets = at.gather_pack(at.gather_seq(lined)).reshape(packs, seqs, padded)
     offsets = offsets[:, :, :bias_len].reshape(-1)
 
+    ring_blocks = at.ring_blocks(packed)
+    shard2, offsets, ids, first, ring_blocks = lax.optimization_barrier(
+        (shard2, offsets, ids, first, ring_blocks)
+    )
     ada2 = at.gather_by(shard2, every)
     ada2 = ada2.reshape(4, seqs // 4, D, n2).transpose(0, 2, 1, 3).reshape(4, D, D)
-    rq = rf // seqs
-    down_rows = lax.all_to_all(down_weight, "seq", 0, 1, tiled=True)
+    if rq == r:
+        down_rows = jnp.concatenate(
+            [
+                sum(
+                    jnp.where(at.seq == s, block[:, skip + s * nd : skip + (s + 1) * nd], 0)
+                    for s in range(seqs)
+                )
+                for block in both
+            ],
+            axis=1,
+        ).astype(BF)
+    else:
+        down_parts = lax.all_to_all(down_weight.reshape(seqs, rq, nd), "seq", 0, 0, tiled=True)
+        down_rows = jnp.concatenate([down_parts[s] for s in range(seqs)], axis=1)
     down_rows, up_weight, ada1 = lax.optimization_barrier((down_rows, up_weight, ada1))
     down_mat = lax.all_gather(down_rows, ("pack", "seq"), axis=0, tiled=True)
     down_mats = down_mat.reshape(seqs, nf, D)
     up_mats = at.gather_by(up_weight, every).reshape(seqs, D, nf)
 
+    x = tokens.reshape(count, D).astype(F32)
+    ring_part = at.ring_join(ring_blocks)
+    cond_act, attn_input, scale_mix = mix_input(
+        condition.reshape(count, D), tokens.reshape(count, D), ada1,
+        offsets[: 2 * D].astype(F32).reshape(2, 1, D),
+    )
+    attn_input = attn_input.reshape(rows, own, D)
     query_offset = offsets[6 * D : 7 * D]
     value_offset = offsets[7 * D : 8 * D]
     out_offset = offsets[8 * D : 9 * D]
     up_offset = offsets[9 * D : 9 * D + FF]
     down_offset = offsets[9 * D + FF :]
 
-    x = tokens.reshape(count, D).astype(F32)
-    cond_act, attn_input, scale_mix = mix_input(
-        condition.reshape(count, D), tokens.reshape(count, D), ada1,
-        offsets[: 2 * D].astype(F32).reshape(2, 1, D),
-    )
-    attn_input = attn_input.reshape(rows, own, D)
     head_offset = jnp.concatenate(
         [
             lax.dynamic_slice_in_dim(query_offset, at.seq * w, w),
@@ -845,13 +1033,9 @@
         ]
     )
 
-    wide = 640
-    out_half = jnp.where(at.c == 0, out_rows[:, :wide], out_rows[:, D - wide :])
-    attn_input, attn_blocks, out_half = lax.optimization_barrier((attn_input, attn_blocks, out_half))
+    row_order = [first, 1 - first]
     starts = [lax.dynamic_index_in_dim(attn_input, row, 0, False) for row in row_order]
-    attn_part = at.ring_join(attn_blocks)
-    attn_mat = at.cross_join(attn_part, at.cross(attn_part)).reshape(D, 3 * w)
-    out_blocks = at.ring_blocks(out_half)
+    ring_other = at.cross(ring_part)
 
     inputs, qkvs, heads, lses, outs = [], [], [], [], []
     id_rows = [lax.dynamic_slice_in_dim(ids, row, 1, 0) for row in row_order]
@@ -860,6 +1044,8 @@
         blocks = []
         for k in range(at.sides):
             block = start if k == 0 else at.side(start, k)
+            if k and row == 0:
+                ring_other, block = after(ring_other, block)
             if k and row + 1 < rows:
                 starts[row + 1], block = after(starts[row + 1], block)
             if k and row:
@@ -867,89 +1053,89 @@
             side = (at.y - k + at.sides) % at.sides
             blocks += [(side * 2 + at.c, block), (side * 2 + 1 - at.c, at.core(block))]
         inputs.append(blocks)
+        if row == 0:
+            packed = at.cross_join(ring_part, ring_other).reshape(D, wide + 3 * w)
+            out_own, attn_mat = packed[:, :wide], packed[:, wide:]
         qkv = jnp.zeros((seqs, own, 3 * w), BF)
         for place, block in blocks:
             part = (dot(block, attn_mat) + head_offset).astype(BF)
             qkv = lax.dynamic_update_slice(qkv, part[None], (place, 0, 0))
         qkvs.append(qkv.reshape(1, length, 3 * w))
-        if row == 0:
-            qkvs[0], out_blocks = after(qkvs[0], out_blocks)
-            out_part = at.ring_join(out_blocks)
-            out_other = at.cross(out_part)
-        if row == 1:
-            qkvs[1], out_other = after(qkvs[1], out_other)
-            out_own = at.cross_join(out_part, out_other).reshape(D, wide)
-            out_far = at.core(out_own)
-        head, lse = attend_forward(qkvs[row], id_rows[row], hpd, 256, 768)
+        head, lse = attend_forward(qkvs[row], id_rows[row], hpd, 256 if row else 768, 768)
         heads.append(head)
         lses.append(lse)
     for row in range(rows):
         outs.append(lax.all_to_all(heads[row][0], "seq", 0, 1, tiled=True))
-    out_left, out_right = at.two(out_own, out_far)
+    out_left, out_right = at.two(out_own, at.core(out_own))
     out_mat = jnp.concatenate([out_left, out_right[:, 2 * wide - D :]], axis=1)
 
     def line(values, parts):
         return values.astype(F32).reshape(parts + (1, -1))
 
+    gate_act, heads[-1] = after(cond_act, heads[-1])
+    gates = feed_gates(gate_act, ada2, line(offsets[2 * D : 6 * D], (4,)))
+    gates, outs[-1] = after(gates, outs[-1])
     attn_out = in_order(outs)
-    gates, branch_mix, middle, feed_input, feed_out_grad = before_feed(
-        cond_act, attn_out, tokens.reshape(count, D), cotangent.reshape(count, D), ada2, out_mat,
-        line(offsets[2 * D : 6 * D], (4,)), line(out_offset, ()),
+    branch_mix, middle, feed_input, feed_out_grad = before_feed(
+        attn_out, tokens.reshape(count, D), cotangent.reshape(count, D), gates, out_mat,
+        line(out_offset, ()),
     )
     branch_feed, shift_sum, up_whole, down_whole, up_sums = feed(
         feed_input, feed_out_grad, up_mats, down_mats, line(up_offset, (seqs,))
     )
     block_out, late, mix_out_grad, attn_out_grad, middle_grad = after_feed(
-        branch_feed, shift_sum, middle, gates, branch_mix, cotangent.reshape(count, D), out_mat,
+        first.astype(jnp.int32).reshape(1), seqs, own, branch_feed, shift_sum, middle, gates, branch_mix, cotangent.reshape(count, D), out_mat,
         line(down_offset, ()),
     )
 
-    attn_out_grad = attn_out_grad.reshape(rows, own, D)
     down_part = lax.psum_scatter(
         down_whole.reshape(FF, D), ("pack", "seq"), scatter_dimension=0, tiled=True
     )
     up_grad = at.scatter_all(up_whole.reshape(seqs, packs, r, nf)).astype(F32)
-    grad_heads = [
-        lax.all_to_all(
-            lax.dynamic_index_in_dim(attn_out_grad, row, 0, False), "seq", 1, 0, tiled=True
-        )
-        for row in row_order
-    ]
+    both_heads = lax.all_to_all(attn_out_grad, "seq", 0, 0, tiled=True)
+    grad_heads = [both_heads[:, row].reshape(length, w) for row in range(rows)]
     out_whole = dot(attn_out, mix_out_grad, TN).astype(BF).reshape(packs, 2, r // 2, D)
     if seqs == 4:
         turn = jnp.stack([y * 2 + core for core in (1 - at.c, at.c) for y in range(2)])
-        late_whole, late_sums = token_products(turn.astype(jnp.int32), cond_act, late)
-        late_whole = late_whole.reshape(2, 2, packs, r, D)
-        late_core = add(late_whole[1], at.core(late_whole[0]))
+        late_give, late_keep, late_sums = late_products(turn.astype(jnp.int32), cond_act, late)
+        late_core = add(late_keep, at.core(late_give)).reshape(2, packs, r, D)
+        late_pair = at.reduce_cross(late_core)
         out_core = at.reduce_core(out_whole)
-        grad_heads[0], late_core, out_core = lax.optimization_barrier(
-            (grad_heads[0], late_core, out_core)
-        )
-        late_pair = at.reduce_cross(late_core)
     else:
-        late_whole, late_sums = token_products(jnp.arange(4, dtype=jnp.int32), cond_act, late)
+        late_give, late_keep, late_sums = late_products(jnp.arange(4, dtype=jnp.int32), cond_act, late)
+        late_whole = jnp.concatenate([late_give, late_keep])
         late_whole = late_whole.reshape(4, packs, r, seqs // 4, n2).transpose(0, 3, 1, 2, 4)
         ada_late = at.scatter_all(late_whole.reshape(seqs, packs, r, n2))
         out_core = at.reduce_core(out_whole)
+    grad_heads[0], out_core = after(grad_heads[0], out_core)
     out_pair = at.reduce_cross(out_core[None])
-
     input_grads, flat_grads = [], []
     for row in range(rows):
-        if row == 1 and seqs == 4:
-            grad_heads[1], late_pair = after(grad_heads[1], late_pair)
-            late_ring = at.reduce_ring(late_pair).astype(BF)
         if row == 1:
-            grad_heads[1], out_pair = after(grad_heads[1], out_pair)
-            out_ring = at.reduce_ring(out_pair)[0].astype(BF)
+            grad_heads[1], flat_grads[0] = after(grad_heads[1], flat_grads[0])
         grad = attend_backward(
-            qkvs[row], grad_heads[row][None], heads[row], lses[row], id_rows[row], hpd, 256, 768
+            qkvs[row], grad_heads[row][None], heads[row], lses[row], id_rows[row], hpd, 256 if row else 768, 768
         )[0]
-        flat_grads.append(grad)
+        if row == 0:
+            grad, down_part = after(grad, down_part)
+        else:
+            grad, input_grads[0] = after(grad, input_grads[0])
         part = dot(grad, attn_mat, NT).astype(BF).reshape(at.sides, 2, own, D)
         input_grads.append(at.reduce_side(at.reduce_core(part)))
+        if row == 1:
+            grad, out_pair = after(grad, out_pair)
+            out_ring = at.reduce_ring(out_pair)[0].astype(BF)
+            if seqs == 4:
+                grad, late_pair = after(grad, late_pair)
+                late_ring = at.reduce_ring(late_pair).astype(BF)
+        flat_grads.append(grad)
+        places = jnp.stack([place for place, _ in inputs[row]]).astype(jnp.int32)
+        attn_whole = head_products(
+            places, [block for _, block in inputs[row]], grad, *([attn_whole] if row else [])
+        )
     late, flat_grads = after(late, flat_grads)
     cond_part = to_condition(late, ada2)
-    input_grad = in_order(input_grads)
+    input_grad, up_grad = after(in_order(input_grads), up_grad)
     out_side = at.reduce_side(out_ring.reshape(r // 2, at.sides, -1).transpose(1, 0, 2))
     out_side = out_side.reshape(r // 2, 2, -1).transpose(1, 0, 2)
     out_far = at.core(lax.dynamic_index_in_dim(out_side, 1 - at.c, 0, False))
@@ -957,54 +1143,51 @@
     out_grad = jnp.concatenate(at.two(out_near, out_far)).astype(F32)
     if seqs == 4:
         ada_late = at.reduce_side(late_ring)
-    attn_whole = 0.0
-    for row in range(rows):
-        for place, block in inputs[row]:
-            piece = lax.dynamic_slice_in_dim(flat_grads[row], place * own, own, 0)
-            attn_whole = attn_whole + dot(block, piece, TN)
-    attn_part = at.reduce_pack(attn_whole.astype(BF).reshape(packs, r, 3 * w)).astype(BF)
-    norm_x, inverse_x = norm_of(x)
-    scale_mix_grad = (input_grad * norm_x).astype(BF)
-    tokens_grad = middle_grad + norm_back(input_grad * (1.0 + scale_mix.astype(F32)), norm_x, inverse_x)
-    shift_mix_grad = input_grad.astype(BF)
-    early = jnp.stack([shift_mix_grad, scale_mix_grad])
-    early_whole, early_sums = token_products(
-        jnp.stack([1 - at.c, at.c]).astype(jnp.int32), cond_act, early
-    )
-    early_whole = early_whole.reshape(2, packs, r, D)
-    early_core = add(early_whole[1], at.core(early_whole[0]))
-    early_pack = at.reduce_pack(early_core).astype(BF)
-    early_side = add(early_pack, *[at.side(early_pack, k) for k in range(1, at.sides)])
-    ada1_parts = ada1.reshape(2, 2, D, half).transpose(0, 2, 1, 3).reshape(2, D, D)
-    condition_grad = to_condition(early, ada1_parts, cond_part, condition.reshape(count, D))
+    attn_pair = at.reduce_cross(attn_whole.astype(BF).reshape(1, packs, r, 3 * w))
+    early, tokens_grad = after_mix(input_grad, tokens.reshape(count, D), scale_mix, middle_grad)
+    early_whole, early_sums = early_products(cond_act, early)
+    early_whole, attn_pair = after(early_whole, attn_pair)
+    attn_part = at.reduce_ring(attn_pair)[0].astype(BF)
+    early_whole = early_whole.reshape(4, packs, r, seqs // 4, n2 // 2).transpose(0, 3, 1, 2, 4)
+    early_got = at.scatter_all(early_whole.reshape(seqs, packs, r, n2 // 2))
+    condition_grad = to_condition(early, ada1, cond_part, condition.reshape(count, D))
+    early_got, condition_grad = after(early_got, condition_grad)
 
     def own_columns(whole):
         n = whole.shape[1] // seqs
         return lax.dynamic_slice_in_dim(whole, at.seq * n, n, 1).astype(F32)
 
     if seqs == 4:
-        early_half = lax.ppermute(early_side[:, :half], "seq", [(1, 0)])
+        early_core = lax.ppermute(early_got, "seq", [(1, 0)])
+        early_half = lax.ppermute(early_got, "seq", [(2, 0), (3, 1)])
         swapped = lax.ppermute(ada_late, "seq", [(0, 1), (1, 2)])
         late_half = lax.ppermute(ada_late[:, half:], "seq", [(2, 3)])
         whole_part = jnp.where(
-            at.seq == 0, early_side, jnp.where(at.seq == 3, ada_late, swapped)
+            at.seq == 0, jnp.concatenate([early_got, early_core], axis=1),
+            jnp.where(at.seq == 3, ada_late, swapped)
         )
-        half_part = jnp.where(
-            at.seq == 1, early_side[:, half:],
-            jnp.where(at.seq == 2, ada_late[:, :half], early_half + late_half),
-        )
+        half_part = jnp.where(at.seq == 2, ada_late[:, :half], early_half + late_half)
         ada_grad = jnp.where(
             at.c == 0,
             jnp.concatenate([whole_part, half_part], axis=1),
             jnp.concatenate([half_part, whole_part], axis=1),
         ).astype(F32)
     else:
-        early_all = jnp.concatenate(at.two(early_side, at.core(early_side)), axis=1)
+        early_all = jnp.concatenate(at.list_seq(early_got), axis=1)
         late_all = at.gather_seq(ada_late).transpose(1, 0, 2).reshape(r, 4 * D)
         ada_grad = own_columns(jnp.concatenate([early_all, late_all], axis=1))
     attn_all = at.gather_seq(attn_part).reshape(seqs, r, 3, w).transpose(1, 2, 0, 3).reshape(r, 3 * D)
 
-    down_grad = lax.all_to_all(down_part, "seq", 1, 0, tiled=True).astype(F32)
+    down_parts = at.list_seq(down_part)
+    down_grad = jnp.concatenate(
+        [
+            sum(
+                jnp.where(at.seq == s, block[:, s * nd : (s + 1) * nd].astype(F32), 0.0)
+                for s in range(seqs)
+            )
+            for block in down_parts
+        ]
+    )
 
     head_sum = sum(token_sum(g) for g in flat_grads).reshape(3, w)
     zero = jnp.zeros((D,), F32)

time: 1180 us -> 1110 us (0.941)
  local copies, waits for them, and re-layouts: 153 us -> 93.7 us
  waiting for transfers between devices: 179 us -> 236 us
  starting transfers between devices: 136 us -> 94.7 us
  matrix products: 89.5 us -> 51.4 us
  Pallas kernels: 486 us -> 513 us
    pallas_call x3 -> x7, Pallas kernels: 55 us -> 118 us  [the longest x2 28.7 us: head_products(): pl.pallas_call(partial(head_products_kernel, len(blocks)), grid_spec=pltp...]
    all_gather x3, waiting for transfers between devices: 49.2 us -> 0.02 us  [gather_by(): lax.all_gather(shard, ('pack', 'seq'), axis=0, tiled=True, axis_index_gro...]
    all_gather x1, waiting for transfers between devices: 0.02 us -> 47.1 us  [per_device(): down_mat = lax.all_gather(down_rows, ('pack', 'seq'), axis=0, tiled=True)]
    dot_general x19 -> x11, matrix products: 89.5 us -> 51.4 us  [dot(): return lax.dot_general(a, b, dims, preferred_element_type=F32)]
    reduce_scatter x1 -> x2, waiting for transfers between devices: 0.01 us -> 36.1 us  [scatter_all(): lax.psum_scatter(whole.reshape(-1, n), ('pack', 'seq'), scatter_dimension...]
    ppermute x9 -> x6, starting transfers between devices: 41.6 us -> 8.31 us  [ring(): return lax.ppermute(value, 'pack', pairs)]
    ppermute x9 -> x6, waiting for transfers between devices: 15.8 us -> 37.3 us  [ring(): return lax.ppermute(value, 'pack', pairs)]
    ppermute x8 -> x6, waiting for transfers between devices: 4.66 us -> 26 us  [cross(): return lax.ppermute(value, 'pack', [(p, p ^ 1) for p in range(self.packs)])]
  transfers between devices with their start and end apart: 71 -> 66, of which waited for: 21 -> 26; matrix products, arithmetic and copies ran while one was open for 28% -> 20% of each run, Pallas kernels for 33% -> 37%
where the time goes in v2:
time: 1110 us; the launch traced here: 1100 us
  Pallas kernels  513 us (46%)
  waiting for transfers between devices  236 us (21%)
  starting transfers between devices  94.7 us (9%)
  local copies, waits for them, and re-layouts  93.7 us (8%)
  other arithmetic  91.8 us (8%)
  matrix products  51.4 us (5%)
  between operations  16.4 us (1%)
    pallas_call x2, Pallas kernels, attend_backward(): pl.pallas_call(partial(backward_kernel, hpd, tq, tk), grid_spec=pltpu.Pre...  141 us
    pallas_call x1, Pallas kernels, feed(): pl.pallas_call(partial(feed_kernel, tm), grid_spec=pltpu.PrefetchScalarGr...  104 us
    pallas_call x2, Pallas kernels, attend_forward(): pl.pallas_call(partial(forward_kernel, hpd, tq, tk), grid_spec=pltpu.Pref...  78.6 us
    dot_general x11, matrix products, dot(): return lax.dot_general(a, b, dims, preferred_element_type=F32)  51.4 us
    all_gather x1, waiting for transfers between devices, per_device(): down_mat = lax.all_gather(down_rows, ('pack', 'seq'), axis=0, tiled=True)  47.1 us
    pallas_call x2, Pallas kernels, to_condition(): pl.pallas_call(partial(to_condition_kernel, parts, len(rest) > 0), grid=(...  41.8 us
    ppermute x6, waiting for transfers between devices, ring(): return lax.ppermute(value, 'pack', pairs)  37.3 us
    reduce_scatter x2, waiting for transfers between devices, scatter_all(): lax.psum_scatter(whole.reshape(-1, n), ('pack', 'seq'), scatter_dimension...  36.1 us
  transfers between devices with their start and end apart: 66, of which 26 were waited for; matrix products, arithmetic and copies ran while one was open for 20% of the time, Pallas kernels for 37%

profile of v2, /device:TPU:1, one launch (start us, length us, event | category | flops | bytes accessed | tf_op | source)
XLA Modules:
  0.0 1096.9 jit_solution(6172404871491720021)
XLA Ops:
  12.1 4.6 collective-permute-start.1
  16.8 4.3 collective-permute-done.1
  35.5 13.5 %collective-permute-done.4 = bf16[4,128]{1,0:T(4,128)(2,1)S(1)} collective-permute-done((bf16[4,128]{1,0:T(4,128)(2,1)S(1)}, bf16[4,128]{1,0:T(4,128)(2,1)S(1)}, u32[]{:S(2)}, u32[]{:S(2)}) %collective-permute-start.4) | collective-permute-done | bytes 1056 | tf_op jit(solution)/shard_map/ppermute | solution.py:814
  82.0 17.0 %collective-permute-done.16 = bf16[144,1504]{1,0:T(8,128)(2,1)S(1)} collective-permute-done((bf16[144,1504]{1,0:T(8,128)(2,1)S(1)}, bf16[144,1504]{1,0:T(8,128)(2,1)S(1)}, u32[]{:S(2)}, u32[]{:S(2)}) %collective-permute-start.16) | collective-permute-done | bytes 433184 | tf_op jit(solution)/shard_map/ppermute | solution.py:806
  99.1 19.4 %collective-permute-done.17 = bf16[144,1504]{1,0:T(8,128)(2,1)S(1)} collective-permute-done((bf16[144,1504]{1,0:T(8,128)(2,1)S(1)}, bf16[144,1504]{1,0:T(8,128)(2,1)S(1)}, u32[]{:S(2)}, u32[]{:S(2)}) %collective-permute-start.17) | collective-permute-done | bytes 433184 | tf_op jit(solution)/shard_map/ppermute | solution.py:806
  131.8 15.0 %mix_input.1 = (bf16[1152,1152]{1,0:T(8,128)(2,1)}, bf16[1152,1152]{1,0:T(8,128)(2,1)}, bf16[1152,1152]{1,0:T(8,128)(2,1)}) custom-call(bf16[1152,1152]{1,0:T(8,128)(2,1)} %bitcast.294, bf16[1152,1152]{1,0:T(8,128)(2,1)} %bitcast.267, bf16[4,1152,576]{2,1,0:T(8,128)(2,1)} %bitcast.277, f32[2,1,1152]{2,1,0:T(1,128)} %reshape.718.bias_ref), custom_call_target="tpu_custom_call" | custom-call | flops 6115295232 | bytes 18579456 | tf_op jit(solution)/shard_map/mix_input/pallas_call | solution.py:407
  166.0 13.5 %collective-permute-done.19 = bf16[4,144,1504]{2,1,0:T(8,128)(2,1)} collective-permute-done((bf16[4,144,1504]{2,1,0:T(8,128)(2,1)}, bf16[4,144,1504]{2,1,0:T(8,128)(2,1)}, u32[]{:S(2)}, u32[]{:S(2)}) %collective-permute-start.19) | collective-permute-done | bytes 1732640 | tf_op jit(solution)/shard_map/ppermute | solution.py:809
  179.5 4.8 collective-permute-done.20.refs_2_
  194.2 4.0 fusion.13
  202.0 4.0 fusion.17
  211.7 43.6 %attend_forward.2 = (bf16[1,2304,288]{2,1,0:T(8,128)(2,1)}, f32[1,2304,128]{2,1,0:T(8,128)}) custom-call(s32[1,3]{1,0:T(1,128)} %bitcast.319, s32[1,3]{1,0:T(1,128)} %bitcast.317, bf16[1,2304,864]{2,1,0:T(8,128)(2,1)} %bitcast.39.qkv_q.qkv_ref, bf16[1,2304,864]{2,1,0:T(8,128)(2,1)} %bitcast.39.qkv_q.qkv_ref, s32[1,2304,1]{2,1,0:T(8,128)} %copy.248.ids_q.ids_ref, ...), custom_call_target="tpu_custom_call" | custom-call | flops 61152952320 | bytes 5308416 | tf_op jit(solution)/shard_map/attend_forward/pallas_call | solution.py:186
  259.1 5.3 all-to-all-start
  264.4 3.9 fusion.23
  268.3 4.0 fusion.25
  277.4 9.9 all-to-all-done
  289.9 4.0 fusion.27
  293.9 35.0 %attend_forward.3 = (bf16[1,2304,288]{2,1,0:T(8,128)(2,1)}, f32[1,2304,128]{2,1,0:T(8,128)}) custom-call(s32[1,9]{1,0:T(1,128)} %bitcast.330, s32[1,9]{1,0:T(1,128)} %bitcast.329, bf16[1,2304,864]{2,1,0:T(8,128)(2,1)} %bitcast.291, bf16[1,2304,864]{2,1,0:T(8,128)(2,1)} %bitcast.292, s32[1,2304,1]{2,1,0:T(8,128)} %copy.251.ids_q.ids_ref, ...), custom_call_target="tpu_custom_call" | custom-call | flops 61152952320 | bytes 5308416 | tf_op jit(solution)/shard_map/attend_forward/pallas_call | solution.py:186
  332.6 4.6 all-to-all-start.1
  337.2 19.9 %feed_gates.1.gates_ref = bf16[4,1152,1152]{2,1,0:T(8,128)(2,1)} custom-call(bf16[1152,1152]{1,0:T(8,128)(2,1)} %get-tuple-element.109.act_ref, bf16[4,1152,1152]{2,1,0:T(8,128)(2,1)} %bitcast.321, f32[4,1,1152]{2,1,0:T(1,128)} %reshape.719.bias_ref), custom_call_target="tpu_custom_call" | custom-call | flops 12230590464 | bytes 23887872 | tf_op jit(solution)/shard_map/feed_gates/pallas_call | solution.py:426
  359.5 4.3 maximum_select_fusion.attn_ref
  363.8 14.1 %before_feed.1 = (bf16[1152,1152]{1,0:T(8,128)(2,1)}, f32[1152,1152]{1,0:T(8,128)}, bf16[1152,1152]{1,0:T(8,128)(2,1)}, bf16[1152,1152]{1,0:T(8,128)(2,1)}) custom-call(bf16[1152,1152]{1,0:T(8,128)(2,1)} %maximum_select_fusion.attn_ref, bf16[1152,1152]{1,0:T(8,128)(2,1)} %bitcast.268, bf16[1152,1152]{1,0:T(8,128)(2,1)} %bitcast.272, ...), custom_call_target="tpu_custom_call" | custom-call | flops 3057647616 | bytes 31850496 | tf_op jit(solution)/shard_map/before_feed/pallas_call | solution.py:457
  378.0 47.1 %all-gather.11.cloned.1.call-done = bf16[4608,1152]{1,0:T(8,128)(2,1)} async-done(((bf16[144,1152]{1,0:T(8,128)(2,1)}), bf16[4608,1152]{1,0:T(8,128)(2,1)}) %all-gather.11.cloned.1.call-update) | async-done | bytes 10616848 | tf_op jit(solution)/shard_map/all_gather | solution.py:1011
  425.1 104.2 %feed.1 = (f32[1152,1152]{1,0:T(8,128)}, f32[1152,1152]{1,0:T(8,128)}, bf16[4,1152,1152]{2,1,0:T(8,128)(2,1)}, bf16[4,1152,1152]{2,1,0:T(8,128)(2,1)}, f32[4,1,1152]{2,1,0:T(1,128)}) custom-call(bf16[1152,1152]{1,0:T(8,128)(2,1)} %get-tuple-element.113.input_ref, bf16[1152,1152]{1,0:T(8,128)(2,1)} %get-tuple-element.114.grad_ref, ...), custom_call_target="tpu_custom_call" | custom-call | flops 73383542784 | bytes 63700992 | tf_op jit(solution)/shard_map/feed/pallas_call | solution.py:528
  531.3 22.4 %after_feed.1 = (bf16[1152,1152]{1,0:T(8,128)(2,1)}, bf16[4,1152,1152]{2,1,0:T(8,128)(2,1)}, bf16[1152,1152]{1,0:T(8,128)(2,1)}, bf16[4,2,576,288]{3,2,1,0:T(8,128)(2,1)}, f32[1152,1152]{1,0:T(8,128)}) custom-call(s32[1]{0:T(128)} %bitcast.18.first, f32[1152,1152]{1,0:T(8,128)} %get-tuple-element.117.branch_ref, f32[1152,1152]{1,0:T(8,128)} %get-tuple-element.118.shift_ref, ...), custom_call_target="tpu_custom_call" | custom-call | flops 3057647616 | bytes 58392576 | tf_op jit(solution)/shard_map/after_feed/pallas_call | solution.py:592
  553.7 5.7 copy.258
  559.5 4.0 all-to-all-start.2
  563.5 6.8 convolution_convert_fusion.2
  574.5 24.1 %late_products.1 = (bf16[2,1152,1152]{2,1,0:T(8,128)(2,1)}, bf16[2,1152,1152]{2,1,0:T(8,128)(2,1)}, f32[4,1,1152]{2,1,0:T(1,128)}) custom-call(s32[4]{0:T(128)} %pad_add_fusion.1.order, bf16[1152,1152]{1,0:T(8,128)(2,1)} %get-tuple-element.109.act_ref, bf16[4,1152,1152]{2,1,0:T(8,128)(2,1)} %get-tuple-element.148.grad_ref.grads_ref), custom_call_target="tpu_custom_call" | custom-call | flops 12230590464 | bytes 23887872 | tf_op jit(solution)/shard_map/late_products/pallas_call | solution.py:640
  602.2 4.8 all-to-all-done.2
  612.4 83.9 %attend_backward.2 = bf16[1,2304,864]{2,1,0:T(8,128)(2,1)} custom-call(s32[1,3]{1,0:T(1,128)} %bitcast.320, s32[1,3]{1,0:T(1,128)} %bitcast.318, bf16[1,2304,864]{2,1,0:T(8,128)(2,1)} %bitcast.39.qkv_q.qkv_ref, bf16[1,2304,288]{2,1,0:T(8,128)(2,1)} %bitcast.303, bf16[1,2304,288]{2,1,0:T(8,128)(2,1)} %get-tuple-element.105.o_ref, ...), custom_call_target="tpu_custom_call" | custom-call | flops 91729428480 | bytes 11943936 | tf_op jit(solution)/shard_map/attend_backward/pallas_call | solution.py:312
  696.3 8.1 convolution_convert_fusion.1
  714.3 5.9 add_convert_fusion
  729.0 57.0 %attend_backward.3 = bf16[1,2304,864]{2,1,0:T(8,128)(2,1)} custom-call(s32[1,3]{1,0:T(1,128)} %bitcast.327, s32[1,3]{1,0:T(1,128)} %bitcast.328, bf16[1,2304,864]{2,1,0:T(8,128)(2,1)} %bitcast.293, bf16[1,2304,288]{2,1,0:T(8,128)(2,1)} %bitcast.302, bf16[1,2304,288]{2,1,0:T(8,128)(2,1)} %get-tuple-element.129.o_ref, ...), custom_call_target="tpu_custom_call" | custom-call | flops 91729428480 | bytes 11943936 | tf_op jit(solution)/shard_map/attend_backward/pallas_call | solution.py:312
  788.7 8.5 convolution_convert_fusion
  813.0 26.1 %reduce-scatter.6.cloned.1.call-done = bf16[144,1152]{1,0:T(8,128)(2,1)} async-done(((bf16[4608,1152]{1,0:T(8,128)(2,1)}), bf16[144,1152]{1,0:T(8,128)(2,1)}) %reduce-scatter.6.cloned.1.call-update) | async-done | bytes 331792 | tf_op jit(solution)/shard_map/reduce_scatter | solution.py:876
  841.0 13.7 %head_products.2.refs_5_ = f32[1152,864]{1,0:T(8,128)} custom-call(s32[4]{0:T(128)} %pad_add_fusion.places, bf16[576,1152]{1,0:T(8,128)(2,1)} %get-tuple-element.238.refs_0_, bf16[576,1152]{1,0:T(8,128)(2,1)} %collective-permute-done.22.refs_1_, bf16[576,1152]{1,0:T(8,128)(2,1)} %collective-permute-done.20.refs_2_, bf16[576,1152]{1,0:T(8,128)(2,1)} %copy-done.47, ...), custom_call_target="tpu_custom_call" | custom-call | flops 4586471424 | bytes 11943936 | tf_op jit(solution)/shard_map/head_products/pallas_call | solution.py:704
  857.1 15.0 %head_products.3 = f32[1152,864]{1,0:T(8,128)} custom-call(s32[4]{0:T(128)} %pad_add_fusion.places, bf16[576,1152]{1,0:T(8,128)(2,1)} %get-tuple-element.100.refs_0_, bf16[576,1152]{1,0:T(8,128)(2,1)} %collective-permute-done.24.refs_1_, bf16[576,1152]{1,0:T(8,128)(2,1)} %collective-permute-done.21.refs_2_, ...), custom_call_target="tpu_custom_call" | custom-call | flops 4586471424 | bytes 11943936 | tf_op jit(solution)/shard_map/head_products/pallas_call | solution.py:704
  890.1 10.2 collective-permute-done.35
  903.1 9.0 collective-permute-done.31
  916.3 10.6 after_mix.1
  931.5 12.6 %early_products.1 = (bf16[4,1152,576]{2,1,0:T(8,128)(2,1)}, f32[2,1,1152]{2,1,0:T(1,128)}) custom-call(bf16[1152,1152]{1,0:T(8,128)(2,1)} %get-tuple-element.109.act_ref, bf16[2,1152,1152]{2,1,0:T(8,128)(2,1)} %get-tuple-element.138.grad_ref.grads_ref), custom_call_target="tpu_custom_call" | custom-call | flops 6115295232 | bytes 13271040 | tf_op jit(solution)/shard_map/early_products/pallas_call | solution.py:672
  961.8 29.3 %all-to-all-done.3 = bf16[2,4,144,1152]{3,2,0,1:T(8,128)(2,1)S(1)} async-done(((bf16[2,4,144,1152]{3,2,0,1:T(8,128)(2,1)}), bf16[2,4,144,1152]{3,2,0,1:T(8,128)(2,1)S(1)}, u32[]{:S(2)}, u32[]{:S(2)}) %all-to-all-start.3) | async-done | bytes 2654240 | tf_op jit(solution)/shard_map/all_to_all | solution.py:894
  998.9 4.5 all-to-all-start.4
  1003.4 23.6 %to_condition.2.refs_0_ = f32[1152,1152]{1,0:T(8,128)} custom-call(bf16[4,1152,1152]{2,1,0:T(8,128)(2,1)} %get-tuple-element.148.grad_ref.grads_ref, bf16[4,1152,1152]{2,1,0:T(8,128)(2,1)} %bitcast.322), custom_call_target="tpu_custom_call" | custom-call | flops 12230590464 | bytes 26542080 | tf_op jit(solution)/shard_map/to_condition/pallas_call | solution.py:779
  1029.4 18.2 %to_condition.3 = f32[1152,1152]{1,0:T(8,128)} custom-call(bf16[2,1152,1152]{2,1,0:T(8,128)(2,1)} %get-tuple-element.138.grad_ref.grads_ref, bf16[4,1152,576]{2,1,0:T(8,128)(2,1)} %bitcast.278, f32[1152,1152]{1,0:T(8,128)} %to_condition.2.refs_0_, bf16[1152,1152]{1,0:T(8,128)(2,1)} %bitcast.295), custom_call_target="tpu_custom_call" | custom-call | flops 6115295232 | bytes 21233664 | tf_op jit(solution)/shard_map/to_condition/pallas_call | solution.py:779
  1061.0 9.9 reduce-scatter.8.cloned.1.call-done
  1071.0 4.3 collective-permute-start.36
  1082.7 4.9 collective-permute-done.39
  (417 shorter events, 257.4 us)
Async XLA Ops:
  7.2 112.3 %all-gather.5.cloned.1.call-start = ((), (), s32[]{:S(2)}) async-start(), calls=%async_computation.10 | async-start | bytes 6082560 | tf_op jit(solution)/shard_map/all_gather | solution.py:821
  10.0 11.0 %collective-permute-start = (bf16[144,1152]{1,0:T(8,128)(2,1)S(1)}, bf16[144,1152]{1,0:T(8,128)(2,1)S(1)}, u32[]{:S(2)}, u32[]{:S(2)}) collective-permute-start(bf16[144,1152]{1,0:T(8,128)(2,1)S(1)} %maximum_select_fusion.3), channel_id=1, source_target_pairs={{0,1},{1,0},{3,2},{4,5},{5,4},{7,6},{8,9},{9,8},{11,10},{12,13},{1... | collective-permute-start | bytes 995336 | tf_op jit(solution)/shard_map/ppermute | solution.py:957
  23.5 313.6 %all-gather.7.cloned.1.call-start = ((), (), s32[]{:S(2)}) async-start(), calls=%async_computation.11 | async-start | bytes 10948608 | tf_op jit(solution)/shard_map/all_gather | solution.py:821
  30.9 25.7 %collective-permute-start.14 = (bf16[144,2304]{1,0:T(8,128)(2,1)S(1)}, bf16[144,2304]{1,0:T(8,128)(2,1)S(1)}, u32[]{:S(2)}, u32[]{:S(2)}) collective-permute-start(bf16[144,2304]{1,0:T(8,128)(2,1)S(1)} %concatenate.68), channel_id=1, source_target_pairs={{0,2},{1,3},{2,0},{3,1},{4,6},{5,7},{6,4},{7,5},{8,10},{9,11},{10,... | collective-permute-start | bytes 1990664 | tf_op jit(solution)/shard_map/ppermute | solution.py:814
  32.7 29.1 %collective-permute-start.13 = (bf16[144,2304]{1,0:T(8,128)(2,1)S(1)}, bf16[144,2304]{1,0:T(8,128)(2,1)S(1)}, u32[]{:S(2)}, u32[]{:S(2)}) collective-permute-start(bf16[144,2304]{1,0:T(8,128)(2,1)S(1)} %concatenate.68), channel_id=1, source_target_pairs={{0,1},{1,0},{2,3},{3,2},{4,5},{5,4},{6,7},{7,6},{8,9},{9,8},{10,11... | collective-permute-start | bytes 1990664 | tf_op jit(solution)/shard_map/ppermute | solution.py:817
  33.4 16.6 %collective-permute-start.3 = (bf16[4,128]{1,0:T(4,128)(2,1)S(1)}, bf16[4,128]{1,0:T(4,128)(2,1)S(1)}, u32[]{:S(2)}, u32[]{:S(2)}) collective-permute-start(bf16[4,128]{1,0:T(4,128)(2,1)S(1)} %pad_bitcast_fusion.1), channel_id=1, source_target_pairs={{0,1},{1,0},{2,3},{3,2},{4,5},{5,4},{6,7},{7,6},{8,9},{9,8},{10,11... | collective-permute-start | bytes 3080 | tf_op jit(solution)/shard_map/ppermute | solution.py:817
  33.4 15.6 %collective-permute-start.4 = (bf16[4,128]{1,0:T(4,128)(2,1)S(1)}, bf16[4,128]{1,0:T(4,128)(2,1)S(1)}, u32[]{:S(2)}, u32[]{:S(2)}) collective-permute-start(bf16[4,128]{1,0:T(4,128)(2,1)S(1)} %pad_bitcast_fusion.1), channel_id=1, source_target_pairs={{0,2},{1,3},{2,0},{3,1},{4,6},{5,7},{6,4},{7,5},{8,10},{9,11},{10,... | collective-permute-start | bytes 3080 | tf_op jit(solution)/shard_map/ppermute | solution.py:814
  34.3 45.7 %collective-permute-start.2 = (bf16[144,1152]{1,0:T(8,128)(2,1)}, bf16[144,1152]{1,0:T(8,128)(2,1)}, u32[]{:S(2)}, u32[]{:S(2)}) collective-permute-start(bf16[144,1152]{1,0:T(8,128)(2,1)} %slice.290), channel_id=1, source_target_pairs={{2,1},{6,5},{10,9},{14,13},{18,17},{22,21},{26,25},{30,29}} | collective-permute-start | bytes 995336 | tf_op jit(solution)/shard_map/ppermute | solution.py:965
  76.6 22.5 %collective-permute-start.16 = (bf16[144,1504]{1,0:T(8,128)(2,1)S(1)}, bf16[144,1504]{1,0:T(8,128)(2,1)S(1)}, u32[]{:S(2)}, u32[]{:S(2)}) collective-permute-start(bf16[144,1504]{1,0:T(8,128)(2,1)S(1)} %pad_maximum_fusion.2), channel_id=1, source_target_pairs={{0,8},{4,12},{8,16},{12,20},{16,24},{20,28},{24,0},{28,4},{1,9},{5... | collective-permute-start | bytes 1299464 | tf_op jit(solution)/shard_map/ppermute | solution.py:806
  76.7 41.8 %collective-permute-start.17 = (bf16[144,1504]{1,0:T(8,128)(2,1)S(1)}, bf16[144,1504]{1,0:T(8,128)(2,1)S(1)}, u32[]{:S(2)}, u32[]{:S(2)}) collective-permute-start(bf16[144,1504]{1,0:T(8,128)(2,1)S(1)} %pad_maximum_fusion.2), channel_id=1, source_target_pairs={{0,16},{4,20},{8,24},{12,28},{16,0},{20,4},{24,8},{28,12},{1,17},{... | collective-permute-start | bytes 1299464 | tf_op jit(solution)/shard_map/ppermute | solution.py:806
  79.1 39.4 %collective-permute-start.18 = (bf16[144,1504]{1,0:T(8,128)(2,1)S(1)}, bf16[144,1504]{1,0:T(8,128)(2,1)S(1)}, u32[]{:S(2)}, u32[]{:S(2)}) collective-permute-start(bf16[144,1504]{1,0:T(8,128)(2,1)S(1)} %pad_maximum_fusion.2), channel_id=1, source_target_pairs={{0,24},{4,28},{8,0},{12,4},{16,8},{20,12},{24,16},{28,20},{1,25},{... | collective-permute-start | bytes 1299464 | tf_op jit(solution)/shard_map/ppermute | solution.py:806
  118.5 259.4 %all-gather.9.cloned.1.call-start = ((), (), s32[]{:S(2)}) async-start(), calls=%async_computation.12 | async-start | bytes 10948608 | tf_op jit(solution)/shard_map/all_gather | solution.py:821
  119.6 305.5 %all-gather.11.cloned.1.call-start = ((), (), s32[]{:S(2)}) async-start(), calls=%async_computation.13 | async-start | bytes 10948608 | tf_op jit(solution)/shard_map/all_gather | solution.py:1011
  128.7 50.8 %collective-permute-start.19 = (bf16[4,144,1504]{2,1,0:T(8,128)(2,1)}, bf16[4,144,1504]{2,1,0:T(8,128)(2,1)}, u32[]{:S(2)}, u32[]{:S(2)}) collective-permute-start(bf16[4,144,1504]{2,1,0:T(8,128)(2,1)} %bitcast_dynamic-update-slice_fusion.2), channel_id=1, source_target_pairs={{0,4},{4,0},{8,12},{12,8},{16,20},{20,16},{24,28},{28,24},{1,5},{5... | collective-permute-start | bytes 5197832 | tf_op jit(solution)/shard_map/ppermute | solution.py:809
  150.2 34.1 %collective-permute-start.20 = (bf16[576,1152]{1,0:T(8,128)(2,1)}, bf16[576,1152]{1,0:T(8,128)(2,1)}, u32[]{:S(2)}, u32[]{:S(2)}) collective-permute-start(bf16[576,1152]{1,0:T(8,128)(2,1)} %get-tuple-element.238.refs_0_), channel_id=1, source_target_pairs={{0,2},{1,3},{2,0},{3,1},{4,6},{5,7},{6,4},{7,5},{8,10},{9,11},{10,... | collective-permute-start | bytes 3981320 | tf_op jit(solution)/shard_map/ppermute | solution.py:814
  159.4 38.8 %collective-permute-start.22 = (bf16[576,1152]{1,0:T(8,128)(2,1)}, bf16[576,1152]{1,0:T(8,128)(2,1)}, u32[]{:S(2)}, u32[]{:S(2)}) collective-permute-start(bf16[576,1152]{1,0:T(8,128)(2,1)} %get-tuple-element.238.refs_0_), channel_id=1, source_target_pairs={{0,1},{1,0},{2,3},{3,2},{4,5},{5,4},{6,7},{7,6},{8,9},{9,8},{10,11... | collective-permute-start | bytes 3981320 | tf_op jit(solution)/shard_map/ppermute | solution.py:817
  184.3 71.1 %collective-permute-start.21 = (bf16[576,1152]{1,0:T(8,128)(2,1)}, bf16[576,1152]{1,0:T(8,128)(2,1)}, u32[]{:S(2)}, u32[]{:S(2)}) collective-permute-start(bf16[576,1152]{1,0:T(8,128)(2,1)} %get-tuple-element.100.refs_0_), channel_id=1, source_target_pairs={{0,2},{1,3},{2,0},{3,1},{4,6},{5,7},{6,4},{7,5},{8,10},{9,11},{10,... | collective-permute-start | bytes 3981320 | tf_op jit(solution)/shard_map/ppermute | solution.py:814
  185.6 78.8 %collective-permute-start.24 = (bf16[576,1152]{1,0:T(8,128)(2,1)}, bf16[576,1152]{1,0:T(8,128)(2,1)}, u32[]{:S(2)}, u32[]{:S(2)}) collective-permute-start(bf16[576,1152]{1,0:T(8,128)(2,1)} %get-tuple-element.100.refs_0_), channel_id=1, source_target_pairs={{0,1},{1,0},{2,3},{3,2},{4,5},{5,4},{6,7},{7,6},{8,9},{9,8},{10,11... | collective-permute-start | bytes 3981320 | tf_op jit(solution)/shard_map/ppermute | solution.py:817
  191.4 80.9 %collective-permute-start.26 = (bf16[1152,640]{1,0:T(8,128)(2,1)}, bf16[1152,640]{1,0:T(8,128)(2,1)}, u32[]{:S(2)}, u32[]{:S(2)}) collective-permute-start(bf16[1152,640]{1,0:T(8,128)(2,1)} %slice.402), channel_id=1, source_target_pairs={{0,1},{1,0},{2,3},{3,2},{4,5},{5,4},{6,7},{7,6},{8,9},{9,8},{10,11... | collective-permute-start | bytes 4423688 | tf_op jit(solution)/shard_map/ppermute | solution.py:817
  191.4 17.7 %collective-permute-start.23 = (bf16[576,1152]{1,0:T(8,128)(2,1)}, bf16[576,1152]{1,0:T(8,128)(2,1)S(1)}, u32[]{:S(2)}, u32[]{:S(2)}) collective-permute-start(bf16[576,1152]{1,0:T(8,128)(2,1)} %collective-permute-done.20.refs_2_), channel_id=1, source_target_pairs={{0,1},{1,0},{2,3},{3,2},{4,5},{5,4},{6,7},{7,6},{8,9},{9,8},{10,11... | collective-permute-start | bytes 3981320 | tf_op jit(solution)/shard_map/ppermute | solution.py:817
  255.3 34.6 %collective-permute-start.25 = (bf16[576,1152]{1,0:T(8,128)(2,1)}, bf16[576,1152]{1,0:T(8,128)(2,1)}, u32[]{:S(2)}, u32[]{:S(2)}) collective-permute-start(bf16[576,1152]{1,0:T(8,128)(2,1)} %collective-permute-done.21.refs_2_), channel_id=1, source_target_pairs={{0,1},{1,0},{2,3},{3,2},{4,5},{5,4},{6,7},{7,6},{8,9},{9,8},{10,11... | collective-permute-start | bytes 3981320 | tf_op jit(solution)/shard_map/ppermute | solution.py:817
  259.1 28.2 %all-to-all-start = ((bf16[4,576,288]{1,2,0:T(8,128)(2,1)}), bf16[4,576,288]{1,2,0:T(8,128)(2,1)}, u32[]{:S(2)}, u32[]{:S(2)}) async-start(bf16[4,576,288]{1,2,0:T(8,128)(2,1)} %copy.250), calls=%async_computation | async-start | bytes 2949120 | tf_op jit(solution)/shard_map/all_to_all | solution.py:1068
  332.6 25.2 %all-to-all-start.1 = ((bf16[4,576,288]{1,2,0:T(8,128)(2,1)}), bf16[4,576,288]{1,2,0:T(8,128)(2,1)S(1)}, u32[]{:S(2)}, u32[]{:S(2)}) async-start(bf16[4,576,288]{1,2,0:T(8,128)(2,1)} %copy.253), calls=%async_computation.1 | async-start | bytes 2949120 | tf_op jit(solution)/shard_map/all_to_all | solution.py:1068
  337.1 359.2 %reduce-scatter.4.cloned.1.call-start = ((), (), s32[]{:S(2)}) async-start(), calls=%async_computation.14 | async-start | bytes 10948608 | tf_op jit(solution)/shard_map/reduce_scatter | solution.py:1091
  559.5 47.5 %all-to-all-start.2 = ((bf16[4,2,576,288]{2,3,1,0:T(8,128)(2,1)}), bf16[4,2,576,288]{2,3,1,0:T(8,128)(2,1)S(1)}, u32[]{:S(2)}, u32[]{:S(2)}) async-start(bf16[4,2,576,288]{2,3,1,0:T(8,128)(2,1)} %copy.258), calls=%async_computation.2 | async-start | bytes 5898240 | tf_op jit(solution)/shard_map/all_to_all | solution.py:1095
  563.5 275.7 %reduce-scatter.6.cloned.1.call-start = ((), (), s32[]{:S(2)}) async-start(), calls=%async_computation.15 | async-start | bytes 10948608 | tf_op jit(solution)/shard_map/reduce_scatter | solution.py:876
  572.9 26.2 %collective-permute-start.27 = (bf16[8,72,1152]{2,1,0:T(8,128)(2,1)}, bf16[8,72,1152]{2,1,0:T(8,128)(2,1)}, u32[]{:S(2)}, u32[]{:S(2)}) collective-permute-start(bf16[8,72,1152]{2,1,0:T(8,128)(2,1)} %dynamic-slice_bitcast_fusion.4), channel_id=1, source_target_pairs={{0,1},{1,0},{2,3},{3,2},{4,5},{5,4},{6,7},{7,6},{8,9},{9,8},{10,11... | collective-permute-start | bytes 3981320 | tf_op jit(solution)/shard_map/ppermute | solution.py:817
  598.6 115.7 %collective-permute-start.33 = (bf16[2,1152,1152]{2,1,0:T(8,128)(2,1)}, bf16[2,1152,1152]{2,1,0:T(8,128)(2,1)}, u32[]{:S(2)}, u32[]{:S(2)}) collective-permute-start(bf16[2,1152,1152]{2,1,0:T(8,128)(2,1)} %get-tuple-element.144), channel_id=1, source_target_pairs={{0,1},{1,0},{2,3},{3,2},{4,5},{5,4},{6,7},{7,6},{8,9},{9,8},{10,11... | collective-permute-start | bytes 15925256 | tf_op jit(solution)/shard_map/ppermute | solution.py:817
  707.8 16.4 %collective-permute-start.28 = (bf16[2,576,1152]{2,1,0:T(8,128)(2,1)}, bf16[2,576,1152]{2,1,0:T(8,128)(2,1)}, u32[]{:S(2)}, u32[]{:S(2)}) collective-permute-start(bf16[2,576,1152]{2,1,0:T(8,128)(2,1)} %dynamic-slice_bitcast_fusion.1), channel_id=1, source_target_pairs={{0,1},{1,0},{2,3},{3,2},{4,5},{5,4},{6,7},{7,6},{8,9},{9,8},{10,11... | collective-permute-start | bytes 7962632 | tf_op jit(solution)/shard_map/ppermute | solution.py:817
  709.5 95.2 %collective-permute-start.32 = (bf16[1,4,72,1152]{3,2,1,0:T(8,128)(2,1)}, bf16[1,4,72,1152]{3,2,1,0:T(8,128)(2,1)}, u32[]{:S(2)}, u32[]{:S(2)}) collective-permute-start(bf16[1,4,72,1152]{3,2,1,0:T(8,128)(2,1)} %dynamic-slice_bitcast_fusion.8), channel_id=1, source_target_pairs={{0,4},{4,0},{8,12},{12,8},{16,20},{20,16},{24,28},{28,24},{1,5},{5... | collective-permute-start | bytes 1990664 | tf_op jit(solution)/shard_map/ppermute | solution.py:809
  723.8 83.2 %collective-permute-start.34 = (bf16[2,4,144,1152]{3,2,0,1:T(8,128)(2,1)}, bf16[2,4,144,1152]{3,2,0,1:T(8,128)(2,1)}, u32[]{:S(2)}, u32[]{:S(2)}) collective-permute-start(bf16[2,4,144,1152]{3,2,0,1:T(8,128)(2,1)} %bitcast.245), channel_id=1, source_target_pairs={{0,4},{4,0},{8,12},{12,8},{16,20},{20,16},{24,28},{28,24},{1,5},{5... | collective-permute-start | bytes 7962632 | tf_op jit(solution)/shard_map/ppermute | solution.py:809
  728.7 57.3 %collective-permute-start.29 = (bf16[576,1152]{1,0:T(8,128)(2,1)}, bf16[576,1152]{1,0:T(8,128)(2,1)}, u32[]{:S(2)}, u32[]{:S(2)}) collective-permute-start(bf16[576,1152]{1,0:T(8,128)(2,1)} %dynamic-slice_bitcast_fusion.3), channel_id=1, source_target_pairs={{0,2},{1,3},{2,0},{3,1},{4,6},{5,7},{6,4},{7,5},{8,10},{9,11},{10,... | collective-permute-start | bytes 3981320 | tf_op jit(solution)/shard_map/ppermute | solution.py:814
  801.2 75.7 %collective-permute-start.30 = (bf16[2,576,1152]{2,1,0:T(8,128)(2,1)}, bf16[2,576,1152]{2,1,0:T(8,128)(2,1)}, u32[]{:S(2)}, u32[]{:S(2)}) collective-permute-start(bf16[2,576,1152]{2,1,0:T(8,128)(2,1)} %dynamic-slice_bitcast_fusion), channel_id=1, source_target_pairs={{0,1},{1,0},{2,3},{3,2},{4,5},{5,4},{6,7},{7,6},{8,9},{9,8},{10,11... | collective-permute-start | bytes 7962632 | tf_op jit(solution)/shard_map/ppermute | solution.py:817
  811.0 43.7 %collective-permute-start.47 = (bf16[144,1152]{1,0:T(8,128)(2,1)S(1)}, bf16[144,1152]{1,0:T(8,128)(2,1)S(1)}, u32[]{:S(2)}, u32[]{:S(2)}) collective-permute-start(bf16[144,1152]{1,0:T(8,128)(2,1)S(1)} %copy-done.27), channel_id=1, source_target_pairs={{0,2},{1,3},{2,0},{3,1},{4,6},{5,7},{6,4},{7,5},{8,10},{9,11},{10,... | collective-permute-start | bytes 995336 | tf_op jit(solution)/shard_map/ppermute | solution.py:814
  812.4 69.7 %collective-permute-start.46 = (bf16[144,1152]{1,0:T(8,128)(2,1)S(1)}, bf16[144,1152]{1,0:T(8,128)(2,1)}, u32[]{:S(2)}, u32[]{:S(2)}) collective-permute-start(bf16[144,1152]{1,0:T(8,128)(2,1)S(1)} %copy-done.27), channel_id=1, source_target_pairs={{0,1},{1,0},{2,3},{3,2},{4,5},{5,4},{6,7},{7,6},{8,9},{9,8},{10,11... | collective-permute-start | bytes 995336 | tf_op jit(solution)/shard_map/ppermute | solution.py:817
  854.6 27.4 %collective-permute-start.48 = (bf16[144,1152]{1,0:T(8,128)(2,1)S(1)}, bf16[144,1152]{1,0:T(8,128)(2,1)S(1)}, u32[]{:S(2)}, u32[]{:S(2)}) collective-permute-start(bf16[144,1152]{1,0:T(8,128)(2,1)S(1)} %collective-permute-done.47), channel_id=1, source_target_pairs={{0,1},{1,0},{2,3},{3,2},{4,5},{5,4},{6,7},{7,6},{8,9},{9,8},{10,11... | collective-permute-start | bytes 995336 | tf_op jit(solution)/shard_map/ppermute | solution.py:817
  875.6 24.8 %collective-permute-start.35 = (bf16[1,4,144,864]{3,2,0,1:T(8,128)(2,1)}, bf16[1,4,144,864]{3,2,0,1:T(8,128)(2,1)}, u32[]{:S(2)}, u32[]{:S(2)}) collective-permute-start(bf16[1,4,144,864]{3,2,0,1:T(8,128)(2,1)} %dynamic-slice_bitcast_fusion.7), channel_id=1, source_target_pairs={{0,4},{4,0},{8,12},{12,8},{16,20},{20,16},{24,28},{28,24},{1,5},{5... | collective-permute-start | bytes 2985992 | tf_op jit(solution)/shard_map/ppermute | solution.py:809
  881.3 30.8 %collective-permute-start.31 = (bf16[576,1152]{1,0:T(8,128)(2,1)}, bf16[576,1152]{1,0:T(8,128)(2,1)}, u32[]{:S(2)}, u32[]{:S(2)}) collective-permute-start(bf16[576,1152]{1,0:T(8,128)(2,1)} %dynamic-slice_bitcast_fusion.2), channel_id=1, source_target_pairs={{0,2},{1,3},{2,0},{3,1},{4,6},{5,7},{6,4},{7,5},{8,10},{9,11},{10,... | collective-permute-start | bytes 3981320 | tf_op jit(solution)/shard_map/ppermute | solution.py:814
  886.6 40.4 %all-to-all-start.5 = ((bf16[1,4,72,1152]{3,2,0,1:T(8,128)(2,1)}), bf16[1,4,72,1152]{3,2,0,1:T(8,128)(2,1)S(1)}, u32[]{:S(2)}, u32[]{:S(2)}) async-start(bf16[1,4,72,1152]{3,2,0,1:T(8,128)(2,1)} %bitcast.299), calls=%async_computation.8 | async-start | bytes 1327104 | tf_op jit(solution)/shard_map/all_to_all | solution.py:894
  927.8 63.3 %all-to-all-start.3 = ((bf16[2,4,144,1152]{3,2,0,1:T(8,128)(2,1)}), bf16[2,4,144,1152]{3,2,0,1:T(8,128)(2,1)S(1)}, u32[]{:S(2)}, u32[]{:S(2)}) async-start(bf16[2,4,144,1152]{3,2,0,1:T(8,128)(2,1)} %fusion), calls=%async_computation.6 | async-start | bytes 5308416 | tf_op jit(solution)/shard_map/all_to_all | solution.py:894
  931.5 139.5 %reduce-scatter.8.cloned.1.call-start = ((), (), s32[]{:S(2)}) async-start(), calls=%async_computation.16 | async-start | bytes 6082560 | tf_op jit(solution)/shard_map/reduce_scatter | solution.py:876
  994.6 32.4 %collective-permute-start.45 = (bf16[72,288]{1,0:T(8,128)(2,1)S(1)}, bf16[72,288]{1,0:T(8,128)(2,1)S(1)}, u32[]{:S(2)}, u32[]{:S(2)}) collective-permute-start(bf16[72,288]{1,0:T(8,128)(2,1)S(1)} %bitcast.310), channel_id=1, source_target_pairs={{0,1},{1,0},{2,3},{3,2},{4,5},{5,4},{6,7},{7,6},{8,9},{9,8},{10,11... | collective-permute-start | bytes 124424 | tf_op jit(solution)/shard_map/ppermute | solution.py:817
  998.9 49.3 %all-to-all-start.4 = ((bf16[1,4,144,864]{3,2,0,1:T(8,128)(2,1)}), bf16[1,4,144,864]{3,2,0,1:T(8,128)(2,1)}, u32[]{:S(2)}, u32[]{:S(2)}) async-start(bf16[1,4,144,864]{3,2,0,1:T(8,128)(2,1)} %fusion.11), calls=%async_computation.7 | async-start | bytes 2064384 | tf_op jit(solution)/shard_map/all_to_all | solution.py:894
  1028.5 24.6 %collective-permute-start.37 = (bf16[144,1152]{1,0:T(8,128)(2,1)S(1)}, bf16[144,1152]{1,0:T(8,128)(2,1)S(1)}, u32[]{:S(2)}, u32[]{:S(2)}) collective-permute-start(bf16[144,1152]{1,0:T(8,128)(2,1)S(1)} %dynamic-slice_bitcast_fusion.9), channel_id=1, source_target_pairs={{0,2},{1,3},{2,0},{3,1},{4,6},{5,7},{6,4},{7,5},{8,10},{9,11},{10,... | collective-permute-start | bytes 995336 | tf_op jit(solution)/shard_map/ppermute | solution.py:814
  1049.6 11.4 %collective-permute-start.41 = (bf16[144,864]{1,0:T(8,128)(2,1)S(1)}, bf16[144,864]{1,0:T(8,128)(2,1)S(1)}, u32[]{:S(2)}, u32[]{:S(2)}) collective-permute-start(bf16[144,864]{1,0:T(8,128)(2,1)S(1)} %reduce.11), channel_id=1, source_target_pairs={{0,1},{1,0},{2,3},{3,2},{4,5},{5,4},{6,7},{7,6},{8,9},{9,8},{10,11... | collective-permute-start | bytes 746504 | tf_op jit(solution)/shard_map/ppermute | solution.py:817
  1054.2 27.3 %collective-permute-start.38 = (bf16[144,1152]{1,0:T(8,128)(2,1)S(1)}, bf16[144,1152]{1,0:T(8,128)(2,1)}, u32[]{:S(2)}, u32[]{:S(2)}) collective-permute-start(bf16[144,1152]{1,0:T(8,128)(2,1)S(1)} %fusion.31), channel_id=1, source_target_pairs={{0,1},{1,2},{4,5},{5,6},{8,9},{9,10},{12,13},{13,14},{16,17},{17,1... | collective-permute-start | bytes 995336 | tf_op jit(solution)/shard_map/ppermute | solution.py:1163
  1057.8 24.9 %collective-permute-start.40 = (bf16[144,576]{1,0:T(8,128)(2,1)}, bf16[144,576]{1,0:T(8,128)(2,1)}, u32[]{:S(2)}, u32[]{:S(2)}) collective-permute-start(bf16[144,576]{1,0:T(8,128)(2,1)} %slice.408), channel_id=1, source_target_pairs={{2,3},{6,7},{10,11},{14,15},{18,19},{22,23},{26,27},{30,31}} | collective-permute-start | bytes 497672 | tf_op jit(solution)/shard_map/ppermute | solution.py:1164
  1060.1 15.2 %collective-permute-start.43 = (bf16[144,864]{1,0:T(8,128)(2,1)S(1)}, bf16[144,864]{1,0:T(8,128)(2,1)S(1)}, u32[]{:S(2)}, u32[]{:S(2)}) collective-permute-start(bf16[144,864]{1,0:T(8,128)(2,1)S(1)} %collective-permute-done.42), channel_id=1, source_target_pairs={{0,1},{1,0},{2,3},{3,2},{4,5},{5,4},{6,7},{7,6},{8,9},{9,8},{10,11... | collective-permute-start | bytes 746504 | tf_op jit(solution)/shard_map/ppermute | solution.py:817
  (67 other events, 705.4 us)
Sparse Core Ops, SparseCore 0:
  23.6 92.5 all-gather.4
  119.8 122.9 all-gather.6
  245.7 88.3 all-gather.8
  337.4 87.6 all-gather.10
  529.5 144.1 reduce-scatter.3
  679.6 159.4 reduce-scatter.5
  944.2 126.7 reduce-scatter.7
